TPU v7x, 128 devices: a whole 4x4x4 slice. The times are simulated.
128 devices in a mesh: dp: 32 (over z, y_hi, x), tp: 4 (over y_lo, core).
Axes of the slice: x: 4, y: 4 (y_hi: 2, y_lo: 2; y = y_hi * 2 + y_lo), z: 4, core: 2. Of those that a mesh axis runs over, the one named last changes fastest.
Arguments:
- tokens: bfloat16 [8192, 2048], P(('dp', 'tp')), may hold values from -6 to 6
- cotangent: bfloat16 [8192, 2048], P(('dp', 'tp')), may hold values from -6 to 6
- seg_ids: int32 [8192], P('dp'), may hold values from 0 to 17, as said below
- parents: int32 [18], replicated, may hold values from 0 to 9, as said below
- tau: float32 [1], replicated, may hold values from 6 to 12
- w_query: bfloat16 [2048, 2048], P('dp', 'tp')
- w_up: bfloat16 [2048, 8192], P('dp', 'tp'), may hold values from -0.125 to 0.125
- w_out: bfloat16 [2048, 2048], P('dp', 'tp'), may hold values from -0.5 to 0.5
- w_down: bfloat16 [2048, 8192], P('dp', 'tp'), may hold values from -0.125 to 0.125
- query_bias: bfloat16 [128, 16], P('dp', 'tp'), may hold values from -3 to 3
- up_bias: bfloat16 [128, 64], P('dp', 'tp'), may hold values from -3 to 3
- w_keyval: bfloat16 [2048, 256], P(('dp', 'tp')), may hold values from -0.125 to 0.125
- value_bias: bfloat16 [128], P(('dp', 'tp')), may hold values from -3 to 3
- norm1_gain: bfloat16 [2048], P(('dp', 'tp')), may hold values from 0.5 to 1.5
- norm1_bias: bfloat16 [2048], P(('dp', 'tp')), may hold values from -2 to 2
- norm2_gain: bfloat16 [2048], P(('dp', 'tp')), may hold values from 0.5 to 1.5
- norm2_bias: bfloat16 [2048], P(('dp', 'tp')), may hold values from -2 to 2
- out_bias: bfloat16 [2048], P(('dp', 'tp')), may hold values from -2 to 2
- down_bias: bfloat16 [2048], P(('dp', 'tp')), may hold values from -2 to 2
Outputs:
- output: bfloat16 [8192, 2048], P(('dp', 'tp'))
- grad_input: float32 [8192, 2048], P(('dp', 'tp'))
- grad_w_query: float32 [2048, 2048], P('dp', 'tp')
- grad_w_up: float32 [2048, 8192], P('dp', 'tp')
- grad_w_out: float32 [2048, 2048], P('dp', 'tp')
- grad_w_down: float32 [2048, 8192], P('dp', 'tp')
- grad_query_bias: float32 [128, 16], P('dp', 'tp')
- grad_up_bias: float32 [128, 64], P('dp', 'tp')
- grad_w_keyval: float32 [2048, 256], P(('dp', 'tp'))
- grad_value_bias: float32 [128], P(('dp', 'tp'))
- grad_norm1_gain: float32 [2048], P(('dp', 'tp'))
- grad_norm1_bias: float32 [2048], P(('dp', 'tp'))
- grad_norm2_gain: float32 [2048], P(('dp', 'tp'))
- grad_norm2_bias: float32 [2048], P(('dp', 'tp'))
- grad_out_bias: float32 [2048], P(('dp', 'tp'))
- grad_down_bias: float32 [2048], P(('dp', 'tp'))
- clipped_query: bfloat16 [2048, 2048], P('dp', 'tp')
- clipped_query_bias: bfloat16 [128, 16], P('dp', 'tp')
Inputs may be any that keep to these rules, and one draw needn't show every extreme that they name: `seg_ids`: each of 2 trees has a trunk segment of 2048 tokens, 4 branch segments and 4 leaf segments of 256 tokens each. Tokens 8 * t * 256 to 8 * (t + 1) * 256 - 1 form trunk t (segment t); after all trunks, aligned blocks of 256 tokens hold the branches (segments 2 to 9) and leaves (the segments after), each leaf after its branch. `parents`: A trunk is its own parent; a branch's parent is a trunk, 4 branches to a trunk; leaf 2 + 2 * 4 + b has branch 2 + b as parent.
All inputs are finite; a program needn't handle non-finite values.
Results may differ from a plain program's by a relative error of at most 0.03.
Values may be sent and summed in bfloat16 or wider, within the bound.
A program may use at most 192 MiB of HBM per device.

v0:
```python
import jax
import jax.numpy as jnp
from jax import lax
from jax.sharding import PartitionSpec as P

EPS = 1e-05


def row_stats(values):
    centred = values - jnp.mean(values, axis=-1, keepdims=True)
    inverse = lax.rsqrt(jnp.mean(centred * centred, axis=-1, keepdims=True) + EPS)
    return (centred * inverse, inverse)


def norm_back(grad, normed, inverse, gain):
    scaled = grad * gain
    return inverse * (
        scaled
        - jnp.mean(scaled, axis=-1, keepdims=True)
        - normed * jnp.mean(scaled * normed, axis=-1, keepdims=True)
    )


def smooth_gate(values):
    return jax.nn.gelu(values, approximate=True)


def gather_rows(values):
    return lax.all_gather(values, "tp", axis=0, tiled=True)


def sum_rows(values):
    return lax.psum_scatter(
        values.astype(jnp.bfloat16), "tp", scatter_dimension=0, tiled=True
    ).astype(jnp.float32)


def local(
    tokens,
    cotangent,
    seg_ids,
    parents,
    tau,
    w_query,
    w_up,
    w_out,
    w_down,
    query_bias,
    up_bias,
    w_keyval,
    value_bias,
    norm1_gain,
    norm1_bias,
    norm2_gain,
    norm2_bias,
    out_bias,
    down_bias,
):
    single = jnp.float32
    half = jnp.bfloat16
    keyval_full, gain_one, shift_one, gain_two, shift_two, attn_bias, mlp_bias, value_full = (
        lax.all_gather(w_keyval, ("dp", "tp"), axis=0, tiled=True),
        lax.all_gather(norm1_gain, ("dp", "tp"), axis=0, tiled=True),
        lax.all_gather(norm1_bias, ("dp", "tp"), axis=0, tiled=True),
        lax.all_gather(norm2_gain, ("dp", "tp"), axis=0, tiled=True),
        lax.all_gather(norm2_bias, ("dp", "tp"), axis=0, tiled=True),
        lax.all_gather(out_bias, ("dp", "tp"), axis=0, tiled=True),
        lax.all_gather(down_bias, ("dp", "tp"), axis=0, tiled=True),
        lax.all_gather(value_bias, ("dp", "tp"), axis=0, tiled=True),
    )
    gain_one = gain_one.astype(single)
    shift_one = shift_one.astype(single)
    gain_two = gain_two.astype(single)
    shift_two = shift_two.astype(single)
    query_full, up_full, out_full, down_full, qbias_full, ubias_full = (
        lax.all_gather(w_query, "dp", axis=0, tiled=True),
        lax.all_gather(w_up, "dp", axis=0, tiled=True),
        lax.all_gather(w_out, "dp", axis=0, tiled=True),
        lax.all_gather(w_down, "dp", axis=0, tiled=True),
        lax.all_gather(query_bias, "dp", axis=0, tiled=True),
        lax.all_gather(up_bias, "dp", axis=0, tiled=True),
    )
    head_size = keyval_full.shape[1] // 2
    local_heads = qbias_full.shape[1]
    qbias_flat = qbias_full.astype(single).T.reshape(-1)
    ubias_flat = ubias_full.astype(single).T.reshape(-1)
    seq_rows = seg_ids.shape[0]
    scale = head_size ** (-0.5)
    resid = tokens.astype(single)
    normed_one, inverse_one = row_stats(resid)
    h_one_own = (normed_one * gain_one + shift_one).astype(half)
    h_one = gather_rows(h_one_own)
    queries = (jnp.dot(h_one, query_full, preferred_element_type=single) + qbias_flat).astype(half)
    value_shift = jnp.concatenate([jnp.zeros((head_size,), single), value_full.astype(single)])
    keyvals = (jnp.dot(h_one, keyval_full, preferred_element_type=single) + value_shift).astype(
        half
    )
    keyval_all, seg_all = (
        lax.all_gather(keyvals, "dp", axis=0, tiled=True),
        lax.all_gather(seg_ids, "dp", axis=0, tiled=True),
    )
    key_all = keyval_all[:, :head_size]
    value_all = keyval_all[:, head_size:]
    total = seg_all.shape[0]
    seg_count = parents.shape[0]
    labels = jnp.arange(seg_count, dtype=jnp.int32)
    parent_hot = (parents[:, None] == labels[None, :]).astype(jnp.int32)
    grand = jnp.sum(parent_hot * parents[None, :], axis=1)
    ancestry = (
        (labels[None, :] == labels[:, None])
        | (labels[None, :] == parents[:, None])
        | (labels[None, :] == grand[:, None])
    ).astype(single)
    query_hot = (seg_ids[:, None] == labels[None, :]).astype(single)
    reach = jnp.dot(query_hot, ancestry)
    key_hot = (labels[:, None] == seg_all[None, :]).astype(single)
    same_path = jnp.dot(reach, key_hot) > 0.5
    query_pos = lax.axis_index("dp") * seq_rows + jnp.arange(seq_rows, dtype=jnp.int32)
    key_pos = jnp.arange(total, dtype=jnp.int32)
    allowed = same_path & (key_pos[None, :] <= query_pos[:, None])
    group = min(local_heads, max(1, 512 // seq_rows))
    blocks = local_heads // group
    block_mask = jnp.tile(allowed, (group, 1))

    def to_blocks(values):
        return (
            values.reshape(seq_rows, local_heads, head_size)
            .transpose(1, 0, 2)
            .reshape(blocks, group * seq_rows, head_size)
        )

    def from_blocks(values):
        return (
            values.reshape(local_heads, seq_rows, head_size)
            .transpose(1, 0, 2)
            .reshape(seq_rows, local_heads * head_size)
        )

    def attend_block(query_block):
        scores = (
            jnp.einsum("qd,kd->qk", query_block, key_all, preferred_element_type=single) * scale
        )
        masked = jnp.where(block_mask, scores, -jnp.inf)
        top = jnp.max(masked, axis=1, keepdims=True)
        weights = jnp.exp(masked - top)
        weight_sum = jnp.sum(weights, axis=1, keepdims=True)
        probs = (weights / weight_sum).astype(half)
        heads = jnp.dot(probs, value_all, preferred_element_type=single).astype(half)
        return (heads, (top + jnp.log(weight_sum))[:, 0], top[:, 0])

    query_blocks = to_blocks(queries)
    head_blocks, log_sums, tops = lax.map(attend_block, query_blocks)
    heads_out = from_blocks(head_blocks)
    attn_part = jnp.einsum("rh,dh->rd", heads_out, out_full, preferred_element_type=single)
    middle = resid + (sum_rows(attn_part) + attn_bias.astype(single))
    normed_two, inverse_two = row_stats(middle)
    h_two_own = (normed_two * gain_two + shift_two).astype(half)
    h_two = gather_rows(h_two_own)
    hidden_pre = jnp.dot(h_two, up_full, preferred_element_type=single) + ubias_flat
    hidden = smooth_gate(hidden_pre).astype(half)
    mlp_part = jnp.einsum("rf,df->rd", hidden, down_full, preferred_element_type=single)
    output = (middle + (sum_rows(mlp_part) + mlp_bias.astype(single))).astype(half)
    head_top = jnp.max(tops.reshape(local_heads, seq_rows), axis=1)
    head_max = lax.pmax(head_top, "dp")
    limit = tau[0]
    factor = limit / jnp.maximum(head_max, limit)
    clipped_query = (w_query.astype(single) * jnp.repeat(factor, head_size)[None, :]).astype(half)
    clipped_bias = (query_bias.astype(single) * factor[None, :]).astype(half)
    cot = cotangent.astype(single)
    grad_down_bias = jnp.sum(cot, axis=0)
    cot_rows = gather_rows(cotangent)
    grad_hidden = jnp.einsum("rd,df->rf", cot_rows, down_full, preferred_element_type=single)
    gate_value, gate_back = jax.vjp(smooth_gate, hidden_pre)
    grad_pre = gate_back(grad_hidden)[0].astype(half)
    grad_up_bias = jnp.sum(grad_pre.astype(single), axis=0).reshape(-1, 128).T
    grad_down = jnp.einsum("rd,rf->df", cot_rows, hidden, preferred_element_type=single)
    grad_up = jnp.einsum("rd,rf->df", h_two, grad_pre, preferred_element_type=single)
    grad_h_two = sum_rows(jnp.einsum("rf,df->rd", grad_pre, up_full, preferred_element_type=single))
    grad_gain_two = jnp.sum(grad_h_two * normed_two, axis=0)
    grad_shift_two = jnp.sum(grad_h_two, axis=0)
    grad_middle = cot + norm_back(grad_h_two, normed_two, inverse_two, gain_two)
    grad_attn_own = grad_middle.astype(half)
    grad_out_bias = jnp.sum(grad_attn_own.astype(single), axis=0)
    grad_attn = gather_rows(grad_attn_own)
    grad_out = jnp.einsum("rd,rh->dh", grad_attn, heads_out, preferred_element_type=single)
    grad_heads = jnp.einsum("rd,dh->rh", grad_attn, out_full, preferred_element_type=single).astype(
        half
    )
    keyval_back = lax.all_gather(keyvals, "dp", axis=0, tiled=True)
    key_back = keyval_back[:, :head_size]
    value_back = keyval_back[:, head_size:]

    def back_block(carry, pieces):
        query_block, grad_block, log_block = pieces
        scores = (
            jnp.einsum("qd,kd->qk", query_block, key_back, preferred_element_type=single) * scale
        )
        masked = jnp.where(block_mask, scores, -jnp.inf)
        probs = jnp.exp(masked - log_block[:, None])
        grad_probs = jnp.einsum("qd,kd->qk", grad_block, value_back, preferred_element_type=single)
        inner = jnp.sum(probs * grad_probs, axis=1, keepdims=True)
        grad_scores = (probs * (grad_probs - inner)).astype(half)
        grad_query = jnp.dot(grad_scores, key_back, preferred_element_type=single) * scale
        grad_key = (
            carry[0]
            + jnp.einsum("qk,qd->kd", grad_scores, query_block, preferred_element_type=single)
            * scale
        )
        grad_value = carry[1] + jnp.einsum(
            "qk,qd->kd", probs.astype(half), grad_block, preferred_element_type=single
        )
        return ((grad_key, grad_value), grad_query)

    empty = jnp.zeros((total, head_size), single)
    (grad_key, grad_value), grad_query_blocks = lax.scan(
        back_block, (empty, empty), (query_blocks, to_blocks(grad_heads), log_sums)
    )
    grad_keyvals = jnp.concatenate([grad_key, grad_value], axis=1)
    grad_kv_own = lax.psum_scatter(
        grad_keyvals, ("dp", "tp"), scatter_dimension=0, tiled=True
    ).astype(half)
    grad_value_bias = jnp.sum(grad_kv_own[:, head_size:].astype(single), axis=0)
    grad_keyval = jnp.einsum("rd,rc->dc", h_one_own, grad_kv_own, preferred_element_type=single)
    grad_query_pre = from_blocks(grad_query_blocks).astype(half)
    grad_query_bias = (
        jnp.sum(grad_query_pre.astype(single), axis=0).reshape(local_heads, head_size).T
    )
    grad_h_one = sum_rows(
        jnp.einsum("rh,dh->rd", grad_query_pre, query_full, preferred_element_type=single)
    )
    grad_h_one = grad_h_one + jnp.einsum(
        "rc,dc->rd", grad_kv_own, keyval_full, preferred_element_type=single
    )
    grad_gain_one = jnp.sum(grad_h_one * normed_one, axis=0)
    grad_shift_one = jnp.sum(grad_h_one, axis=0)
    grad_input = grad_middle + norm_back(grad_h_one, normed_one, inverse_one, gain_one)
    grad_query = jnp.einsum("rd,rh->dh", h_one, grad_query_pre, preferred_element_type=single)
    query_sum, up_sum, out_sum, down_sum, qbias_sum, ubias_sum = (
        lax.psum_scatter(
            grad_query.astype(jnp.bfloat16), "dp", scatter_dimension=0, tiled=True
        ).astype(jnp.float32),
        lax.psum_scatter(
            grad_up.astype(jnp.bfloat16), "dp", scatter_dimension=0, tiled=True
        ).astype(jnp.float32),
        lax.psum_scatter(
            grad_out.astype(jnp.bfloat16), "dp", scatter_dimension=0, tiled=True
        ).astype(jnp.float32),
        lax.psum_scatter(
            grad_down.astype(jnp.bfloat16), "dp", scatter_dimension=0, tiled=True
        ).astype(jnp.float32),
        lax.psum_scatter(
            grad_query_bias.astype(jnp.bfloat16), "dp", scatter_dimension=0, tiled=True
        ).astype(jnp.float32),
        lax.psum_scatter(
            grad_up_bias.astype(jnp.bfloat16), "dp", scatter_dimension=0, tiled=True
        ).astype(jnp.float32),
    )
    (
        keyval_sum,
        gain_one_sum,
        shift_one_sum,
        gain_two_sum,
        shift_two_sum,
        outb_sum,
        downb_sum,
        valueb_sum,
    ) = (
        lax.psum_scatter(grad_keyval, ("dp", "tp"), scatter_dimension=0, tiled=True),
        lax.psum_scatter(grad_gain_one, ("dp", "tp"), scatter_dimension=0, tiled=True),
        lax.psum_scatter(grad_shift_one, ("dp", "tp"), scatter_dimension=0, tiled=True),
        lax.psum_scatter(grad_gain_two, ("dp", "tp"), scatter_dimension=0, tiled=True),
        lax.psum_scatter(grad_shift_two, ("dp", "tp"), scatter_dimension=0, tiled=True),
        lax.psum_scatter(grad_out_bias, ("dp", "tp"), scatter_dimension=0, tiled=True),
        lax.psum_scatter(grad_down_bias, ("dp", "tp"), scatter_dimension=0, tiled=True),
        lax.psum_scatter(grad_value_bias, ("dp", "tp"), scatter_dimension=0, tiled=True),
    )
    return (
        output,
        grad_input,
        query_sum,
        up_sum,
        out_sum,
        down_sum,
        qbias_sum,
        ubias_sum,
        keyval_sum,
        valueb_sum,
        gain_one_sum,
        shift_one_sum,
        gain_two_sum,
        shift_two_sum,
        outb_sum,
        downb_sum,
        clipped_query,
        clipped_bias,
    )


def solution(mesh):
    in_specs = (
        P(("dp", "tp"), None),
        P(("dp", "tp"), None),
        P("dp"),
        P(),
        P(),
        P("dp", "tp"),
        P("dp", "tp"),
        P("dp", "tp"),
        P("dp", "tp"),
        P("dp", "tp"),
        P("dp", "tp"),
        P(("dp", "tp"), None),
        P(("dp", "tp")),
        P(("dp", "tp")),
        P(("dp", "tp")),
        P(("dp", "tp")),
        P(("dp", "tp")),
        P(("dp", "tp")),
        P(("dp", "tp")),
    )
    out_specs = (
        P(("dp", "tp"), None),
        P(("dp", "tp"), None),
        P("dp", "tp"),
        P("dp", "tp"),
        P("dp", "tp"),
        P("dp", "tp"),
        P("dp", "tp"),
        P("dp", "tp"),
        P(("dp", "tp"), None),
        P(("dp", "tp")),
        P(("dp", "tp")),
        P(("dp", "tp")),
        P(("dp", "tp")),
        P(("dp", "tp")),
        P(("dp", "tp")),
        P(("dp", "tp")),
        P("dp", "tp"),
        P("dp", "tp"),
    )
    return jax.shard_map(local, mesh=mesh, in_specs=in_specs, out_specs=out_specs, check_vma=False)
```

profile of v0, /device:TPU:0, one launch (start us, length us, event | category | flops | bytes accessed | tf_op | source)
XLA Modules:
  0.0 3105.0 jit_solution(7817228534407352108)
XLA Ops:
  15.4 68.9 %all-reduce.18 = (bf16[2048]{0:T(1024)(128)(2,1)S(1)}, bf16[2048]{0:T(1024)(128)(2,1)S(1)}, bf16[2048]{0:T(1024)(128)(2,1)S(1)}, bf16[2048]{0:T(1024)(128)(2,1)S...) all-reduce(bf16[2048]{0:T(1024)(128)(2,1)S(1)} %dynamic-update-slic, ...), channel_id=1, replica_groups=mesh['dp'=32,'tp'=4] {'dp','tp'}, use_global_device_ids=true, to_apply=%add.6 | all-reduce | flops 12416 | bytes 49664
  88.3 15.5 all-gather.14.cloned.1.call-done
  103.8 193.5 %all-gather.18.cloned.1.call-done = bf16[2048,256]{1,0:T(8,128)(2,1)} async-done(((bf16[16,256]{1,0:T(8,128)(2,1)}), bf16[2048,256]{1,0:T(8,128)(2,1)}) %all-gather.18.cloned.1.call-update) | async-done | bytes 1048592 | tf_op jit(solution)/shard_map/all_gather | solution.py:62
  301.6 91.8 %all-gather = bf16[32,4,4]{2,1,0:T(4,128)(2,1)S(1)} all-gather(bf16[1,4,4]{2,1,0:T(4,128)(2,1)} %bitcast.179), channel_id=1, replica_groups=mesh['dp'=32,'tp'=4] {'dp'}, dimensions={0}, use_global_device_ids=true | all-gather | bytes 1056 | tf_op jit(solution)/shard_map/all_gather | solution.py:80
  393.5 88.2 %all-gather.1 = s32[32,1,256]{2,1,0:T(1,128)S(1)} all-gather(s32[1,1,256]{2,1,0:T(1,128)} %bitcast.181), channel_id=1, replica_groups=mesh['dp'=32,'tp'=4] {'dp'}, dimensions={0}, use_global_device_ids=true | all-gather | bytes 33792 | tf_op jit(solution)/shard_map/all_gather | solution.py:100
  489.4 4.5 fusion.76
  493.8 35.5 %while.30 = (s32[]{:T(128)}, bf16[2,512,128]{2,1,0:T(8,128)(2,1)S(1)}, f32[2,512]{1,0:T(2,128)S(1)}, f32[2,512]{1,0:T(2,128)S(1)}, bf16[2,512,128]{2,1,0:T(8,128...) while((s32[]{:T(128)}, ...), condition=%wide.region_6.7_spmd.clone, body=%wide.region_3.6_spmd.clone.sunk | while | flops 2197880320 | bytes 86274200 | solution.py:152
  493.8 4.9 fusion.136
  498.8 5.2 fusion.137
  503.9 5.1 divide_convert_fusion.2
  511.6 4.9 fusion.136
  516.5 5.2 fusion.137
  521.7 5.1 divide_convert_fusion.2
  534.6 13.9 reduce-scatter.14.cloned.1.call-done
  553.3 95.0 %all-gather.2 = bf16[32,4,16]{2,1,0:T(4,128)(2,1)S(1)} all-gather(bf16[1,4,16]{2,1,0:T(4,128)(2,1)S(1)} %bitcast.182), channel_id=1, replica_groups=mesh['dp'=32,'tp'=4] {'dp'}, dimensions={0}, use_global_device_ids=true | all-gather | bytes 4224 | tf_op jit(solution)/shard_map/all_gather | solution.py:81
  648.4 32.6 %all-gather.28.cloned.1.call-done = bf16[2048,2048]{1,0:T(8,128)(2,1)} async-done(((bf16[64,2048]{1,0:T(8,128)(2,1)}), bf16[2048,2048]{1,0:T(8,128)(2,1)}) %all-gather.28.cloned.1.call-update) | async-done | bytes 8388624 | tf_op jit(solution)/shard_map/all_gather | solution.py:79
  680.9 7.4 fusion.77
  688.3 13.4 all-gather.24.cloned.1.call-done
  701.7 108.6 %all-gather.26.cloned.1.call-done = bf16[2048,2048]{1,0:T(8,128)(2,1)} async-done(((bf16[64,2048]{1,0:T(8,128)(2,1)}), bf16[2048,2048]{1,0:T(8,128)(2,1)}) %all-gather.26.cloned.1.call-update) | async-done | bytes 8388624 | tf_op jit(solution)/shard_map/all_gather | solution.py:77
  810.3 10.1 fusion.74
  824.7 7.7 convolution_convert_fusion.7
  832.5 10.1 reduce-scatter.18.cloned.1.call-done
  844.4 21.8 reduce-scatter.16.cloned.1.call-done
  869.3 22.0 all-gather.32.cloned.1.call-done
  894.1 116.2 %while.31 = (s32[]{:T(128)}, f32[8192,128]{1,0:T(8,128)}, f32[8192,128]{1,0:T(8,128)}, bf16[2,512,128]{2,1,0:T(8,128)(2,1)S(1)}, bf16[2,512,128]{2,1,0:T(8,128)(...) while((s32[]{:T(128)}, f32[8192,128]{1,0:T(8,128)}, ...), condition=%wide.region_16.17_spmd.clone, body=%wide.region_14.16_spmd.clone.sunk | while | flops 5411765760 | bytes 260843760 | solution.py:215
  894.5 9.8 fusion.148
  904.3 12.6 multiply_reduce_fusion.4
  916.9 15.1 multiply_convert_fusion.7
  939.8 5.9 fusion.150
  950.1 9.8 fusion.148
  960.0 12.6 multiply_reduce_fusion.4
  972.6 15.1 multiply_convert_fusion.7
  991.0 6.6 convolution_add_fusion.6
  997.6 5.9 fusion.150
  1003.5 6.6 fusion.149
  1010.3 7.2 pad_maximum_fusion
  1023.3 7.5 convert_bitcast_fusion
  1030.9 12.3 copy.81
  1044.6 5.6 convolution_convert_fusion.1
  1053.8 615.4 %reduce-scatter.22.cloned.1.call-done = f32[64,256]{1,0:T(8,128)} async-done(((f32[8192,256]{1,0:T(8,128)}), f32[64,256]{1,0:T(8,128)}) %reduce-scatter.22.cloned.1.call-update) | async-done | bytes 65552 | tf_op jit(solution)/shard_map/reduce_scatter | solution.py:219
  1673.9 89.0 %pmax.7 = f32[4]{0:T(128)S(1)} all-reduce(f32[4]{0:T(128)S(1)} %reduce_max.20), channel_id=1, replica_groups=mesh['dp'=32,'tp'=4] {'dp'}, use_global_device_ids=true, to_apply=%region_45.46 | all-reduce | flops 4 | bytes 32 | tf_op jit(solution)/shard_map/pmax | solution.py:164
  1764.4 178.2 %all-reduce.19 = (bf16[128,4]{1,0:T(8,128)(2,1)S(1)}, bf16[128,16]{0,1:T(8,128)(2,1)S(1)}) all-reduce(bf16[128,4]{1,0:T(8,128)(2,1)S(1)} %copy.78, bf16[128,16]{0,1:T(8,128)(2,1)S(1)} %bitcast.178), channel_id=11, replica_groups=mesh['dp'=32,'tp'=4] {'dp'}, use_global_device_ids=true, to_apply=%region_26.27.clone | all-reduce | flops 2560 | bytes 10240
  1945.5 91.0 %reduce-scatter.24.cloned.1.call-done = bf16[64,512]{1,0:T(8,128)(2,1)} async-done(((bf16[2048,512]{1,0:T(8,128)(2,1)}), bf16[64,512]{1,0:T(8,128)(2,1)}) %reduce-scatter.24.cloned.1.call-update) | async-done | bytes 65552 | tf_op jit(solution)/shard_map/reduce_scatter | solution.py:239
  2038.0 198.7 %reduce-scatter.32.cloned.1.call-done = bf16[64,2048]{1,0:T(8,128)(2,1)} async-done(((bf16[2048,2048]{1,0:T(8,128)(2,1)}), bf16[64,2048]{1,0:T(8,128)(2,1)}) %reduce-scatter.32.cloned.1.call-update) | async-done | bytes 262160
  2238.9 197.6 %reduce-scatter.26.cloned.1.call-done = bf16[64,2048]{1,0:T(8,128)(2,1)} async-done(((bf16[2048,2048]{1,0:T(8,128)(2,1)}), bf16[64,2048]{1,0:T(8,128)(2,1)}) %reduce-scatter.26.cloned.1.call-update) | async-done | bytes 262160 | tf_op jit(solution)/shard_map/reduce_scatter | solution.py:242
  2438.4 15.4 reduce-scatter.20.cloned.1.call-done
  2455.4 67.6 %all-reduce.17 = (f32[128]{0:T(128)S(1)}, f32[2048]{0:T(1024)S(1)}, f32[2048]{0:T(1024)S(1)}, f32[2048]{0:T(1024)S(1)}, f32[2048]{0:T(1024)S(1)}, /*index=5*/f32[2048]{0:T(1024)S(1)}, f32[2048]{0:T(1024)S(1)}) all-reduce(f32[128]{0:T(128)S(1)} %convert_reduce_fusion.4, ...), channel_id=14, replica_groups=mesh['dp'=32,'tp'=4] {'dp','tp'}, use_global_device_ids=true, to_apply=%region_31.32.clone | all-reduce | flops 12416 | bytes 99328
  2528.2 569.9 %reduce-scatter.30.cloned.1.call-done = f32[16,256]{1,0:T(8,128)} async-done(((f32[2048,256]{1,0:T(8,128)}), f32[16,256]{1,0:T(8,128)}) %reduce-scatter.30.cloned.1.call-update) | async-done | bytes 16400 | tf_op jit(solution)/shard_map/reduce_scatter | solution.py:268
  (236 shorter events, 96.5 us)
Async XLA Ops:
  7.2 96.6 %all-gather.14.cloned.1.call-start = ((), (), s32[]{:S(2)}) async-start(), calls=%async_computation.10 | async-start | bytes 1310720 | tf_op jit(solution)/shard_map/all_gather | solution.py:29
  9.0 292.6 %copy-start.26 = (f32[64]{0:T(128)}, f32[64]{0:T(128)S(1)}, u32[]{:S(2)}) copy-start(f32[64]{0:T(128)S(1)} %broadcast_multiply_fusion.5) | copy-start | bytes 772
  10.2 471.4 %copy-start.32 = (f32[64]{0:T(128)}, f32[64]{0:T(128)S(1)}, u32[]{:S(2)}) copy-start(f32[64]{0:T(128)S(1)} %add_rsqrt_fusion.1) | copy-start | bytes 772
  86.8 210.6 %all-gather.18.cloned.1.call-start = ((), (), s32[]{:S(2)}) async-start(), calls=%async_computation.12 | async-start | bytes 1056768 | tf_op jit(solution)/shard_map/all_gather | solution.py:62
  87.5 397.7 %all-gather.16.cloned.1.call-start = ((), (), s32[]{:S(2)}) async-start(), calls=%async_computation.11 | async-start | bytes 2162688 | tf_op jit(solution)/shard_map/all_gather | solution.py:76
  88.3 401.1 %all-gather.20.cloned.1.call-start = ((), (), s32[]{:S(2)}) async-start(), calls=%async_computation.13 | async-start | bytes 4325376 | tf_op jit(solution)/shard_map/all_gather | solution.py:99
  300.0 229.5 %all-gather.22.cloned.1.call-start = ((), (), s32[]{:S(2)}) async-start(), calls=%async_computation.14 | async-start | bytes 2162688 | tf_op jit(solution)/shard_map/all_gather | solution.py:78
  300.6 247.9 %reduce-scatter.14.cloned.1.call-start = ((), (), s32[]{:S(2)}) async-start(), calls=%async_computation.15 | async-start | bytes 1310720 | tf_op jit(solution)/shard_map/reduce_scatter | solution.py:33
  529.3 159.0 %copy-start.30 = (f32[2,512]{1,0:T(2,128)}, f32[2,512]{1,0:T(2,128)S(1)}, u32[]{:S(2)}) copy-start(f32[2,512]{1,0:T(2,128)S(1)} %get-tuple-element.121) | copy-start | bytes 12292
  529.3 19.1 copy-start.4
  529.3 24.0 copy-start.34
  529.5 158.8 %copy-start.8 = (bf16[256,4,128]{0,2,1:T(8,128)(2,1)}, bf16[256,4,128]{0,2,1:T(8,128)(2,1)S(1)}, u32[]{:S(2)}) copy-start(bf16[256,4,128]{0,2,1:T(8,128)(2,1)S(1)} %copy.74) | copy-start | bytes 786436
  533.0 115.4 %all-gather.30.cloned.1.call-start = ((), (), s32[]{:S(2)}) async-start(), calls=%async_computation.20 | async-start | bytes 1310720 | tf_op jit(solution)/shard_map/all_gather | solution.py:29
  533.7 147.2 %all-gather.28.cloned.1.call-start = ((), (), s32[]{:S(2)}) async-start(), calls=%async_computation.18 | async-start | bytes 8650752 | tf_op jit(solution)/shard_map/all_gather | solution.py:79
  534.5 167.2 %all-gather.24.cloned.1.call-start = ((), (), s32[]{:S(2)}) async-start(), calls=%async_computation.16 | async-start | bytes 1310720 | tf_op jit(solution)/shard_map/all_gather | solution.py:29
  552.7 257.6 %all-gather.26.cloned.1.call-start = ((), (), s32[]{:S(2)}) async-start(), calls=%async_computation.17 | async-start | bytes 8650752 | tf_op jit(solution)/shard_map/all_gather | solution.py:77
  553.2 289.3 %reduce-scatter.18.cloned.1.call-start = ((), (), s32[]{:S(2)}) async-start(), calls=%async_computation.21 | async-start | bytes 1310720 | tf_op jit(solution)/shard_map/reduce_scatter | solution.py:33
  810.3 11.0 copy-start.35
  824.6 41.6 %reduce-scatter.16.cloned.1.call-start = ((), (), s32[]{:S(2)}) async-start(), calls=%async_computation.19 | async-start | bytes 1310720 | tf_op jit(solution)/shard_map/reduce_scatter | solution.py:33
  824.7 17.9 copy-start.6
  824.7 41.5 %copy-start.18 = (bf16[64,2048]{1,0:T(8,128)(2,1)S(1)}, bf16[64,2048]{1,0:T(8,128)(2,1)}, u32[]{:S(2)}) copy-start(bf16[64,2048]{1,0:T(8,128)(2,1)} %param.24) | copy-start | bytes 786436
  832.4 58.9 %all-gather.32.cloned.1.call-start = ((), (), s32[]{:S(2)}) async-start(), calls=%async_computation.22 | async-start | bytes 1310720 | tf_op jit(solution)/shard_map/all_gather | solution.py:29
  869.3 799.9 %reduce-scatter.22.cloned.1.call-start = ((), (), s32[]{:S(2)}) async-start(), calls=%async_computation.24 | async-start | bytes 8454144 | tf_op jit(solution)/shard_map/reduce_scatter | solution.py:219
  894.5 9.8 copy-start.2
  916.9 18.4 copy-start
  972.6 18.4 copy-start
  1017.5 926.4 %reduce-scatter.28.cloned.1.call-start = ((), (), s32[]{:S(2)}) async-start(), calls=%async_computation.27 | async-start | bytes 2162688 | tf_op jit(solution)/shard_map/reduce_scatter | solution.py:245
  1021.0 1015.5 %reduce-scatter.24.cloned.1.call-start = ((), (), s32[]{:S(2)}) async-start(), calls=%async_computation.25 | async-start | bytes 2162688 | tf_op jit(solution)/shard_map/reduce_scatter | solution.py:239
  1023.3 1213.4 %reduce-scatter.32.cloned.1.call-start = ((), (), s32[]{:S(2)}) async-start(), calls=%async_computation.29 | async-start | bytes 8650752
  1043.1 1393.4 %reduce-scatter.26.cloned.1.call-start = ((), (), s32[]{:S(2)}) async-start(), calls=%async_computation.26 | async-start | bytes 8650752 | tf_op jit(solution)/shard_map/reduce_scatter | solution.py:242
  1050.3 619.7 %copy-start.7 = (bf16[64,2048]{1,0:T(8,128)(2,1)S(1)}, bf16[64,2048]{1,0:T(8,128)(2,1)}, u32[]{:S(2)}) copy-start(bf16[64,2048]{1,0:T(8,128)(2,1)} %fusion.51) | copy-start | bytes 786436
  1050.3 622.3 %copy-start.38 = (u32[128]{0:T(128)S(1)}, u32[128]{0:T(128)}, u32[]{:S(2)}) copy-start(u32[128]{0:T(128)} %constant.130) | copy-start | bytes 1540
  1050.3 622.9 %copy-start.31 = (f32[2,512]{1,0:T(2,128)S(1)}, f32[2,512]{1,0:T(2,128)}, u32[]{:S(2)}) copy-start(f32[2,512]{1,0:T(2,128)} %copy-done.30) | copy-start | bytes 12292
  1050.3 712.6 %copy-start.29 = (bf16[4,4]{1,0:T(4,128)(2,1)S(1)}, bf16[4,4]{1,0:T(4,128)(2,1)}, u32[]{:S(2)}) copy-start(bf16[4,4]{1,0:T(4,128)(2,1)} %param.32) | copy-start | bytes 100
  1050.3 713.2 %copy-start.19 = (bf16[64,512]{1,0:T(8,128)(2,1)S(1)}, bf16[64,512]{1,0:T(8,128)(2,1)}, u32[]{:S(2)}) copy-start(bf16[64,512]{1,0:T(8,128)(2,1)} %param.28) | copy-start | bytes 196612
  1050.3 714.1 %copy-start.28 = (bf16[2048]{0:T(1024)(128)(2,1)S(1)}, bf16[2048]{0:T(1024)(128)(2,1)}, u32[]{:S(2)}) copy-start(bf16[2048]{0:T(1024)(128)(2,1)} %get-tuple-element.348) | copy-start | bytes 12292
  1050.3 1403.4 %reduce-scatter.20.cloned.1.call-start = ((), (), s32[]{:S(2)}) async-start(), calls=%async_computation.23 | async-start | bytes 1310720 | tf_op jit(solution)/shard_map/reduce_scatter | solution.py:33
  1053.7 1400.1 %copy-start.5 = (bf16[64,2048]{1,0:T(8,128)(2,1)S(1)}, bf16[64,2048]{1,0:T(8,128)(2,1)}, u32[]{:S(2)}) copy-start(bf16[64,2048]{1,0:T(8,128)(2,1)} %param.23) | copy-start | bytes 786436
  1053.7 1400.1 %copy-start.21 = (f32[2048]{0:T(1024)S(1)}, f32[2048]{0:T(1024)}, u32[]{:S(2)}) copy-start(f32[2048]{0:T(1024)} %copy-done.20) | copy-start | bytes 24580
  1053.7 1400.1 %copy-start.27 = (f32[64]{0:T(128)S(1)}, f32[64]{0:T(128)}, u32[]{:S(2)}) copy-start(f32[64]{0:T(128)} %copy-done.26) | copy-start | bytes 772
  1053.7 1400.1 %copy-start.33 = (f32[64]{0:T(128)S(1)}, f32[64]{0:T(128)}, u32[]{:S(2)}) copy-start(f32[64]{0:T(128)} %copy-done.32) | copy-start | bytes 772
  1053.7 1400.1 %copy-start.36 = (bf16[2048,256]{1,0:T(8,128)(2,1)S(1)}, bf16[2048,256]{1,0:T(8,128)(2,1)}, u32[]{:S(2)}) copy-start(bf16[2048,256]{1,0:T(8,128)(2,1)} %all-gather.18.cloned.1.call-done) | copy-start | bytes 3145732
  1053.7 2044.3 %reduce-scatter.30.cloned.1.call-start = ((), (), s32[]{:S(2)}) async-start(), calls=%async_computation.28 | async-start | bytes 2113536 | tf_op jit(solution)/shard_map/reduce_scatter | solution.py:268
  1671.8 783.6 %copy-start.22 = (f32[2048]{0:T(1024)S(1)}, f32[2048]{0:T(1024)}, u32[]{:S(2)}) copy-start(f32[2048]{0:T(1024)} %get-tuple-element.285) | copy-start | bytes 24580
  1671.8 783.6 %copy-start.23 = (f32[2048]{0:T(1024)S(1)}, f32[2048]{0:T(1024)}, u32[]{:S(2)}) copy-start(f32[2048]{0:T(1024)} %get-tuple-element.292) | copy-start | bytes 24580
  1671.8 783.6 %copy-start.24 = (f32[2048]{0:T(1024)S(1)}, f32[2048]{0:T(1024)}, u32[]{:S(2)}) copy-start(f32[2048]{0:T(1024)} %get-tuple-element.345) | copy-start | bytes 24580
  1671.8 783.6 %copy-start.25 = (f32[2048]{0:T(1024)S(1)}, f32[2048]{0:T(1024)}, u32[]{:S(2)}) copy-start(f32[2048]{0:T(1024)} %get-tuple-element.357) | copy-start | bytes 24580
  1671.8 855.2 %copy-start.11 = (f32[64,2048]{1,0:T(8,128)S(1)}, f32[64,2048]{1,0:T(8,128)}, u32[]{:S(2)}) copy-start(f32[64,2048]{1,0:T(8,128)} %get-tuple-element.347) | copy-start | bytes 1572868
  (15 other events, 49.7 us)
Sparse Core Ops, SparseCore 0:
  86.9 16.8 all-gather.13
  105.5 191.7 all-gather.17
  300.4 69.3 all-gather.15
  373.3 77.2 all-gather.19
  453.4 68.5 all-gather.21
  533.1 15.3 reduce-scatter.13
  550.2 21.9 all-gather.29
  575.7 105.2 all-gather.27
  683.3 18.3 all-gather.23
  705.0 105.2 all-gather.25
  824.8 17.7 reduce-scatter.17
  844.8 21.3 reduce-scatter.15
  869.4 21.8 all-gather.31
  1017.7 651.4 reduce-scatter.21
  1671.4 180.7 reduce-scatter.27
  1854.5 181.9 reduce-scatter.23
  2038.8 197.9 reduce-scatter.31
  2239.0 197.5 reduce-scatter.25
  2439.0 14.7 reduce-scatter.19
  2456.7 641.3 reduce-scatter.29
where the time goes:
time: 3110 us
  waiting for transfers between devices  2120 us (68%)
  blocking collectives  679 us (22%)
  matrix products  159 us (5%)
  other arithmetic  80.9 us (3%)
  local copies, waits for them, and re-layouts  43.9 us (1%)
    reduce_scatter x1, waiting for transfers between devices, local(): lax.psum_scatter(grad_keyvals, ('dp', 'tp'), scatter_dimension=0, tiled=T...  615 us
    reduce_scatter x1, waiting for transfers between devices, local(): lax.psum_scatter(grad_keyval, ('dp', 'tp'), scatter_dimension=0, tiled=True)  570 us
    unnamed x3, blocking collectives  315 us
    unnamed x21, waiting for transfers between devices  203 us
    reduce_scatter x1, waiting for transfers between devices, local(): lax.psum_scatter(grad_up.astype(jnp.bfloat16), 'dp', scatter_dimension=0,...  198 us
    all_gather x1, waiting for transfers between devices, local(): lax.all_gather(w_keyval, ('dp', 'tp'), axis=0, tiled=True)  194 us
    all_gather x1, waiting for transfers between devices, local(): lax.all_gather(w_up, 'dp', axis=0, tiled=True)  109 us
    all_gather x1, blocking collectives, local(): lax.all_gather(up_bias, 'dp', axis=0, tiled=True)  95 us
  transfers between devices with their start and end apart: 20, of which 15 were waited for; matrix products, arithmetic and copies ran while one was open for 4% of the time, Pallas kernels for 0%

commit v1 on v0

v1 whole, which is shorter than its diff:
```python
import itertools

import jax
import jax.numpy as jnp
from jax import lax
from jax.experimental import pallas as pl
from jax.experimental.pallas import tpu as pltpu
from jax.sharding import Mesh, PartitionSpec as P

EPS = 1e-05
AXES = ("z", "yh", "x", "yl", "c")
F32 = jnp.float32
BF16 = jnp.bfloat16
VMEM = pltpu.VMEM
NEG = -1e30


class Net:
    def __init__(self, send_sems, recv_sems):
        self.z, self.yh, self.x, self.yl, self.c = (lax.axis_index(a) for a in AXES)
        self.y = self.yh * 2 + self.yl
        self.yu, self.yo, self.yd = (lax.rem(self.y + s, 4) for s in (1, 2, 3))
        self.xu, self.xo, self.xd = (lax.rem(self.x + s, 4) for s in (1, 2, 3))
        self.zu, self.zo, self.zd = (lax.rem(self.z + s, 4) for s in (1, 2, 3))
        up, down = lax.rem(self.yh + self.yl, 2), lax.rem(self.yh + 1 - self.yl, 2)
        self.dev = {
            "yu": {"yh": up, "yl": 1 - self.yl},
            "yd": {"yh": down, "yl": 1 - self.yl},
            "yo": {"yh": 1 - self.yh},
            "c": {"c": 1 - self.c},
            "xu": {"x": self.xu},
            "xd": {"x": self.xd},
            "xo": {"x": self.xo},
            "zu": {"z": self.zu},
            "zd": {"z": self.zd},
            "zo": {"z": self.zo},
        }
        self.send_sems, self.recv_sems = send_sems, recv_sems
        self.count = 0
        self.sent = []

    def barrier(self, names):
        sem = pltpu.get_barrier_semaphore()
        for name in names:
            pl.semaphore_signal(
                sem, inc=1, device_id=self.dev[name], device_id_type=pl.DeviceIdType.MESH
            )
        pl.semaphore_wait(sem, len(names))

    def slot(self):
        self.count += 1
        return self.count - 1

    def copy(self, src, dst, k, name):
        return pltpu.make_async_remote_copy(
            src_ref=src,
            dst_ref=dst,
            send_sem=self.send_sems.at[k],
            recv_sem=self.recv_sems.at[k],
            device_id=self.dev[name],
            device_id_type=pl.DeviceIdType.MESH,
        )

    def send(self, src, dst, k, name):
        one = self.copy(src, dst, k, name)
        one.start()
        self.sent.append(one)

    def got(self, ref, k):
        self.copy(ref, ref, k, "c").wait_recv()

    def finish(self):
        for one in self.sent:
            one.wait_send()


def run_all(*steps):
    live = list(steps)
    while live:
        rest = []
        for one in live:
            try:
                next(one)
                rest.append(one)
            except StopIteration:
                pass
        live = rest


def group_gather(net, src, out):
    y, c, yu, yd, yo = net.y, net.c, net.yu, net.yd, net.yo
    k = [net.slot() for _ in range(9)]
    half = src.shape[0] // 2
    lo, hi = pl.ds(0, half), pl.ds(half, half)
    mine = out.at[y, c]
    net.send(src, mine, k[0], "yu")
    net.send(src, mine, k[1], "yd")
    net.send(src, mine, k[2], "c")
    yield
    net.got(out.at[yd, c], k[0])
    net.send(out.at[yd, c, lo], out.at[yd, c, lo], k[3], "yu")
    net.send(out.at[yd, c], out.at[yd, c], k[4], "c")
    net.got(out.at[yu, c], k[1])
    net.send(out.at[yu, c, hi], out.at[yu, c, hi], k[5], "yd")
    net.send(out.at[yu, c], out.at[yu, c], k[6], "c")
    yield
    net.got(out.at[yo, c, lo], k[3])
    net.send(out.at[yo, c, lo], out.at[yo, c, lo], k[7], "c")
    net.got(out.at[yo, c, hi], k[5])
    net.send(out.at[yo, c, hi], out.at[yo, c, hi], k[8], "c")
    yield
    net.got(out.at[y, 1 - c], k[2])
    net.got(out.at[yd, 1 - c], k[4])
    net.got(out.at[yu, 1 - c], k[6])
    net.got(out.at[yo, 1 - c, lo], k[7])
    net.got(out.at[yo, 1 - c, hi], k[8])


def group_scatter(net, part, from_core, held, from_half, from_full, total):
    y, c, yu, yd, yo = net.y, net.c, net.yu, net.yd, net.yo
    k = [net.slot() for _ in range(8)]
    n = part.shape[2]
    half = n // 2
    lo, hi = pl.ds(0, half), pl.ds(half, half)
    for i, d in enumerate((yo, yu, yd, y)):
        net.send(part.at[d, 1 - c], from_core.at[d], k[i], "c")

    def core_sum(i, d):
        net.got(from_core.at[d], k[i])
        held[d] = (part[d, c].astype(F32) + from_core[d].astype(F32)).astype(BF16)

    yield
    core_sum(0, yo)
    net.send(held.at[yo, lo], from_half.at[0], k[4], "yu")
    net.send(held.at[yo, hi], from_half.at[1], k[5], "yd")
    core_sum(1, yu)
    core_sum(2, yd)
    yield
    net.got(from_half.at[0], k[4])
    held[yu, lo] = (held[yu, lo].astype(F32) + from_half[0].astype(F32)).astype(BF16)
    net.send(held.at[yu], from_full.at[0], k[6], "yu")
    net.got(from_half.at[1], k[5])
    held[yd, hi] = (held[yd, hi].astype(F32) + from_half[1].astype(F32)).astype(BF16)
    net.send(held.at[yd], from_full.at[1], k[7], "yd")
    core_sum(3, y)
    yield
    net.got(from_full.at[0], k[6])
    net.got(from_full.at[1], k[7])
    total(held[y].astype(F32) + from_full[0].astype(F32) + from_full[1].astype(F32))


def scatter_scratch(n, w):
    return [VMEM((4, n, w), BF16), VMEM((4, n, w), BF16), VMEM((2, n // 2, w), BF16), VMEM((2, n, w), BF16)]


BOTH = slice(None)


def plane_gather(net, o):
    z, x, xu, xd, xo, zu, zd, zo = net.z, net.x, net.xu, net.xd, net.xo, net.zu, net.zd, net.zo
    k = [net.slot() for _ in range(16)]
    every = slice(None)

    def send(view, i, name):
        net.send(view, view, k[i], name)

    def got(view, i):
        net.got(view, k[i])

    send(o(z, BOTH, x, 0), 0, "xu")
    send(o(z, BOTH, x, 0), 1, "xd")
    send(o(z, BOTH, x, 1), 2, "zu")
    send(o(z, BOTH, x, 1), 3, "zd")
    yield
    got(o(z, BOTH, xd, 0), 0)
    send(o(z, 0, xd, 0), 4, "xu")
    got(o(zd, BOTH, x, 1), 2)
    send(o(zd, 0, x, 1), 6, "zu")
    got(o(z, BOTH, xu, 0), 1)
    send(o(z, 1, xu, 0), 5, "xd")
    got(o(zu, BOTH, x, 1), 3)
    send(o(zu, 1, x, 1), 7, "zd")
    yield
    got(o(z, 0, xo, 0), 4)
    got(o(z, 1, xo, 0), 5)
    send(o(z, BOTH, every, 0), 8, "zu")
    send(o(z, BOTH, every, 0), 9, "zd")
    got(o(zo, 0, x, 1), 6)
    got(o(zo, 1, x, 1), 7)
    send(o(every, BOTH, x, 1), 10, "xu")
    send(o(every, BOTH, x, 1), 11, "xd")
    yield
    got(o(zd, BOTH, every, 0), 8)
    send(o(zd, 0, every, 0), 12, "zu")
    got(o(every, BOTH, xd, 1), 10)
    send(o(every, 0, xd, 1), 14, "xu")
    got(o(zu, BOTH, every, 0), 9)
    send(o(zu, 1, every, 0), 13, "zd")
    got(o(every, BOTH, xu, 1), 11)
    send(o(every, 1, xu, 1), 15, "xd")
    yield
    got(o(zo, 0, every, 0), 12)
    got(o(zo, 1, every, 0), 13)
    got(o(every, 0, xo, 1), 14)
    got(o(every, 1, xo, 1), 15)


def add_into(dst, *others):
    for index in itertools.product(*[range(n) for n in dst.shape[:-2]]):
        at = index + (slice(None), slice(None))
        total = dst[at].astype(F32)
        for other in others:
            total = total + other[at].astype(F32)
        dst[at] = total.astype(dst.dtype)


def plane_scatter(net, g, tmp):
    z, x, xu, xd, xo, zu, zd, zo = net.z, net.x, net.xu, net.xd, net.xo, net.zu, net.zd, net.zo
    t1, t2, u1, u2, t3, t4, u3, u4 = tmp
    k = [net.slot() for _ in range(16)]
    every = slice(None)

    def send(src, dst, i, name):
        net.send(src, dst, k[i], name)

    def got(ref, i):
        net.got(ref, k[i])

    send(g(zo, 0, every, 0), t1.at[0], 0, "zu")
    send(g(zo, 1, every, 0), t1.at[1], 1, "zd")
    send(g(every, 0, xo, 1), t2.at[0], 2, "xu")
    send(g(every, 1, xo, 1), t2.at[1], 3, "xd")
    yield
    got(t1.at[0], 0)
    add_into(g(zu, 0, every, 0), t1.at[0])
    send(g(zu, BOTH, every, 0), u1.at[0], 4, "zu")
    got(t2.at[0], 2)
    add_into(g(every, 0, xu, 1), t2.at[0])
    send(g(every, BOTH, xu, 1), u2.at[0], 6, "xu")
    got(t1.at[1], 1)
    add_into(g(zd, 1, every, 0), t1.at[1])
    send(g(zd, BOTH, every, 0), u1.at[1], 5, "zd")
    got(t2.at[1], 3)
    add_into(g(every, 1, xd, 1), t2.at[1])
    send(g(every, BOTH, xd, 1), u2.at[1], 7, "xd")
    yield
    got(u1.at[0], 4)
    got(u1.at[1], 5)
    add_into(g(z, BOTH, every, 0), u1.at[0], u1.at[1])
    send(g(z, 0, xo, 0), t3.at[0], 8, "xu")
    send(g(z, 1, xo, 0), t3.at[1], 9, "xd")
    got(u2.at[0], 6)
    got(u2.at[1], 7)
    add_into(g(every, BOTH, x, 1), u2.at[0], u2.at[1])
    send(g(zo, 0, x, 1), t4.at[0], 10, "zu")
    send(g(zo, 1, x, 1), t4.at[1], 11, "zd")
    yield
    got(t3.at[0], 8)
    add_into(g(z, 0, xu, 0), t3.at[0])
    send(g(z, BOTH, xu, 0), u3.at[0], 12, "xu")
    got(t4.at[0], 10)
    add_into(g(zu, 0, x, 1), t4.at[0])
    send(g(zu, BOTH, x, 1), u4.at[0], 14, "zu")
    got(t3.at[1], 9)
    add_into(g(z, 1, xd, 0), t3.at[1])
    send(g(z, BOTH, xd, 0), u3.at[1], 13, "xd")
    got(t4.at[1], 11)
    add_into(g(zd, 1, x, 1), t4.at[1])
    send(g(zd, BOTH, x, 1), u4.at[1], 15, "zd")
    yield
    got(u3.at[0], 12)
    got(u3.at[1], 13)
    add_into(g(z, BOTH, x, 0), u3.at[0], u3.at[1])
    got(u4.at[0], 14)
    got(u4.at[1], 15)
    add_into(g(z, BOTH, x, 1), u4.at[0], u4.at[1])


def plane_scratch(n, w):
    return [
        VMEM((2, 4, n, w), BF16),
        VMEM((2, 4, n, w), BF16),
        VMEM((2, 2, 4, n, w), BF16),
        VMEM((2, 4, 2, n, w), BF16),
        VMEM((2, n, w), BF16),
        VMEM((2, n, w), BF16),
        VMEM((2, 2, n, w), BF16),
        VMEM((2, 2, n, w), BF16),
    ]


def column_view(ref):
    w = ref.shape[-1] // 2

    def view(zz, half, xx, part):
        return ref.at[zz, half, xx, :, pl.ds(part * w, w)]

    return view


def sems(n):
    return [pltpu.SemaphoreType.DMA((n,)), pltpu.SemaphoreType.DMA((n,))]


def params(cid, limit=56 << 20):
    return pltpu.CompilerParams(collective_id=cid, has_side_effects=True, vmem_limit_bytes=limit)


ANY = pl.BlockSpec(memory_space=pl.ANY)
INV = pl.BlockSpec(memory_space=pltpu.VMEM)
INS = pl.BlockSpec(memory_space=pltpu.SMEM)
PLANE = ("xu", "xd", "zu", "zd")
RING = ("yu", "yd", "c")


def opening(tokens, cotangent, small, wq_own, wq_oth, wo_own, wo_oth):
    def kernel(tok, cot, small, qa, qb, oa, ob, tok_out, cot_out, small_out, q_out, o_out, local, ss, rs):
        net = Net(ss, rs)
        z, yh, x, yl, c = net.z, net.yh, net.x, net.yl, net.c
        locals_ = [
            pltpu.make_async_copy(src, dst, local.at[i])
            for i, (src, dst) in enumerate(
                (
                    (qa, q_out.at[z, yh, x]),
                    (oa, o_out.at[z, yh, x]),
                    (tok, tok_out.at[net.y, c]),
                    (cot, cot_out.at[net.y, c]),
                    (small, small_out.at[z, net.y * 2 + c, x]),
                )
            )
        ]
        for one in locals_:
            one.start()
        net.barrier(PLANE + RING + ("yo",))

        def weight(own, oth, out, i):
            k = net.slot()
            net.send(oth, out.at[z, yh, x], k, "yo")
            yield
            locals_[i].wait()
            net.got(out.at[z, 1 - yh, x], k)
            yield from plane_gather(net, column_view(out))

        def small_all():
            k = [net.slot() for _ in range(7)]
            y = net.y

            def at(yy, cc):
                return small_out.at[z, yy * 2 + cc, x]

            net.send(small, at(y, c), k[0], "yu")
            net.send(small, at(y, c), k[1], "yd")
            net.send(small, at(y, c), k[2], "yo")
            net.send(small, at(y, c), k[3], "c")
            yield
            for i, d in enumerate((net.yd, net.yu, net.yo)):
                net.got(at(d, c), k[i])
                net.send(at(d, c), at(d, c), k[4 + i], "c")
            yield
            for i, d in enumerate((y, net.yd, net.yu, net.yo)):
                net.got(at(d, 1 - c), k[3 + i])
            locals_[4].wait()

            def view(zz, half, xx, part):
                which = pl.ds(0, 8) if half == BOTH else pl.ds(4 * half, 4)
                cols = pl.ds(0, 256) if part == 0 else pl.ds(256, 128)
                return small_out.at[zz, which, xx, :, cols]

            yield from plane_gather(net, view)

        run_all(
            small_all(),
            weight(qa, qb, q_out, 0),
            weight(oa, ob, o_out, 1),
            group_gather(net, tok, tok_out),
            group_gather(net, cot, cot_out),
        )
        locals_[2].wait()
        locals_[3].wait()
        net.finish()

    n, d = tokens.shape
    weight = jax.ShapeDtypeStruct((4, 2, 4, n, wq_own.shape[1]), BF16)
    rows = jax.ShapeDtypeStruct((4, 2, n, d), BF16)
    return pl.pallas_call(
        kernel,
        out_shape=(rows, rows, jax.ShapeDtypeStruct((4, 8, 4) + small.shape, BF16), weight, weight),
        in_specs=[ANY] * 7,
        out_specs=(ANY,) * 5,
        scratch_shapes=[pltpu.SemaphoreType.DMA((5,))] + sems(17 * 2 + 7 + 16 + 18),
        compiler_params=params(1),
        name="opening",
    )(tokens, cotangent, small, wq_own, wq_oth, wo_own, wo_oth)


def gather_ff(up_own, up_oth, dn_own, dn_oth):
    def kernel(ua, ub, da, db, u_out, d_out, local, ss, rs):
        net = Net(ss, rs)
        z, yh, x = net.z, net.yh, net.x
        mine = [
            pltpu.make_async_copy(ua, u_out.at[z, yh, x], local.at[0]),
            pltpu.make_async_copy(da, d_out.at[z, yh, x], local.at[1]),
        ]
        for one in mine:
            one.start()
        net.barrier(PLANE + ("yo",))

        def weight(oth, out, one):
            k = net.slot()
            net.send(oth, out.at[z, yh, x], k, "yo")
            yield
            one.wait()
            net.got(out.at[z, 1 - yh, x], k)
            yield from plane_gather(net, column_view(out))

        run_all(weight(ub, u_out, mine[0]), weight(db, d_out, mine[1]))
        net.finish()

    shape = jax.ShapeDtypeStruct((4, 2, 4) + up_own.shape, BF16)
    return pl.pallas_call(
        kernel,
        out_shape=(shape, shape),
        in_specs=[ANY] * 4,
        out_specs=(ANY, ANY),
        scratch_shapes=[pltpu.SemaphoreType.DMA((2,))] + sems(34),
        compiler_params=params(2),
        name="gather_ff",
    )(up_own, up_oth, dn_own, dn_oth)


def gather_kv(kv):
    def kernel(kv, out, local, ss, rs):
        net = Net(ss, rs)
        z, x, c = net.z, net.x, net.c
        me = pltpu.make_async_copy(kv.at[c], out.at[z, c, x], local)
        me.start()
        net.barrier(PLANE + ("c",))
        me.wait()

        def view(zz, half, xx, part):
            rows = pl.ds(0, 256) if half == BOTH else pl.ds(128 * half, 128)
            return out.at[zz, c, xx, rows, pl.ds(part * 128, 128)]

        run_all(plane_gather(net, view))
        k = net.slot()
        net.send(out.at[:, c], out.at[:, c], k, "c")
        net.got(out.at[:, 1 - c], k)
        net.finish()

    return pl.pallas_call(
        kernel,
        out_shape=jax.ShapeDtypeStruct((4, 2, 4, 256, 256), BF16),
        in_specs=[ANY],
        out_specs=ANY,
        scratch_shapes=[pltpu.SemaphoreType.DMA] + sems(17),
        compiler_params=params(3),
        name="gather_kv",
    )(kv)


def block_place(segs, parents, block):
    seg = segs[block]
    parent = parents[seg]
    trunk = parents[parent]
    parent_block = jnp.int32(16)
    for b in range(16, 32):
        parent_block = jnp.where(segs[b] == parent, b, parent_block)
    return trunk, parent_block, seg >= 10, seg >= 2


def attend(q, kv, segs, parents):
    def kernel(segs, parents, q, kv, o, log_sum, tops, scores):
        z, x = lax.axis_index("z"), lax.axis_index("x")
        lane = lax.broadcasted_iota(jnp.int32, (256, 512), 1) & 255
        row = lax.broadcasted_iota(jnp.int32, (256, 512), 0)
        best = []
        for b in range(2):
            block = z * 8 + b * 4 + x
            trunk, parent_block, leaf, branch = block_place(segs, parents, block)
            both = jnp.concatenate([q[b, :, :128], q[b, :, 128:]], axis=0)

            def score(key_block):
                return (
                    lax.dot_general(
                        kv[key_block, :, :128], both, (((1,), (1,)), ((), ())), preferred_element_type=F32
                    )
                    * 128**-0.5
                )

            def trunk_score(i, top):
                s = score(trunk * 8 + i)
                gap = (block - trunk * 8 - i) * 256
                s = jnp.where(row - lane <= gap, s, NEG)
                scores[i] = s
                return jnp.maximum(top, jnp.max(s, axis=0, keepdims=True))

            top = lax.fori_loop(0, 8, trunk_score, jnp.full((1, 512), NEG, F32))
            s = jnp.where(leaf, score(parent_block), NEG)
            scores[8] = s
            top = jnp.maximum(top, jnp.max(s, axis=0, keepdims=True))
            s = jnp.where((row <= lane) & branch, score(block), NEG)
            scores[9] = s
            top = jnp.maximum(top, jnp.max(s, axis=0, keepdims=True))

            def weigh(i, carry):
                acc, total = carry
                w = jnp.exp(scores[i] - top)
                key_block = jnp.where(i < 8, trunk * 8 + i, jnp.where(i == 8, parent_block, block))
                acc = acc + lax.dot_general(
                    kv[key_block, :, 128:], w.astype(BF16), (((0,), (0,)), ((), ())), preferred_element_type=F32
                )
                return acc, total + jnp.sum(w, axis=0, keepdims=True)

            acc, total = lax.fori_loop(0, 10, weigh, (jnp.zeros((128, 512), F32), jnp.zeros((1, 512), F32)))
            heads = (acc / total).T.astype(BF16)
            o[b, :, :128] = heads[:256]
            o[b, :, 128:] = heads[256:]
            log_sum[b] = jnp.broadcast_to(top + jnp.log(total), (8, 512))
            best.append(top)
        top = jnp.maximum(best[0], best[1])
        for h in range(2):
            tops[h] = jnp.full((8, 128), jnp.max(top[:, h * 256 : (h + 1) * 256]), F32)

    return pl.pallas_call(
        kernel,
        out_shape=(
            jax.ShapeDtypeStruct((2, 256, 256), BF16),
            jax.ShapeDtypeStruct((2, 8, 512), F32),
            jax.ShapeDtypeStruct((2, 8, 128), F32),
        ),
        in_specs=[INS, INS, INV, INV],
        out_specs=(INV, INV, INV),
        scratch_shapes=[VMEM((10, 256, 512), F32)],
        compiler_params=pltpu.CompilerParams(vmem_limit_bytes=56 << 20),
        name="attend",
    )(segs, parents, q, kv)


def attend_back(q, kv, o, go, log_sum, segs, parents):
    def kernel(segs, parents, q, kv, o, go, log_sum, dq, dkv):
        z, x = lax.axis_index("z"), lax.axis_index("x")
        lane = lax.broadcasted_iota(jnp.int32, (256, 512), 1) & 255
        row = lax.broadcasted_iota(jnp.int32, (256, 512), 0)
        for b in range(2):
            block = z * 8 + b * 4 + x
            trunk, parent_block, leaf, branch = block_place(segs, parents, block)

            def stacked(ref):
                return jnp.concatenate([ref[b, :, :128], ref[b, :, 128:]], axis=0)

            both, grad = stacked(q), stacked(go)
            logs = log_sum[b, 0:1]
            inner = jnp.sum((grad.astype(F32) * stacked(o).astype(F32)).T, axis=0, keepdims=True)

            def one(i, key_block, mask, acc):
                key, value = kv[key_block, :, :128], kv[key_block, :, 128:]
                nt = (((1,), (1,)), ((), ()))
                s = lax.dot_general(key, both, nt, preferred_element_type=F32) * 128**-0.5
                p = jnp.where(mask, jnp.exp(jnp.minimum(s - logs, 1.0)), 0.0)
                dp = lax.dot_general(value, grad, nt, preferred_element_type=F32)
                ds = (p * (dp - inner)).astype(BF16)
                dk = jnp.dot(ds, both, preferred_element_type=F32) * 128**-0.5
                dv = jnp.dot(p.astype(BF16), grad, preferred_element_type=F32)
                dkv[b, i, :, :128] = dk.astype(BF16)
                dkv[b, i, :, 128:] = dv.astype(BF16)
                return acc + lax.dot_general(key, ds, (((0,), (0,)), ((), ())), preferred_element_type=F32)

            def trunk_one(i, acc):
                gap = (block - trunk * 8 - i) * 256
                return one(i, trunk * 8 + i, row - lane <= gap, acc)

            acc = lax.fori_loop(0, 8, trunk_one, jnp.zeros((128, 512), F32))
            acc = one(8, parent_block, jnp.broadcast_to(leaf, (256, 512)), acc)
            acc = one(9, block, (row <= lane) & branch, acc)
            grad_q = (acc * 128**-0.5).T.astype(BF16)
            dq[b, :, :128] = grad_q[:256]
            dq[b, :, 128:] = grad_q[256:]

    return pl.pallas_call(
        kernel,
        out_shape=(
            jax.ShapeDtypeStruct((2, 256, 256), BF16),
            jax.ShapeDtypeStruct((2, 10, 256, 256), BF16),
        ),
        in_specs=[INS, INS, INV, INV, INV, INV, INV],
        out_specs=(INV, INV),
        compiler_params=pltpu.CompilerParams(vmem_limit_bytes=56 << 20),
        name="attend_back",
    )(segs, parents, q, kv, o, go, log_sum)


def normed(values):
    centred = values - jnp.mean(values, axis=-1, keepdims=True)
    inverse = lax.rsqrt(jnp.mean(centred * centred, axis=-1, keepdims=True) + EPS)
    return centred * inverse, inverse


def norm_back(grad, norm, inverse, gain):
    scaled = grad * gain
    return inverse * (
        scaled
        - jnp.mean(scaled, axis=-1, keepdims=True)
        - norm * jnp.mean(scaled * norm, axis=-1, keepdims=True)
    )


def middle(part, tokens, out_bias, gain, shift, tops):
    def kernel(part, tokens, bias, gain, shift, tops, x1, h2, best, own, mine, got, local, *rest):
        *scratch, ss, rs = rest
        net = Net(ss, rs)
        net.barrier(PLANE + RING + ("yo",))

        def rows():
            def total(summed):
                value = tokens[...].astype(F32) + (summed + bias[...])
                x1[...] = value
                own[...] = (normed(value)[0] * gain[...] + shift[...]).astype(BF16)

            yield from group_scatter(net, part, *scratch, total)
            me = pltpu.make_async_copy(own, h2.at[net.y, net.c], local)
            me.start()
            yield from group_gather(net, own, h2)
            me.wait()

        def largest():
            mine[0] = tops[...]
            yield from heads_max(net, mine, got, best)

        run_all(rows(), largest())
        net.finish()

    n, d = tokens.shape
    return pl.pallas_call(
        kernel,
        out_shape=(
            jax.ShapeDtypeStruct((n, d), F32),
            jax.ShapeDtypeStruct((4, 2, n, d), BF16),
            jax.ShapeDtypeStruct((2, 16, 128), F32),
        ),
        in_specs=[INV] * 6,
        out_specs=(INV, ANY, INV),
        scratch_shapes=[
            VMEM((n, d), BF16),
            VMEM((5, 16, 128), F32),
            VMEM((7, 16, 128), F32),
            pltpu.SemaphoreType.DMA,
        ]
        + scatter_scratch(n, d)
        + sems(9 + 8 + 7),
        compiler_params=params(4),
        name="middle",
    )(part, tokens, out_bias, gain, shift, tops)


def heads_max(net, mine, got, best):
    for i, (up, down) in enumerate((("xu", "xd"), ("zu", "zd"))):
        k = [net.slot() for _ in range(3)]
        a, b, d = got.at[3 * i], got.at[3 * i + 1], got.at[3 * i + 2]
        net.send(mine.at[2 * i], a, k[0], up)
        net.send(mine.at[2 * i], b, k[1], down)
        yield
        net.got(a, k[0])
        net.got(b, k[1])
        mine[2 * i + 1] = jnp.maximum(mine[2 * i], jnp.maximum(a[...], b[...]))
        net.send(mine.at[2 * i + 1], d, k[2], up)
        yield
        net.got(d, k[2])
        mine[2 * i + 2] = jnp.maximum(mine[2 * i + 1], d[...])
    k = net.slot()
    net.send(mine.at[4], got.at[6], k, "yo")
    yield
    net.got(got.at[6], k)
    best[net.yh] = mine[4]
    best[1 - net.yh] = got[6]


def turn(mlp, back, x1, cotangent, gain, down_bias):
    def kernel(mlp, back, x1, cot, gain, bias, output, dx1, dz, sums, own, local, *rest):
        first, second, (ss, rs) = rest[:4], rest[4:8], rest[8:]
        net = Net(ss, rs)
        net.barrier(RING)

        def gradient():
            def total(summed):
                norm, inverse = normed(x1[...])
                grad = cot[...].astype(F32) + norm_back(summed, norm, inverse, gain[...])
                dx1[...] = grad
                rounded = grad.astype(BF16)
                own[...] = rounded
                parts = [
                    jnp.sum(v, axis=0, keepdims=True)
                    for v in (summed * norm, summed, rounded.astype(F32), cot[...].astype(F32))
                ]
                zero = jnp.zeros((2, parts[0].shape[1]), F32)
                sums[...] = jnp.concatenate([zero] + parts + [zero], axis=0)

            yield from group_scatter(net, back, *first, total)
            me = pltpu.make_async_copy(own, dz.at[net.y, net.c], local)
            me.start()
            yield from group_gather(net, own, dz)
            me.wait()

        def forward():
            def total(summed):
                output[...] = (x1[...] + (summed + bias[...])).astype(BF16)

            yield
            yield from group_scatter(net, mlp, *second, total)

        run_all(gradient(), forward())
        net.finish()

    n, d = cotangent.shape
    return pl.pallas_call(
        kernel,
        out_shape=(
            jax.ShapeDtypeStruct((n, d), BF16),
            jax.ShapeDtypeStruct((n, d), F32),
            jax.ShapeDtypeStruct((4, 2, n, d), BF16),
            jax.ShapeDtypeStruct((8, d), F32),
        ),
        in_specs=[INV] * 6,
        out_specs=(INV, INV, ANY, INV),
        scratch_shapes=[VMEM((n, d), BF16), pltpu.SemaphoreType.DMA]
        + scatter_scratch(n, d)
        + scatter_scratch(n, d)
        + sems(9 + 8 + 8),
        compiler_params=params(5),
        name="turn",
    )(mlp, back, x1, cotangent, gain, down_bias)


def weight_scatter(net, g, tmp, swap, out):
    z, yh, x = net.z, net.yh, net.x
    w = g.shape[-1]
    k = net.slot()
    yield from plane_scatter(net, column_view(g), tmp)
    net.send(g.at[z, 1 - yh, x], swap, k, "yo")
    out[:, pl.ds(pl.multiple_of(yh * w, 128), w)] = g[z, yh, x].astype(F32)
    yield
    net.got(swap, k)
    out[:, pl.ds(pl.multiple_of((1 - yh) * w, 128), w)] = swap[...].astype(F32)


def scatter_weights(grads, cid):
    count = len(grads)

    def kernel(*refs):
        g, outs = refs[:count], refs[count : 2 * count]
        scratch, (ss, rs) = refs[2 * count : -2], refs[-2:]
        net = Net(ss, rs)
        net.barrier(PLANE + ("yo",))
        run_all(
            *[
                weight_scatter(net, g[i], scratch[9 * i : 9 * i + 8], scratch[9 * i + 8], outs[i])
                for i in range(count)
            ]
        )
        net.finish()

    scratch = []
    for one in grads:
        n, w = one.shape[-2:]
        scratch += plane_scratch(n, w // 2) + [VMEM((n, w), BF16)]
    return pl.pallas_call(
        kernel,
        out_shape=tuple(jax.ShapeDtypeStruct((g.shape[-2], 2 * g.shape[-1]), F32) for g in grads),
        in_specs=[INV] * count,
        out_specs=(INV,) * count,
        scratch_shapes=scratch + sems(17 * count),
        compiler_params=params(cid),
        name="scatter_weights",
    )(*grads)


def scatter_kv(slots, segs, parents):
    def kernel(segs, parents, slots, out, full, from_core, held, ring, *rest):
        tmp, (ss, rs) = rest[:8], rest[8:]
        net = Net(ss, rs)
        z, x, c, y = net.z, net.x, net.c, net.y
        net.barrier(PLANE + RING + ("yo",))
        for b in range(2):
            block = z * 8 + b * 4 + x
            trunk, parent_block, leaf, branch = block_place(segs, parents, block)

            def place(kb, carry):
                slot = jnp.where(kb < 16, kb & 7, jnp.where(kb == block, 9, 8))
                valid = jnp.where(
                    kb < 16,
                    (kb >> 3) == trunk,
                    ((kb == block) & branch) | ((kb == parent_block) & leaf),
                )
                value = jnp.where(valid, slots[b, slot], jnp.zeros((256, 256), BF16))
                at = (kb >> 3, (kb >> 2) & 1, kb & 3)
                if b == 0:
                    full[at] = value
                else:
                    full[at] = full[at] + value
                return carry

            lax.fori_loop(0, 32, place, 0)
        k = [net.slot() for _ in range(8)]
        net.send(full.at[:, 1 - c], from_core, k[0], "c")
        net.got(from_core, k[0])
        for zz in range(4):
            for xx in range(4):
                held[zz, xx] = (full[zz, c, xx].astype(F32) + from_core[zz, xx].astype(F32)).astype(BF16)

        def view(zz, half, xx, part):
            rows = pl.ds(0, 256) if half == BOTH else pl.ds(128 * half, 128)
            return held.at[zz, xx, rows, pl.ds(part * 128, 128)]

        run_all(plane_scatter(net, view, tmp))
        mine = held.at[z, x]

        def rows(yy):
            return pl.ds(pl.multiple_of(yy * 64, 64), 64)

        for i, (name, d) in enumerate((("yu", net.yu), ("yd", net.yd), ("yo", net.yo))):
            net.send(mine.at[rows(d)], ring.at[i], k[1 + i], name)
        for i in range(3):
            net.got(ring.at[i], k[1 + i])
        own = held[z, x, rows(y)].astype(F32)
        for i in range(3):
            own = own + ring[i].astype(F32)
        out[c, rows(y)] = own.astype(BF16)
        view = out.at[c, rows(y)]
        for i, name in enumerate(("yu", "yd", "yo")):
            net.send(view, view, k[4 + i], name)
        for i, d in enumerate((net.yd, net.yu, net.yo)):
            net.got(out.at[c, rows(d)], k[4 + i])
        net.send(out.at[c], out.at[c], k[7], "c")
        net.got(out.at[1 - c], k[7])
        net.finish()

    return pl.pallas_call(
        kernel,
        out_shape=jax.ShapeDtypeStruct((2, 256, 256), BF16),
        in_specs=[INS, INS, INV],
        out_specs=INV,
        scratch_shapes=[
            VMEM((4, 2, 4, 256, 256), BF16),
            VMEM((4, 4, 256, 256), BF16),
            VMEM((4, 4, 256, 256), BF16),
            VMEM((3, 64, 256), BF16),
            VMEM((2, 4, 128, 128), BF16),
            VMEM((2, 4, 128, 128), BF16),
            VMEM((2, 4, 256, 128), BF16),
            VMEM((2, 4, 256, 128), BF16),
            VMEM((2, 128, 128), BF16),
            VMEM((2, 128, 128), BF16),
            VMEM((2, 256, 128), BF16),
            VMEM((2, 256, 128), BF16),
        ]
        + sems(16 + 8),
        compiler_params=params(6),
        name="scatter_kv",
    )(segs, parents, slots)


def closing(back, tokens, dx1, from_kv, gain, sums, grad_q, small):
    def kernel(back, tokens, dx1, from_kv, gain, sums, gq, small, grad_input, out_q, vec, small_out,
               vecs, vec_z, vec_x, lone, small_z, small_x, small_y, swap, *rest):
        first, tmp, (ss, rs) = rest[:4], rest[4:12], rest[12:]
        net = Net(ss, rs)
        z, yh, x, y, c = net.z, net.yh, net.x, net.y, net.c
        net.barrier(PLANE + RING + ("yo", "xo", "zo"))

        def rows():
            def total(summed):
                grad = summed + from_kv[...]
                norm, inverse = normed(tokens[...].astype(F32))
                grad_input[...] = dx1[...] + norm_back(grad, norm, inverse, gain[...])
                one = jnp.sum(grad * norm, axis=0, keepdims=True)
                two = jnp.sum(grad, axis=0, keepdims=True)
                vecs[y, c] = jnp.concatenate([one, two, sums[2:8]], axis=0)

            yield from group_scatter(net, back, *first, total)
            k = [net.slot() for _ in range(13)]
            at = vecs.at[y, c]
            for i, name in enumerate(("yu", "yd", "yo", "c")):
                net.send(at, at, k[i], name)
            yield
            for i, d in enumerate((net.yd, net.yu, net.yo)):
                net.got(vecs.at[d, c], k[i])
                net.send(vecs.at[d, c], vecs.at[d, c], k[4 + i], "c")
            yield
            for i, d in enumerate((y, net.yd, net.yu, net.yo)):
                net.got(vecs.at[d, 1 - c], k[3 + i])
            acc = vecs[0, 0]
            for i in range(1, 8):
                acc = acc + vecs[i // 2, i % 2]
            for i in range(4):
                vec_z[i] = acc[:, i * 512 : (i + 1) * 512]
            for i, (name, d) in enumerate((("zu", net.zu), ("zd", net.zd), ("zo", net.zo))):
                net.send(vec_z.at[d], vec_z.at[4 + i], k[7 + i], name)
            yield
            for i in range(3):
                net.got(vec_z.at[4 + i], k[7 + i])
            acc = vec_z[z] + vec_z[4] + vec_z[5] + vec_z[6]
            vec_x[0] = jnp.where(yh == 0, acc[:, :256], acc[:, 256:])
            for i, name in enumerate(("xu", "xd", "xo")):
                net.send(vec_x.at[0], vec_x.at[1 + i], k[10 + i], name)
            yield
            for i in range(3):
                net.got(vec_x.at[1 + i], k[10 + i])
            vec[...] = vec_x[0] + vec_x[1] + vec_x[2] + vec_x[3]

        def small_sums():
            k = [net.slot() for _ in range(7)]
            for i, (name, d) in enumerate((("zu", net.zu), ("zd", net.zd), ("zo", net.zo))):
                net.send(small.at[d], small_z.at[i], k[i], name)
            yield
            for i in range(3):
                net.got(small_z.at[i], k[i])
            for xx in range(4):
                small_x[xx] = small[z, xx] + small_z[0, xx] + small_z[1, xx] + small_z[2, xx]
            for i, (name, d) in enumerate((("xu", net.xu), ("xd", net.xd), ("xo", net.xo))):
                net.send(small_x.at[d], small_x.at[4 + i], k[3 + i], name)
            yield
            for i in range(3):
                net.got(small_x.at[4 + i], k[3 + i])
            lone[...] = small_x[x] + small_x[4] + small_x[5] + small_x[6]
            net.send(lone, small_y, k[6], "yo")
            yield
            net.got(small_y, k[6])
            small_out[0] = lone[...]
            small_out[1] = small_y[...]

        run_all(rows(), weight_scatter(net, gq, tmp, swap, out_q), small_sums())
        net.finish()

    n, d = tokens.shape
    w = grad_q.shape[-1]
    tile = small.shape[-2:]
    return pl.pallas_call(
        kernel,
        out_shape=(
            jax.ShapeDtypeStruct((n, d), F32),
            jax.ShapeDtypeStruct((n, 2 * w), F32),
            jax.ShapeDtypeStruct((8, 256), F32),
            jax.ShapeDtypeStruct((2,) + tile, F32),
        ),
        in_specs=[INV] * 8,
        out_specs=(INV,) * 4,
        scratch_shapes=[
            VMEM((4, 2, 8, d), F32),
            VMEM((7, 8, 512), F32),
            VMEM((4, 8, 256), F32),
            VMEM(tile, F32),
            VMEM((3, 4) + tile, F32),
            VMEM((7,) + tile, F32),
            VMEM(tile, F32),
            VMEM((n, w), BF16),
        ]
        + scatter_scratch(n, d)
        + plane_scratch(n, w // 2)
        + sems(8 + 13 + 7 + 17),
        compiler_params=params(7),
        name="closing",
    )(back, tokens, dx1, from_kv, gain, sums, grad_q, small)


def local(
    tokens,
    cotangent,
    seg_ids,
    parents,
    tau,
    w_query,
    w_up,
    w_out,
    w_down,
    query_bias,
    up_bias,
    w_keyval,
    value_bias,
    norm1_gain,
    norm1_bias,
    norm2_gain,
    norm2_bias,
    out_bias,
    down_bias,
):
    z, yh, x, yl, c = (lax.axis_index(a) for a in AXES)
    tp = yl * 2 + c
    d = tokens.shape[1]

    def dot(left, right, dims):
        return lax.dot_general(left, right, ((dims[:1], dims[1:]), ((), ())), preferred_element_type=F32)

    def halves(weight):
        w = weight.shape[1] // 2
        return (
            lax.dynamic_slice_in_dim(weight, yh * w, w, 1),
            lax.dynamic_slice_in_dim(weight, (1 - yh) * w, w, 1),
        )

    def lanes(values):
        flat = values.reshape(1, -1).astype(BF16)
        return jnp.pad(flat, ((0, 0), (0, 128 - flat.shape[1])))

    pieces = [norm1_gain, norm1_bias, norm2_gain, norm2_bias, out_bias, down_bias, value_bias, up_bias, query_bias]
    pieces = [lanes(v) for v in pieces] + [lanes(seg_ids[:1])]
    small = jnp.concatenate(pieces + [jnp.zeros((16 - len(pieces), 128), BF16)], axis=0)
    small = jnp.concatenate([w_keyval, small], axis=1)
    tok_all, cot_all, small_all, wq, wo = opening(
        tokens, cotangent, small, *halves(w_query), *halves(w_out)
    )
    tok_all = tok_all.reshape(512, d)
    cot_all = cot_all.reshape(512, d)
    wq = wq.reshape(d, -1)
    wo = wo.reshape(d, -1)
    small_all = small_all.reshape(4, 2, 4, 4, 16, 384).transpose(0, 1, 3, 2, 4, 5)
    w_kv = small_all[..., :256].reshape(d, 256)
    tail = small_all[..., 256:]
    vectors = tail[..., :6, :16].transpose(4, 0, 1, 2, 3, 5).reshape(6, d).astype(F32)
    gain1, shift1, gain2, shift2, bias_out, bias_down = (vectors[i : i + 1] for i in range(6))
    value_full = tail[..., 6, 0].reshape(128).astype(F32)
    mine = lax.dynamic_index_in_dim(tail, tp, axis=3, keepdims=False)
    ub = lax.dynamic_slice_in_dim(mine[..., 7, :64].reshape(128, 16), yh * 8, 8, 1)
    ub = ub.T.reshape(1, 1024).astype(F32)
    qb = lax.dynamic_slice_in_dim(mine[..., 8, :16].reshape(128, 4), yh * 2, 2, 1)
    qb = qb.T.reshape(1, 256).astype(F32)
    segs = tail[..., 0, 9, 0].reshape(32).astype(jnp.int32)

    h1 = (normed(tok_all.astype(F32))[0] * gain1 + shift1).astype(BF16)
    q = (dot(h1, wq, (1, 0)) + qb).astype(BF16)
    kv = (dot(h1, w_kv, (1, 0)) + jnp.concatenate([jnp.zeros((128,), F32), value_full])).astype(BF16)
    kv_all = gather_kv(kv.reshape(2, 256, 256)).reshape(32, 256, 256)
    q_blocks = q.reshape(2, 256, 256)
    o, log_sum, tops = attend(q_blocks, kv_all, segs, parents)
    o_rows = o.reshape(512, 256)
    attn = dot(o_rows, wo, (1, 1)).astype(BF16).reshape(4, 2, 64, d)
    x1, h2, best = middle(attn, tokens, bias_out, gain2, shift2, tops.reshape(16, 128))
    h2 = h2.reshape(512, d)
    wu, wd = gather_ff(*halves(w_up), *halves(w_down))
    wu = wu.reshape(d, -1)
    wd = wd.reshape(d, -1)

    limit = tau[0]
    head_max = best.reshape(4, 8, 128)[:, 0, 0]
    factor = limit / jnp.maximum(head_max, limit)
    clipped_query = (w_query.astype(F32) * jnp.repeat(factor, 128)[None, :]).astype(BF16)
    clipped_bias = (query_bias.astype(F32) * factor[None, :]).astype(BF16)

    def gate(values):
        return jax.nn.gelu(values, approximate=True)

    u = dot(h2, wu, (1, 0)) + ub
    a, gate_back = jax.vjp(gate, u)
    a = a.astype(BF16)
    mlp = dot(a, wd, (1, 1)).astype(BF16).reshape(4, 2, 64, d)
    du = gate_back(dot(cot_all, wd, (1, 0)))[0].astype(BF16)
    grad_ub = jnp.sum(du.astype(F32), axis=0)
    grad_down = dot(cot_all, a, (0, 0)).astype(BF16)
    grad_up = dot(h2, du, (0, 0)).astype(BF16)
    back2 = dot(du, wu, (1, 1)).astype(BF16).reshape(4, 2, 64, d)
    output, dx1, dz, sums = turn(mlp, back2, x1, cotangent, gain2, bias_down)
    dz = dz.reshape(512, d)
    go = dot(dz, wo, (1, 0)).astype(BF16).reshape(2, 256, 256)
    grad_out = dot(dz, o_rows, (0, 0)).astype(BF16)
    up_sum, down_sum, out_sum = scatter_weights(
        [v.reshape(4, 2, 4, 64, -1) for v in (grad_up, grad_down, grad_out)], 8
    )
    dq, slots = attend_back(q_blocks, kv_all, o, go, log_sum, segs, parents)
    dq = dq.reshape(512, 256)
    dkv = scatter_kv(slots, segs, parents).reshape(512, 256)
    back1 = dot(dq, wq, (1, 1)).astype(BF16).reshape(4, 2, 64, d)
    grad_q = dot(h1, dq, (0, 0)).astype(BF16).reshape(4, 2, 4, 64, 256)
    grad_kv = dot(h1, dkv, (0, 0)).reshape(4, 2, 4, 4, 16, 256)
    grad_kv = lax.dynamic_index_in_dim(lax.dynamic_index_in_dim(grad_kv, yh, 1, False), tp, 2, False)
    dkv_own = lax.dynamic_slice_in_dim(dkv, yh * 256 + tp * 64, 64, 0)
    from_kv = dot(dkv_own, w_kv, (1, 1))
    gqb = jnp.sum(dq.astype(F32), axis=0).reshape(2, 128).T.reshape(4, 2, 4, 8)
    gub = grad_ub.reshape(8, 128).T.reshape(4, 2, 4, 32)
    gvb = jnp.sum(dkv[:, 128:].astype(F32), axis=0).reshape(4, 2, 4, 4)
    gvb = lax.dynamic_index_in_dim(lax.dynamic_index_in_dim(gvb, yh, 1, False), tp, 2, False)
    bias_rows = jnp.concatenate([gqb, gub], axis=3).transpose(0, 2, 1, 3)
    bias_rows = jnp.pad(bias_rows, ((0, 0), (0, 0), (0, 1), (0, 256 - 40)))
    bias_rows = bias_rows.at[:, :, 2, 0].set(gvb)
    bias_rows = jnp.pad(bias_rows, ((0, 0), (0, 0), (0, 5), (0, 0)))
    small_grads = jnp.concatenate([grad_kv, bias_rows], axis=2)
    grad_input, query_sum, vec, small_sum = closing(
        back1, tokens, dx1, from_kv, gain1, sums, grad_q, small_grads
    )
    keyval_sum = small_sum[0, :16]
    valueb_sum = small_sum[0, 18, :1]
    own_bias = lax.dynamic_index_in_dim(small_sum[0, 16:18, :40], yh, 0, False)
    oth_bias = lax.dynamic_index_in_dim(small_sum[1, 16:18, :40], yh, 0, False)
    first = jnp.where(yh == 0, own_bias, oth_bias)
    second = jnp.where(yh == 0, oth_bias, own_bias)
    qbias_sum = jnp.concatenate([first[:8].reshape(4, 2), second[:8].reshape(4, 2)], axis=1)
    ubias_sum = jnp.concatenate([first[8:].reshape(4, 8), second[8:].reshape(4, 8)], axis=1)
    vec = lax.dynamic_slice(vec, (jnp.int32(0), x * 64 + tp * 16), (6, 16))
    return (
        output,
        grad_input,
        query_sum,
        up_sum,
        out_sum,
        down_sum,
        qbias_sum,
        ubias_sum,
        keyval_sum,
        valueb_sum,
        vec[0],
        vec[1],
        vec[2],
        vec[3],
        vec[4],
        vec[5],
        clipped_query,
        clipped_bias,
    )


def solution(mesh):
    fine = Mesh(mesh.devices.reshape(4, 2, 4, 2, 2), AXES)
    dp, tp = ("z", "yh", "x"), ("yl", "c")
    rows, flat, weight = P(AXES, None), P(AXES), P(dp, tp)
    in_specs = (rows, rows, P(dp), P(), P()) + (weight,) * 6 + (rows,) + (flat,) * 7
    out_specs = (rows, rows) + (weight,) * 6 + (rows,) + (flat,) * 7 + (weight, weight)
    return jax.shard_map(local, mesh=fine, in_specs=in_specs, out_specs=out_specs, check_vma=False)
```

time: 3110 us -> 484 us (0.16)
  waiting for transfers between devices: 2120 us -> 0 us
  blocking collectives: 679 us -> 0 us
  Pallas kernels: 0 us -> 377 us
  matrix products: 159 us -> 44.6 us
  other arithmetic: 80.9 us -> 13.3 us
    reduce_scatter x9 -> x0, waiting for transfers between devices: 1540 us -> none  [the longest x1 615 us: local(): lax.psum_scatter(grad_keyvals, ('dp', 'tp'), scatter_dimension=0, tiled=T...]
    all_gather x10 -> x0, waiting for transfers between devices: 386 us -> none  [the longest x1 194 us: local(): lax.all_gather(w_keyval, ('dp', 'tp'), axis=0, tiled=True)]
    pallas_call x0 -> x10, Pallas kernels: none -> 377 us  [the longest x1 62.8 us: scatter_weights(): pl.pallas_call(kernel, out_shape=tuple((jax.ShapeDtypeStruct((g.shape[-2]...]
    unnamed x3 -> x0, blocking collectives: 315 us -> none
    all_gather x3 -> x0, blocking collectives: 275 us -> none  [the longest x1 95 us: local(): lax.all_gather(up_bias, 'dp', axis=0, tiled=True)]
    unnamed x21 -> x0, waiting for transfers between devices: 203 us -> none
    dot_general x30 -> x15, matrix products: 159 us -> 44.6 us  [dot(): lax.dot_general(left, right, ((dims[:1], dims[1:]), ((), ())), preferred_...]
    pmax x1 -> x0, blocking collectives: 89 us -> none  [local(): head_max = lax.pmax(head_top, 'dp')]
  transfers between devices with their start and end apart: 20 -> 0, of which waited for: 15 -> 0; matrix products, arithmetic and copies ran while one was open for 4% -> 0% of each run, Pallas kernels for 0% -> 0%
where the time goes in v1:
time: 484 us; the launch traced here: 477 us
  Pallas kernels  377 us (78%)
  matrix products  44.6 us (9%)
  local copies, waits for them, and re-layouts  39.1 us (8%)
  other arithmetic  13.3 us (3%)
    pallas_call x1, Pallas kernels, scatter_weights(): pl.pallas_call(kernel, out_shape=tuple((jax.ShapeDtypeStruct((g.shape[-2]...  62.8 us
    pallas_call x1, Pallas kernels, gather_ff(): pl.pallas_call(kernel, out_shape=(shape, shape), in_specs=[ANY] * 4, out_...  54.5 us
    pallas_call x1, Pallas kernels, opening(): pl.pallas_call(kernel, out_shape=(rows, rows, jax.ShapeDtypeStruct((4, 8,...  48.4 us
    dot_general x15, matrix products, dot(): lax.dot_general(left, right, ((dims[:1], dims[1:]), ((), ())), preferred_...  44.6 us
    pallas_call x1, Pallas kernels, scatter_kv(): pl.pallas_call(kernel, out_shape=jax.ShapeDtypeStruct((2, 256, 256), BF16...  42.6 us
    pallas_call x1, Pallas kernels, turn(): pl.pallas_call(kernel, out_shape=(jax.ShapeDtypeStruct((n, d), BF16), jax...  39.1 us
    pallas_call x1, Pallas kernels, closing(): pl.pallas_call(kernel, out_shape=(jax.ShapeDtypeStruct((n, d), F32), jax....  35.2 us
    pallas_call x1, Pallas kernels, middle(): pl.pallas_call(kernel, out_shape=(jax.ShapeDtypeStruct((n, d), F32), jax....  33.8 us

profile of v1, /device:TPU:0, one launch (start us, length us, event | category | flops | bytes accessed | tf_op | source)
XLA Modules:
  0.0 476.6 jit_solution(1943459759669530116)
XLA Ops:
  2.7 0.8 reshape.389
  7.5 0.8 reshape.390
  8.3 1.3 pad_maximum_fusion.small
  9.6 1.5 constant_dynamic-slice_fusion.8
  11.1 1.9 constant_dynamic-slice_fusion.4
  13.0 48.4 %opening.1 = (bf16[4,2,64,2048]{3,2,1,0:T(8,128)(2,1)}, bf16[4,2,64,2048]{3,2,1,0:T(8,128)(2,1)}, bf16[4,8,4,16,384]{4,3,2,1,0:T(8,128)(2,1)}, bf16[4,2,4,64,256...) custom-call(bf16[64,2048]{1,0:T(8,128)(2,1)} %tokens.3, bf16[64,2048]{1,0:T(8,128)(2,1)} %cot.3, ...), custom_call_target="tpu_custom_call" | custom-call | tf_op jit(solution)/shard_map/opening/pallas_call | solution.py:385
  61.4 1.7 copy.85
  63.1 1.1 copy-done.1
  66.8 1.0 slice.201
  68.8 1.1 slice.198
  71.7 1.0 convert_bitcast_fusion
  72.7 2.3 slice.200
  76.1 1.4 copy.67
  79.9 0.7 slice.165.bias
  80.7 2.1 add_convert_fusion
  82.9 2.2 fusion.3
  85.0 2.9 copy.75
  88.0 3.2 fusion.12
  91.1 1.4 fusion.11
  92.6 30.5 %gather_kv.1 = bf16[4,2,4,256,256]{4,3,2,1,0:T(8,128)(2,1)} custom-call(bf16[2,256,256]{2,1,0:T(8,128)(2,1)} %bitcast.164), custom_call_target="tpu_custom_call" | custom-call | tf_op jit(solution)/shard_map/gather_kv/pallas_call | solution.py:450
  123.0 13.3 %attend.1 = (bf16[2,256,256]{2,1,0:T(8,128)(2,1)}, f32[2,8,512]{2,1,0:T(8,128)}, f32[2,8,128]{2,1,0:T(8,128)}) custom-call(s32[32]{0:T(128)} %reshape.423.segs, s32[18]{0:T(128)} %parents.5, bf16[2,256,256]{2,1,0:T(8,128)(2,1)} %bitcast.153, bf16[32,256,256]{2,1,0:T(8,128)(2,1)} %bitcast.127), custom_call_target="tpu_custom_call" | custom-call | tf_op jit(solution)/shard_map/attend/pallas_call | solution.py:524
  136.4 3.1 convolution_convert_fusion.5
  139.4 33.8 %middle.1 = (f32[64,2048]{1,0:T(8,128)}, bf16[4,2,64,2048]{3,2,1,0:T(8,128)(2,1)}, f32[2,16,128]{2,1,0:T(8,128)}) custom-call(bf16[4,2,64,2048]{3,2,1,0:T(8,128)(2,1)} %bitcast.132, bf16[64,2048]{1,0:T(8,128)(2,1)} %tokens.3, f32[1,2048]{1,0:T(1,128)} %slice.165.bias, f32[1,2048]{1,0:T(1,128)} %slice.167.gain, f32[1,2048]{1,0:T(1,128)} %slice.169.shift, ...), custom_call_target="tpu_custom_call" | custom-call | tf_op jit(solution)/shard_map/middle/pallas_call | solution.py:633
  173.2 0.7 slice.208
  175.3 54.5 %gather_ff.1 = (bf16[4,2,4,64,1024]{4,3,2,1,0:T(8,128)(2,1)}, bf16[4,2,4,64,1024]{4,3,2,1,0:T(8,128)(2,1)}) custom-call(bf16[64,1024]{1,0:T(8,128)(2,1)} %get-tuple-element.108.ua, bf16[64,1024]{1,0:T(8,128)(2,1)} %get-tuple-element.109.ub, bf16[64,1024]{1,0:T(8,128)(2,1)} %get-tuple-element.91.da, bf16[64,1024]{1,0:T(8,128)(2,1)} %get-tuple-element.90.db), custom_call_target="tpu_custom_call" | custom-call | tf_op jit(solution)/shard_map/gather_ff/pallas_call | solution.py:420
  229.8 5.3 %fusion.20 = f32[512,1024]{1,0:T(8,128)S(1)} fusion(bf16[512,2048]{1,0:T(8,128)(2,1)} %bitcast.178, bf16[2048,1024]{1,0:T(8,128)(2,1)} %bitcast.174), kind=kOutput, calls=%fused_computation.87 | convolution fusion | flops 2147483648 | bytes 8388608 | tf_op jit(solution)/shard_map/dot_general | solution.py:990
  235.2 3.5 convert_reduce_fusion.1
  238.7 3.9 convolution_convert_fusion.4
  242.6 4.5 convolution_convert_fusion
  247.1 3.9 convolution_convert_fusion.3
  251.0 39.1 %turn.1 = (bf16[64,2048]{1,0:T(8,128)(2,1)}, f32[64,2048]{1,0:T(8,128)}, bf16[4,2,64,2048]{3,2,1,0:T(8,128)(2,1)}, f32[8,2048]{1,0:T(8,128)}) custom-call(bf16[4,2,64,2048]{3,2,1,0:T(8,128)(2,1)} %bitcast.145, bf16[4,2,64,2048]{3,2,1,0:T(8,128)(2,1)} %bitcast.146, f32[64,2048]{1,0:T(8,128)} %get-tuple-element.66.x1, bf16[64,2048]{1,0:T(8,128)(2,1)} %cot.3, ...), custom_call_target="tpu_custom_call" | custom-call | tf_op jit(solution)/shard_map/turn/pallas_call | solution.py:714
  290.1 3.2 convolution_convert_fusion.8
  293.3 1.8 convolution_convert_fusion.6
  295.0 16.5 %attend_back.1 = (bf16[2,256,256]{2,1,0:T(8,128)(2,1)}, bf16[2,10,256,256]{3,2,1,0:T(8,128)(2,1)}) custom-call(s32[32]{0:T(128)} %reshape.423.segs, s32[18]{0:T(128)} %parents.5, bf16[2,256,256]{2,1,0:T(8,128)(2,1)} %bitcast.154, bf16[32,256,256]{2,1,0:T(8,128)(2,1)} %bitcast.128, bf16[2,256,256]{2,1,0:T(8,128)(2,1)} %get-tuple-element.59.o, ...), custom_call_target="tpu_custom_call" | custom-call | tf_op jit(solution)/shard_map/attend_back/pallas_call | solution.py:579
  311.5 42.6 %scatter_kv.1 = bf16[2,256,256]{2,1,0:T(8,128)(2,1)} custom-call(s32[32]{0:T(128)} %reshape.423.segs, s32[18]{0:T(128)} %parents.5, bf16[2,10,256,256]{3,2,1,0:T(8,128)(2,1)} %get-tuple-element.72.slots), custom_call_target="tpu_custom_call" | custom-call | tf_op jit(solution)/shard_map/scatter_kv/pallas_call | solution.py:836
  354.1 2.0 fusion.13.from_kv
  356.1 1.7 convolution_convert_fusion.7
  360.0 0.8 select_maximum_fusion.small
  360.8 2.1 convolution_convert_fusion.2
  362.8 35.2 %closing.1 = (f32[64,2048]{1,0:T(8,128)}, f32[64,512]{1,0:T(8,128)}, f32[8,256]{1,0:T(8,128)}, f32[2,24,256]{2,1,0:T(8,128)}) custom-call(bf16[4,2,64,2048]{3,2,1,0:T(8,128)(2,1)} %bitcast.131, bf16[64,2048]{1,0:T(8,128)(2,1)} %tokens.3, f32[64,2048]{1,0:T(8,128)} %get-tuple-element.71.dx1, f32[64,2048]{1,0:T(8,128)} %fusion.13.from_kv, ...), custom_call_target="tpu_custom_call" | custom-call | tf_op jit(solution)/shard_map/closing/pallas_call | solution.py:936
  398.1 1.2 slice.186
  400.0 1.3 slice_bitcast_fusion
  403.2 0.8 constant_dynamic-slice_fusion
  404.5 4.4 convolution_convert_fusion.1
  408.8 62.8 %scatter_weights.1 = (f32[64,2048]{1,0:T(8,128)}, f32[64,2048]{1,0:T(8,128)}, f32[64,512]{1,0:T(8,128)}) custom-call(bf16[4,2,4,64,1024]{4,3,2,1,0:T(8,128)(2,1)} %bitcast.139, bf16[4,2,4,64,1024]{4,3,2,1,0:T(8,128)(2,1)} %bitcast.138, bf16[4,2,4,64,256]{4,3,2,1,0:T(8,128)(2,1)} %bitcast.151), custom_call_target="tpu_custom_call" | custom-call | tf_op jit(solution)/shard_map/scatter_weights/pallas_call | solution.py:765
  472.4 0.8 copy.96
  473.9 0.8 copy.98
  475.4 0.8 copy.100
  (139 shorter events, 22.3 us)
Async XLA Ops:
  61.4 4.2 copy-start
  63.1 1.1 copy-start.1
  85.0 2.9 copy-start.26
  87.9 3.2 copy-start.2
  87.9 3.2 copy-start.5
  87.9 3.2 copy-start.19
  123.0 13.3 %copy-start.7 = (bf16[4,2,4,64,256]{4,3,2,1,0:T(8,128)(2,1)S(1)}, bf16[4,2,4,64,256]{4,3,2,1,0:T(8,128)(2,1)}, u32[]{:S(2)}) copy-start(bf16[4,2,4,64,256]{4,3,2,1,0:T(8,128)(2,1)} %get-tuple-element.60) | copy-start | bytes 3145732
  136.3 37.7 %copy-start.20 = (bf16[4,4]{1,0:T(4,128)(2,1)S(1)}, bf16[4,4]{1,0:T(4,128)(2,1)}, u32[]{:S(2)}) copy-start(bf16[4,4]{1,0:T(4,128)(2,1)} %param.30) | copy-start | bytes 100
  136.3 38.3 %copy-start.15 = (bf16[64,512]{1,0:T(8,128)(2,1)S(1)}, bf16[64,512]{1,0:T(8,128)(2,1)}, u32[]{:S(2)}) copy-start(bf16[64,512]{1,0:T(8,128)(2,1)} %param.26) | copy-start | bytes 196612
  229.8 5.3 %copy-start.18 = (f32[8,128]{1,0:T(8,128)S(1)}, f32[8,128]{1,0:T(8,128)}, u32[]{:S(2)}) copy-start(f32[8,128]{1,0:T(8,128)} %copy.72) | copy-start | bytes 12292
  229.8 5.3 %copy-start.22 = (bf16[4,2,4,64,1024]{4,3,2,1,0:T(8,128)(2,1)S(1)}, bf16[4,2,4,64,1024]{4,3,2,1,0:T(8,128)(2,1)}, u32[]{:S(2)}) copy-start(bf16[4,2,4,64,1024]{4,3,2,1,0:T(8,128)(2,1)} %get-tuple-element.64) | copy-start | bytes 12582916
  229.8 5.3 %copy-start.24 = (bf16[4,2,64,2048]{3,2,1,0:T(8,128)(2,1)S(1)}, bf16[4,2,64,2048]{3,2,1,0:T(8,128)(2,1)}, u32[]{:S(2)}) copy-start(bf16[4,2,64,2048]{3,2,1,0:T(8,128)(2,1)} %get-tuple-element.65) | copy-start | bytes 6291460
  238.7 8.4 %copy-start.27 = (bf16[512,1024]{1,0:T(8,128)(2,1)}, bf16[512,1024]{1,0:T(8,128)(2,1)S(1)}, u32[]{:S(2)}) copy-start(bf16[512,1024]{1,0:T(8,128)(2,1)S(1)} %get-tuple-element.83) | copy-start | bytes 3145732
  242.6 4.5 copy-start.21
  251.0 39.1 %copy-start.8 = (bf16[4,2,4,64,256]{4,3,2,1,0:T(8,128)(2,1)S(1)}, bf16[4,2,4,64,256]{4,3,2,1,0:T(8,128)(2,1)}, u32[]{:S(2)}) copy-start(bf16[4,2,4,64,256]{4,3,2,1,0:T(8,128)(2,1)} %get-tuple-element.60) | copy-start | bytes 3145732
  290.1 3.2 copy-start.9
  290.1 3.2 copy-start.25
  311.5 44.6 %copy-start.3 = (bf16[4,2,64,2048]{3,2,1,0:T(8,128)(2,1)S(1)}, bf16[4,2,64,2048]{3,2,1,0:T(8,128)(2,1)}, u32[]{:S(2)}) copy-start(bf16[4,2,64,2048]{3,2,1,0:T(8,128)(2,1)} %add_convert_fusion) | copy-start | bytes 6291460
  311.5 44.6 %copy-start.10 = (bf16[2,256,256]{2,1,0:T(8,128)(2,1)S(1)}, bf16[2,256,256]{2,1,0:T(8,128)(2,1)}, u32[]{:S(2)}) copy-start(bf16[2,256,256]{2,1,0:T(8,128)(2,1)} %get-tuple-element.70) | copy-start | bytes 786436
  356.1 1.8 copy-start.4
  358.6 2.2 copy-start.6
  362.8 41.6 %copy-start.23 = (bf16[4,2,64,2048]{3,2,1,0:T(8,128)(2,1)S(1)}, bf16[4,2,64,2048]{3,2,1,0:T(8,128)(2,1)}, u32[]{:S(2)}) copy-start(bf16[4,2,64,2048]{3,2,1,0:T(8,128)(2,1)} %get-tuple-element.62) | copy-start | bytes 6291460
  362.8 41.6 %copy-start.28 = (bf16[512,1024]{1,0:T(8,128)(2,1)S(1)}, bf16[512,1024]{1,0:T(8,128)(2,1)}, u32[]{:S(2)}) copy-start(bf16[512,1024]{1,0:T(8,128)(2,1)} %copy-done.27) | copy-start | bytes 3145732
  408.8 62.9 %copy-start.14 = (bf16[64,2048]{1,0:T(8,128)(2,1)S(1)}, bf16[64,2048]{1,0:T(8,128)(2,1)}, u32[]{:S(2)}) copy-start(bf16[64,2048]{1,0:T(8,128)(2,1)} %get-tuple-element.130) | copy-start | bytes 786436
  408.8 63.6 %copy-start.11 = (f32[64,2048]{1,0:T(8,128)S(1)}, f32[64,2048]{1,0:T(8,128)}, u32[]{:S(2)}) copy-start(f32[64,2048]{1,0:T(8,128)} %get-tuple-element.131) | copy-start | bytes 1572868
  408.8 64.4 %copy-start.16 = (f32[64,512]{1,0:T(8,128)S(1)}, f32[64,512]{1,0:T(8,128)}, u32[]{:S(2)}) copy-start(f32[64,512]{1,0:T(8,128)} %get-tuple-element.132) | copy-start | bytes 393220
  471.7 2.2 copy-start.13
  471.7 3.0 copy-start.17
  471.7 3.6 copy-start.12

commit v2 on v1

--- a/solution.py
+++ b/solution.py
@@ -116,13 +116,15 @@
     net.got(out.at[yo, 1 - c, hi], k[8])
 
 
-def group_scatter(net, part, from_core, held, from_half, from_full, total):
+def group_scatter(net, part, from_core, held, from_half, from_full, total, make=None):
     y, c, yu, yd, yo = net.y, net.c, net.yu, net.yd, net.yo
     k = [net.slot() for _ in range(8)]
     n = part.shape[2]
     half = n // 2
     lo, hi = pl.ds(0, half), pl.ds(half, half)
     for i, d in enumerate((yo, yu, yd, y)):
+        if make is not None:
+            make(i, d)
         net.send(part.at[d, 1 - c], from_core.at[d], k[i], "c")
 
     def core_sum(i, d):
@@ -313,149 +315,347 @@
 RING = ("yu", "yd", "c")
 
 
-def opening(tokens, cotangent, small, wq_own, wq_oth, wo_own, wo_oth):
-    def kernel(tok, cot, small, qa, qb, oa, ob, tok_out, cot_out, small_out, q_out, o_out, local, ss, rs):
+class Ticks:
+    def __init__(self, *steps):
+        self.steps = list(steps)
+
+    def tick(self, count=1):
+        for _ in range(count):
+            for one in self.steps:
+                next(one, None)
+
+
+def weight_gather(net, weight, out, local):
+    z, yh, x = net.z, net.yh, net.x
+    n, w = weight.shape[0], weight.shape[1] // 2
+    k = net.slot()
+
+    def half(which):
+        return weight.at[:, pl.ds(pl.multiple_of(which * w, 128), w)]
+
+    mine = pltpu.make_async_copy(half(yh), out.at[z, yh, x, pl.ds(0, n)], local)
+    mine.start()
+    net.send(half(1 - yh), out.at[z, yh, x, pl.ds(0, n)], k, "yo")
+    yield
+    mine.wait()
+    net.got(out.at[z, 1 - yh, x, pl.ds(0, n)], k)
+    yield from plane_gather(net, column_view(out))
+
+
+def splat(row, lane, at):
+    return jnp.sum(jnp.where(lane == at, row, 0.0), axis=1, keepdims=True)
+
+
+def place_of(segs, parents, block):
+    lane = lax.broadcasted_iota(jnp.int32, (1, 128), 1)
+    seg = splat(segs, lane, block)
+    lanes = lane.astype(F32)
+    parent = splat(parents, lanes, seg)
+    trunk = splat(parents, lanes, parent)
+    leaf = (seg >= 10.0).astype(F32)
+    branch = (seg >= 2.0).astype(F32)
+    above = [(splat(segs, lane, b) == parent).astype(F32) * leaf for b in range(16, 32)]
+    return trunk, leaf, branch, above
+
+
+def wide(value):
+    return jnp.broadcast_to(value, (1, 128)).astype(BF16)
+
+
+def trunk_block(kv, which, i, trunk):
+    one = wide(trunk)
+    return kv[which, 0, i // 4, i % 4] * (1 - one) + kv[which, 1, i // 4, i % 4] * one
+
+
+def parent_block(kv, which, above):
+    total = kv[which, 2, 0, 0] * wide(above[0])
+    for j in range(1, 16):
+        total = total + kv[which, 2 + j // 8, j // 4 % 2, j % 4] * wide(above[j])
+    return total
+
+
+NT = (((1,), (1,)), ((), ()))
+TN = (((0,), (0,)), ((), ()))
+SCALE = 128**-0.5
+
+
+def attend(b, z, x, q, kv, segs, parents, scores, o, log_sum):
+    lane = (lax.broadcasted_iota(jnp.int32, (256, 512), 1) & 255).astype(F32)
+    row = lax.broadcasted_iota(jnp.int32, (256, 512), 0).astype(F32)
+    block = z * 8 + b * 4 + x
+    trunk, leaf, branch, above = place_of(segs, parents, block)
+    rows = pl.ds(b * 256, 256)
+    both = jnp.concatenate([q[rows, :128], q[rows, 128:]], axis=0)
+    start = block.astype(F32) - 8.0 * trunk
+
+    def score(key):
+        return lax.dot_general(key, both, NT, preferred_element_type=F32) * SCALE
+
+    def trunk_score(i, top):
+        gap = (start - i.astype(F32)) * 256.0
+        s = jnp.where(row - lane <= gap, score(trunk_block(kv, 0, i, trunk)), NEG)
+        scores[i] = s
+        return jnp.maximum(top, jnp.max(s, axis=0, keepdims=True))
+
+    top = lax.fori_loop(0, 8, trunk_score, jnp.full((1, 512), NEG, F32))
+    s = score(parent_block(kv, 0, above)) + (leaf - 1.0) * 1e30
+    scores[8] = s
+    top = jnp.maximum(top, jnp.max(s, axis=0, keepdims=True))
+    s = jnp.where(row <= lane, score(kv[0, z, b, x]), NEG) + (branch - 1.0) * 1e30
+    scores[9] = s
+    top = jnp.maximum(top, jnp.max(s, axis=0, keepdims=True))
+
+    def weigh(i, value, carry):
+        acc, total = carry
+        w = jnp.exp(scores[i] - top)
+        acc = acc + lax.dot_general(value, w.astype(BF16), TN, preferred_element_type=F32)
+        return acc, total + jnp.sum(w, axis=0, keepdims=True)
+
+    carry = (jnp.zeros((128, 512), F32), jnp.zeros((1, 512), F32))
+    carry = lax.fori_loop(0, 8, lambda i, c: weigh(i, trunk_block(kv, 1, i, trunk), c), carry)
+    carry = weigh(8, parent_block(kv, 1, above), carry)
+    acc, total = weigh(9, kv[1, z, b, x], carry)
+    heads = (acc / total).T.astype(BF16)
+    o[rows, :128] = heads[:256]
+    o[rows, 128:] = heads[256:]
+    log_sum[b] = jnp.broadcast_to(top + jnp.log(total), (8, 512))
+    return top
+
+
+def forward(tokens, cotangent, pack, biases, parents, w_query, w_out, w_up, w_down):
+    def kernel(tok, cot, pack, biases, parents, wq_in, wo_in, wu_in, wd_in,
+               cot_out, h2, wu, wd, wq_out, wo_out, pack_out, h1_out, q_out, kv_out, o, log_sum, x1, best, vec, ub,
+               tok_all, h1, packs, wq, wo, q, kv, scores, part, own, mine, got, local, *rest):
+        *scratch, ss, rs = rest
         net = Net(ss, rs)
-        z, yh, x, yl, c = net.z, net.yh, net.x, net.yl, net.c
-        locals_ = [
+        z, yh, x, yl, c, y = net.z, net.yh, net.x, net.yl, net.c, net.y
+        starts = [
             pltpu.make_async_copy(src, dst, local.at[i])
             for i, (src, dst) in enumerate(
                 (
-                    (qa, q_out.at[z, yh, x]),
-                    (oa, o_out.at[z, yh, x]),
-                    (tok, tok_out.at[net.y, c]),
-                    (cot, cot_out.at[net.y, c]),
-                    (small, small_out.at[z, net.y * 2 + c, x]),
+                    (tok, tok_all.at[y, c]),
+                    (cot, cot_out.at[y, c]),
+                    (pack.at[c], packs.at[z, yh, x, yl, c]),
+                    (biases.at[yh], wq.at[z, yh, x, pl.ds(64, 16)]),
                 )
             )
         ]
-        for one in locals_:
+        for one in starts:
             one.start()
         net.barrier(PLANE + RING + ("yo",))
 
-        def weight(own, oth, out, i):
-            k = net.slot()
-            net.send(oth, out.at[z, yh, x], k, "yo")
+        def parameters():
+            k = [net.slot() for _ in range(4)]
+            pair = packs.at[z, yh, x, yl]
+            net.send(pack.at[1 - c], packs.at[z, yh, x, yl, c], k[0], "c")
             yield
-            locals_[i].wait()
-            net.got(out.at[z, 1 - yh, x], k)
-            yield from plane_gather(net, column_view(out))
-
-        def small_all():
-            k = [net.slot() for _ in range(7)]
-            y = net.y
-
-            def at(yy, cc):
-                return small_out.at[z, yy * 2 + cc, x]
-
-            net.send(small, at(y, c), k[0], "yu")
-            net.send(small, at(y, c), k[1], "yd")
-            net.send(small, at(y, c), k[2], "yo")
-            net.send(small, at(y, c), k[3], "c")
+            starts[2].wait()
+            net.got(packs.at[z, yh, x, yl, 1 - c], k[0])
+            for i, name in enumerate(("yu", "yd", "yo")):
+                net.send(pair, pair, k[1 + i], name)
             yield
             for i, d in enumerate((net.yd, net.yu, net.yo)):
-                net.got(at(d, c), k[i])
-                net.send(at(d, c), at(d, c), k[4 + i], "c")
+                net.got(packs.at[z, d // 2, x, lax.rem(d, 2)], k[1 + i])
+
+            def view(zz, half, xx, part):
+                return packs.at[zz, part, xx, pl.ds(0, 2) if half == BOTH else half]
+
+            yield from plane_gather(net, view)
+
+        def bias():
+            k = net.slot()
+            there = wq.at[z, yh, x, pl.ds(64, 16)]
+            net.send(biases.at[1 - yh], there, k, "yo")
             yield
-            for i, d in enumerate((y, net.yd, net.yu, net.yo)):
-                net.got(at(d, 1 - c), k[3 + i])
-            locals_[4].wait()
-
-            def view(zz, half, xx, part):
-                which = pl.ds(0, 8) if half == BOTH else pl.ds(4 * half, 4)
-                cols = pl.ds(0, 256) if part == 0 else pl.ds(256, 128)
-                return small_out.at[zz, which, xx, :, cols]
-
-            yield from plane_gather(net, view)
-
-        run_all(
-            small_all(),
-            weight(qa, qb, q_out, 0),
-            weight(oa, ob, o_out, 1),
-            group_gather(net, tok, tok_out),
-            group_gather(net, cot, cot_out),
+            starts[3].wait()
+            net.got(wq.at[z, 1 - yh, x, pl.ds(64, 16)], k)
+
+        def query():
+            steps = weight_gather(net, wq_in, wq, local.at[4])
+            next(steps)
+            yield from bias()
+            yield from steps
+
+        later = Ticks(
+            weight_gather(net, wo_in, wo, local.at[5]),
+            weight_gather(net, wu_in, wu, local.at[6]),
+            weight_gather(net, wd_in, wd, local.at[7]),
         )
-        locals_[2].wait()
-        locals_[3].wait()
+
+        def start_later():
+            yield
+            later.tick()
+
+        run_all(group_gather(net, tok, tok_all), parameters(), query(), start_later())
+        starts[0].wait()
+        later.tick()
+
+        lane = lax.broadcasted_iota(jnp.int32, (16, 128), 1)
+        values = jnp.zeros((16, 128), F32)
+        segs = jnp.zeros((16, 128), F32)
+        for j in range(16):
+            block = jnp.zeros((16, 128), F32)
+            for k in range(8):
+                dev = 8 * j + k
+                dp, tp = dev // 4, dev % 4
+                tile = packs[dp // 8, dp // 4 % 2, dp % 4, tp // 2, tp % 2, 16:32].astype(F32)
+                block = jnp.where(lane // 16 == k, tile, block)
+                values = jnp.where(lane == dev, tile, values)
+                if tp == 0:
+                    segs = jnp.where(lane == dp, tile, segs)
+            vec[:, j * 128 : (j + 1) * 128] = block
+        value_bias = values[6:7]
+        segs = segs[7:8]
+        vec[8:9, 0:128] = segs
+        query_bias = jnp.zeros((16, 256), F32)
+        lane = lax.broadcasted_iota(jnp.int32, (16, 256), 1) & 127
+        for dp in range(32):
+            tile = wq[dp // 8, dp // 4 % 2, dp % 4, 64:80].astype(F32)
+            query_bias = jnp.where(lane // 4 == dp, tile, query_bias)
+        ub[...] = query_bias[:8, 128:]
+        query_bias = jnp.concatenate([query_bias[0:1, :128], query_bias[1:2, :128]], axis=1)
+
+        gain1, shift1 = vec[0:1], vec[1:2]
+
+        def norm_rows(i, carry):
+            rows = tok_all[i // 2, i % 2].astype(F32)
+            h1[pl.ds(pl.multiple_of(i * 64, 64), 64)] = (normed(rows)[0] * gain1 + shift1).astype(BF16)
+            return carry
+
+        lax.fori_loop(0, 8, norm_rows, 0)
+
+        def project(i, carry):
+            rows = pl.ds(pl.multiple_of(i * 256, 256), 256)
+            h = h1[rows]
+            weight = wq[:, :, :, :64].reshape(2048, 256)
+            q[rows] = (jnp.dot(h, weight, preferred_element_type=F32) + query_bias).astype(BF16)
+            weight = packs[:, :, :, :, :, :16].reshape(2048, 128)
+            shift = value_bias * c.astype(F32)
+            kv[c, z, i, x] = (jnp.dot(h, weight, preferred_element_type=F32) + shift).astype(BF16)
+            return carry
+
+        lax.fori_loop(0, 2, project, 0)
+
+        def view(zz, half, xx, part):
+            rows = pl.ds(0, 256) if half == BOTH else pl.ds(128 * half, 128)
+            return kv.at[c, zz, part, xx, rows]
+
+        keys = plane_gather(net, view)
+        cots = group_gather(net, cot, cot_out)
+        next(keys)
+        later.tick()
+        next(cots)
+        next(keys)
+        next(keys)
+        next(cots)
+        next(keys)
+        later.tick()
+        for _ in keys:
+            pass
+        k = net.slot()
+        net.send(kv.at[c], kv.at[c], k, "c")
+        next(cots)
+        net.got(kv.at[1 - c], k)
+
+        saves = [
+            pltpu.make_async_copy(src, dst, local.at[8 + i])
+            for i, (src, dst) in enumerate(
+                ((wq, wq_out), (packs, pack_out), (h1, h1_out), (q, q_out), (kv, kv_out), (wo, wo_out))
+            )
+        ]
+        for one in saves[:5]:
+            one.start()
+        parent = parents[0:1]
+        top = attend(0, z, x, q, kv, segs, parent, scores, o, log_sum)
+        next(later.steps[0], None)
+        top = jnp.maximum(top, attend(1, z, x, q, kv, segs, parent, scores, o, log_sum))
+        for h in range(2):
+            mine[0, 8 * h : 8 * h + 8] = jnp.full((8, 128), jnp.max(top[:, h * 256 : (h + 1) * 256]), F32)
+        for _ in later.steps[0]:
+            pass
+        saves[5].start()
+        later.tick()
+
+        def project_out(i, d):
+            rows = o[pl.ds(pl.multiple_of(d * 128, 128), 128)]
+            for j in range(4):
+                weight = wo[j].reshape(512, 256)
+                out = lax.dot_general(rows, weight, NT, preferred_element_type=F32).astype(BF16)
+                part[d, 0, :, j * 512 : (j + 1) * 512] = out[:64]
+                part[d, 1, :, j * 512 : (j + 1) * 512] = out[64:]
+
+        def rows():
+            def total(summed):
+                value = tok[...].astype(F32) + (summed + vec[4:5])
+                x1[...] = value
+                own[...] = (normed(value)[0] * vec[2:3] + vec[3:4]).astype(BF16)
+
+            yield from group_scatter(net, part, *scratch, total, project_out)
+            me = pltpu.make_async_copy(own, h2.at[y, c], local.at[14])
+            me.start()
+            yield from group_gather(net, own, h2)
+            me.wait()
+
+        run_all(rows(), heads_max(net, mine, got, best))
+        for _ in cots:
+            pass
+        later.tick()
+        starts[1].wait()
+        for one in saves:
+            one.wait()
         net.finish()
 
     n, d = tokens.shape
-    weight = jax.ShapeDtypeStruct((4, 2, 4, n, wq_own.shape[1]), BF16)
     rows = jax.ShapeDtypeStruct((4, 2, n, d), BF16)
+
+    def bf(*shape):
+        return jax.ShapeDtypeStruct(shape, BF16)
+
+    def f32(*shape):
+        return jax.ShapeDtypeStruct(shape, F32)
+
     return pl.pallas_call(
         kernel,
-        out_shape=(rows, rows, jax.ShapeDtypeStruct((4, 8, 4) + small.shape, BF16), weight, weight),
-        in_specs=[ANY] * 7,
-        out_specs=(ANY,) * 5,
-        scratch_shapes=[pltpu.SemaphoreType.DMA((5,))] + sems(17 * 2 + 7 + 16 + 18),
+        out_shape=(
+            rows,
+            rows,
+            bf(4, 2, 4, n, 1024),
+            bf(4, 2, 4, n, 1024),
+            bf(4, 2, 4, 80, 256),
+            bf(4, 2, 4, n, 256),
+            bf(4, 2, 4, 2, 2, 32, 128),
+            bf(512, d),
+            bf(512, 256),
+            bf(2, 4, 2, 4, 256, 128),
+            bf(512, 256),
+            f32(2, 8, 512),
+            f32(n, d),
+            f32(2, 16, 128),
+            f32(16, d),
+            f32(8, 128),
+        ),
+        in_specs=[INV, ANY, INV, INV, INV, ANY, ANY, ANY, ANY],
+        out_specs=(ANY,) * 10 + (INV,) * 6,
+        scratch_shapes=[
+            VMEM((4, 2, n, d), BF16),
+            VMEM((512, d), BF16),
+            VMEM((4, 2, 4, 2, 2, 32, 128), BF16),
+            VMEM((4, 2, 4, 80, 256), BF16),
+            VMEM((4, 2, 4, n, 256), BF16),
+            VMEM((512, 256), BF16),
+            VMEM((2, 4, 2, 4, 256, 128), BF16),
+            VMEM((10, 256, 512), F32),
+            VMEM((4, 2, n, d), BF16),
+            VMEM((n, d), BF16),
+            VMEM((5, 16, 128), F32),
+            VMEM((7, 16, 128), F32),
+            pltpu.SemaphoreType.DMA((15,)),
+        ]
+        + scatter_scratch(n, d)
+        + sems(160),
         compiler_params=params(1),
-        name="opening",
-    )(tokens, cotangent, small, wq_own, wq_oth, wo_own, wo_oth)
-
-
-def gather_ff(up_own, up_oth, dn_own, dn_oth):
-    def kernel(ua, ub, da, db, u_out, d_out, local, ss, rs):
-        net = Net(ss, rs)
-        z, yh, x = net.z, net.yh, net.x
-        mine = [
-            pltpu.make_async_copy(ua, u_out.at[z, yh, x], local.at[0]),
-            pltpu.make_async_copy(da, d_out.at[z, yh, x], local.at[1]),
-        ]
-        for one in mine:
-            one.start()
-        net.barrier(PLANE + ("yo",))
-
-        def weight(oth, out, one):
-            k = net.slot()
-            net.send(oth, out.at[z, yh, x], k, "yo")
-            yield
-            one.wait()
-            net.got(out.at[z, 1 - yh, x], k)
-            yield from plane_gather(net, column_view(out))
-
-        run_all(weight(ub, u_out, mine[0]), weight(db, d_out, mine[1]))
-        net.finish()
-
-    shape = jax.ShapeDtypeStruct((4, 2, 4) + up_own.shape, BF16)
-    return pl.pallas_call(
-        kernel,
-        out_shape=(shape, shape),
-        in_specs=[ANY] * 4,
-        out_specs=(ANY, ANY),
-        scratch_shapes=[pltpu.SemaphoreType.DMA((2,))] + sems(34),
-        compiler_params=params(2),
-        name="gather_ff",
-    )(up_own, up_oth, dn_own, dn_oth)
-
-
-def gather_kv(kv):
-    def kernel(kv, out, local, ss, rs):
-        net = Net(ss, rs)
-        z, x, c = net.z, net.x, net.c
-        me = pltpu.make_async_copy(kv.at[c], out.at[z, c, x], local)
-        me.start()
-        net.barrier(PLANE + ("c",))
-        me.wait()
-
-        def view(zz, half, xx, part):
-            rows = pl.ds(0, 256) if half == BOTH else pl.ds(128 * half, 128)
-            return out.at[zz, c, xx, rows, pl.ds(part * 128, 128)]
-
-        run_all(plane_gather(net, view))
-        k = net.slot()
-        net.send(out.at[:, c], out.at[:, c], k, "c")
-        net.got(out.at[:, 1 - c], k)
-        net.finish()
-
-    return pl.pallas_call(
-        kernel,
-        out_shape=jax.ShapeDtypeStruct((4, 2, 4, 256, 256), BF16),
-        in_specs=[ANY],
-        out_specs=ANY,
-        scratch_shapes=[pltpu.SemaphoreType.DMA] + sems(17),
-        compiler_params=params(3),
-        name="gather_kv",
-    )(kv)
+        name="forward",
+    )(tokens, cotangent, pack, biases, parents, w_query, w_out, w_up, w_down)
 
 
 def block_place(segs, parents, block):
@@ -466,74 +666,6 @@
     for b in range(16, 32):
         parent_block = jnp.where(segs[b] == parent, b, parent_block)
     return trunk, parent_block, seg >= 10, seg >= 2
-
-
-def attend(q, kv, segs, parents):
-    def kernel(segs, parents, q, kv, o, log_sum, tops, scores):
-        z, x = lax.axis_index("z"), lax.axis_index("x")
-        lane = lax.broadcasted_iota(jnp.int32, (256, 512), 1) & 255
-        row = lax.broadcasted_iota(jnp.int32, (256, 512), 0)
-        best = []
-        for b in range(2):
-            block = z * 8 + b * 4 + x
-            trunk, parent_block, leaf, branch = block_place(segs, parents, block)
-            both = jnp.concatenate([q[b, :, :128], q[b, :, 128:]], axis=0)
-
-            def score(key_block):
-                return (
-                    lax.dot_general(
-                        kv[key_block, :, :128], both, (((1,), (1,)), ((), ())), preferred_element_type=F32
-                    )
-                    * 128**-0.5
-                )
-
-            def trunk_score(i, top):
-                s = score(trunk * 8 + i)
-                gap = (block - trunk * 8 - i) * 256
-                s = jnp.where(row - lane <= gap, s, NEG)
-                scores[i] = s
-                return jnp.maximum(top, jnp.max(s, axis=0, keepdims=True))
-
-            top = lax.fori_loop(0, 8, trunk_score, jnp.full((1, 512), NEG, F32))
-            s = jnp.where(leaf, score(parent_block), NEG)
-            scores[8] = s
-            top = jnp.maximum(top, jnp.max(s, axis=0, keepdims=True))
-            s = jnp.where((row <= lane) & branch, score(block), NEG)
-            scores[9] = s
-            top = jnp.maximum(top, jnp.max(s, axis=0, keepdims=True))
-
-            def weigh(i, carry):
-                acc, total = carry
-                w = jnp.exp(scores[i] - top)
-                key_block = jnp.where(i < 8, trunk * 8 + i, jnp.where(i == 8, parent_block, block))
-                acc = acc + lax.dot_general(
-                    kv[key_block, :, 128:], w.astype(BF16), (((0,), (0,)), ((), ())), preferred_element_type=F32
-                )
-                return acc, total + jnp.sum(w, axis=0, keepdims=True)
-
-            acc, total = lax.fori_loop(0, 10, weigh, (jnp.zeros((128, 512), F32), jnp.zeros((1, 512), F32)))
-            heads = (acc / total).T.astype(BF16)
-            o[b, :, :128] = heads[:256]
-            o[b, :, 128:] = heads[256:]
-            log_sum[b] = jnp.broadcast_to(top + jnp.log(total), (8, 512))
-            best.append(top)
-        top = jnp.maximum(best[0], best[1])
-        for h in range(2):
-            tops[h] = jnp.full((8, 128), jnp.max(top[:, h * 256 : (h + 1) * 256]), F32)
-
-    return pl.pallas_call(
-        kernel,
-        out_shape=(
-            jax.ShapeDtypeStruct((2, 256, 256), BF16),
-            jax.ShapeDtypeStruct((2, 8, 512), F32),
-            jax.ShapeDtypeStruct((2, 8, 128), F32),
-        ),
-        in_specs=[INS, INS, INV, INV],
-        out_specs=(INV, INV, INV),
-        scratch_shapes=[VMEM((10, 256, 512), F32)],
-        compiler_params=pltpu.CompilerParams(vmem_limit_bytes=56 << 20),
-        name="attend",
-    )(segs, parents, q, kv)
 
 
 def attend_back(q, kv, o, go, log_sum, segs, parents):
@@ -602,54 +734,6 @@
         - jnp.mean(scaled, axis=-1, keepdims=True)
         - norm * jnp.mean(scaled * norm, axis=-1, keepdims=True)
     )
-
-
-def middle(part, tokens, out_bias, gain, shift, tops):
-    def kernel(part, tokens, bias, gain, shift, tops, x1, h2, best, own, mine, got, local, *rest):
-        *scratch, ss, rs = rest
-        net = Net(ss, rs)
-        net.barrier(PLANE + RING + ("yo",))
-
-        def rows():
-            def total(summed):
-                value = tokens[...].astype(F32) + (summed + bias[...])
-                x1[...] = value
-                own[...] = (normed(value)[0] * gain[...] + shift[...]).astype(BF16)
-
-            yield from group_scatter(net, part, *scratch, total)
-            me = pltpu.make_async_copy(own, h2.at[net.y, net.c], local)
-            me.start()
-            yield from group_gather(net, own, h2)
-            me.wait()
-
-        def largest():
-            mine[0] = tops[...]
-            yield from heads_max(net, mine, got, best)
-
-        run_all(rows(), largest())
-        net.finish()
-
-    n, d = tokens.shape
-    return pl.pallas_call(
-        kernel,
-        out_shape=(
-            jax.ShapeDtypeStruct((n, d), F32),
-            jax.ShapeDtypeStruct((4, 2, n, d), BF16),
-            jax.ShapeDtypeStruct((2, 16, 128), F32),
-        ),
-        in_specs=[INV] * 6,
-        out_specs=(INV, ANY, INV),
-        scratch_shapes=[
-            VMEM((n, d), BF16),
-            VMEM((5, 16, 128), F32),
-            VMEM((7, 16, 128), F32),
-            pltpu.SemaphoreType.DMA,
-        ]
-        + scatter_scratch(n, d)
-        + sems(9 + 8 + 7),
-        compiler_params=params(4),
-        name="middle",
-    )(part, tokens, out_bias, gain, shift, tops)
 
 
 def heads_max(net, mine, got, best):
@@ -989,55 +1073,32 @@
     def dot(left, right, dims):
         return lax.dot_general(left, right, ((dims[:1], dims[1:]), ((), ())), preferred_element_type=F32)
 
-    def halves(weight):
-        w = weight.shape[1] // 2
-        return (
-            lax.dynamic_slice_in_dim(weight, yh * w, w, 1),
-            lax.dynamic_slice_in_dim(weight, (1 - yh) * w, w, 1),
-        )
-
-    def lanes(values):
-        flat = values.reshape(1, -1).astype(BF16)
-        return jnp.pad(flat, ((0, 0), (0, 128 - flat.shape[1])))
-
-    pieces = [norm1_gain, norm1_bias, norm2_gain, norm2_bias, out_bias, down_bias, value_bias, up_bias, query_bias]
-    pieces = [lanes(v) for v in pieces] + [lanes(seg_ids[:1])]
-    small = jnp.concatenate(pieces + [jnp.zeros((16 - len(pieces), 128), BF16)], axis=0)
-    small = jnp.concatenate([w_keyval, small], axis=1)
-    tok_all, cot_all, small_all, wq, wo = opening(
-        tokens, cotangent, small, *halves(w_query), *halves(w_out)
+    def row(values):
+        return jnp.tile(values.astype(BF16).reshape(1, -1), (1, 128 // values.size))
+
+    tile = [row(v) for v in (norm1_gain, norm1_bias, norm2_gain, norm2_bias, out_bias, down_bias, value_bias, seg_ids[:1])]
+    tile = jnp.concatenate(tile + [jnp.zeros((8, 128), BF16)], axis=0)
+    pack = jnp.stack([jnp.concatenate([w_keyval[:, :128], tile]), jnp.concatenate([w_keyval[:, 128:], tile])])
+    qbt = jnp.pad(jnp.tile(query_bias.T, (1, 32)).reshape(2, 2, 128), ((0, 0), (0, 14), (0, 0)))
+    ubt = jnp.pad(jnp.tile(up_bias.T, (1, 32)).reshape(2, 8, 128), ((0, 0), (0, 8), (0, 0)))
+    biases = jnp.concatenate([qbt, ubt], axis=2)
+    ancestors = jnp.pad(jnp.broadcast_to(parents.astype(F32)[None], (8, 18)), ((0, 0), (0, 110)))
+    (cot_all, h2, wu, wd, wq, wo, packs, h1, q, kv6, o_rows, log_sum, x1, best, vec, ub) = forward(
+        tokens, cotangent, pack, biases, ancestors, w_query, w_out, w_up, w_down
     )
-    tok_all = tok_all.reshape(512, d)
     cot_all = cot_all.reshape(512, d)
-    wq = wq.reshape(d, -1)
+    wq = wq[:, :, :, :64].reshape(d, -1)
     wo = wo.reshape(d, -1)
-    small_all = small_all.reshape(4, 2, 4, 4, 16, 384).transpose(0, 1, 3, 2, 4, 5)
-    w_kv = small_all[..., :256].reshape(d, 256)
-    tail = small_all[..., 256:]
-    vectors = tail[..., :6, :16].transpose(4, 0, 1, 2, 3, 5).reshape(6, d).astype(F32)
-    gain1, shift1, gain2, shift2, bias_out, bias_down = (vectors[i : i + 1] for i in range(6))
-    value_full = tail[..., 6, 0].reshape(128).astype(F32)
-    mine = lax.dynamic_index_in_dim(tail, tp, axis=3, keepdims=False)
-    ub = lax.dynamic_slice_in_dim(mine[..., 7, :64].reshape(128, 16), yh * 8, 8, 1)
-    ub = ub.T.reshape(1, 1024).astype(F32)
-    qb = lax.dynamic_slice_in_dim(mine[..., 8, :16].reshape(128, 4), yh * 2, 2, 1)
-    qb = qb.T.reshape(1, 256).astype(F32)
-    segs = tail[..., 0, 9, 0].reshape(32).astype(jnp.int32)
-
-    h1 = (normed(tok_all.astype(F32))[0] * gain1 + shift1).astype(BF16)
-    q = (dot(h1, wq, (1, 0)) + qb).astype(BF16)
-    kv = (dot(h1, w_kv, (1, 0)) + jnp.concatenate([jnp.zeros((128,), F32), value_full])).astype(BF16)
-    kv_all = gather_kv(kv.reshape(2, 256, 256)).reshape(32, 256, 256)
-    q_blocks = q.reshape(2, 256, 256)
-    o, log_sum, tops = attend(q_blocks, kv_all, segs, parents)
-    o_rows = o.reshape(512, 256)
-    attn = dot(o_rows, wo, (1, 1)).astype(BF16).reshape(4, 2, 64, d)
-    x1, h2, best = middle(attn, tokens, bias_out, gain2, shift2, tops.reshape(16, 128))
-    h2 = h2.reshape(512, d)
-    wu, wd = gather_ff(*halves(w_up), *halves(w_down))
     wu = wu.reshape(d, -1)
     wd = wd.reshape(d, -1)
-
+    h2 = h2.reshape(512, d)
+    w_kv = lax.all_gather(packs[..., :16, :].reshape(d, 128), "c", axis=1, tiled=True)
+    gain1, shift1, gain2, shift2, bias_out, bias_down = (vec[i : i + 1] for i in range(6))
+    segs = vec[8, :32].astype(jnp.int32)
+    ub = ub.reshape(1, 1024)
+    q_blocks = q.reshape(2, 256, 256)
+    o = o_rows.reshape(2, 256, 256)
+    kv_all = kv6.reshape(2, 32, 256, 128).transpose(1, 2, 0, 3).reshape(32, 256, 256)
     limit = tau[0]
     head_max = best.reshape(4, 8, 128)[:, 0, 0]
     factor = limit / jnp.maximum(head_max, limit)

time: 484 us -> 434 us (0.90)
  Pallas kernels: 377 us -> 322 us
  between operations: 2.93 us -> 15.9 us
  matrix products: 44.6 us -> 38.5 us
  other arithmetic: 13.3 us -> 8.24 us
    pallas_call x5 -> x1, Pallas kernels: 180 us -> 126 us  [forward(): pl.pallas_call(kernel, out_shape=(rows, rows, bf(4, 2, 4, n, 1024), bf(4,...]
    reshape x3 -> x2, local copies, waits for them, and re-layouts: 3.27 us -> 16.1 us  [local(): kv6.reshape(2, 32, 256, 128).transpose(1, 2, 0, 3).reshape(32, 256, 256)]
    slice x19 -> x4, local copies, waits for them, and re-layouts: 10.3 us -> 4.26 us  [the longest x1 1.87 us: local(): packs[..., :16, :].reshape(d, 128)]
    dot_general x15 -> x12, matrix products: 44.6 us -> 38.5 us  [dot(): lax.dot_general(left, right, ((dims[:1], dims[1:]), ((), ())), preferred_...]
    another operation x2 -> x19, local copies, waits for them, and re-layouts: 0.17 us -> 5.5 us  [the longest x14 4.53 us: row(): return jnp.tile(values.astype(BF16).reshape(1, -1), (1, 128 // values.size))]
  transfers between devices with their start and end apart: 0 -> 1, of which waited for: 0 -> 0; matrix products, arithmetic and copies ran while one was open for 0% -> 15% of each run, Pallas kernels for 0% -> 37%
where the time goes in v2:
time: 434 us; the launch traced here: 429 us
  Pallas kernels  322 us (74%)
  local copies, waits for them, and re-layouts  43.9 us (10%)
  matrix products  38.5 us (9%)
  between operations  15.9 us (4%)
  other arithmetic  8.24 us (2%)
    pallas_call x1, Pallas kernels, forward(): pl.pallas_call(kernel, out_shape=(rows, rows, bf(4, 2, 4, n, 1024), bf(4,...  126 us
    pallas_call x1, Pallas kernels, scatter_weights(): pl.pallas_call(kernel, out_shape=tuple((jax.ShapeDtypeStruct((g.shape[-2]...  64.5 us
    pallas_call x1, Pallas kernels, turn(): pl.pallas_call(kernel, out_shape=(jax.ShapeDtypeStruct((n, d), BF16), jax...  39.5 us
    pallas_call x1, Pallas kernels, scatter_kv(): pl.pallas_call(kernel, out_shape=jax.ShapeDtypeStruct((2, 256, 256), BF16...  39 us
    dot_general x12, matrix products, dot(): lax.dot_general(left, right, ((dims[:1], dims[1:]), ((), ())), preferred_...  38.5 us
    pallas_call x1, Pallas kernels, closing(): pl.pallas_call(kernel, out_shape=(jax.ShapeDtypeStruct((n, d), F32), jax....  36.5 us
    pallas_call x1, Pallas kernels, attend_back(): pl.pallas_call(kernel, out_shape=(jax.ShapeDtypeStruct((2, 256, 256), BF1...  16.5 us
    reshape x2, local copies, waits for them, and re-layouts, local(): kv6.reshape(2, 32, 256, 128).transpose(1, 2, 0, 3).reshape(32, 256, 256)  16.1 us
  transfers between devices with their start and end apart: 1, of which 0 were waited for; matrix products, arithmetic and copies ran while one was open for 15% of the time, Pallas kernels for 37%

profile of v2, /device:TPU:0, one launch (start us, length us, event | category | flops | bytes accessed | tf_op | source)
XLA Modules:
  0.0 428.8 jit_solution(3824920999968002138)
XLA Ops:
  7.9 0.7 convert.3
  8.6 0.7 convert_element_type.71
  9.2 0.8 copy.51
  10.0 0.7 tile.80
  10.8 0.7 tile.82
  11.5 0.7 tile.84
  12.3 0.7 tile.86
  13.0 0.7 tile.88
  13.8 0.7 tile.90
  14.5 0.7 fusion.16
  15.5 0.7 tile.98
  18.2 126.2 %forward.1 = (bf16[4,2,64,2048]{3,2,1,0:T(8,128)(2,1)}, bf16[4,2,64,2048]{3,2,1,0:T(8,128)(2,1)}, bf16[4,2,4,64,1024]{4,3,2,1,0:T(8,128)(2,1)}, bf16[4,2,4,64,10...) custom-call(bf16[64,2048]{1,0:T(8,128)(2,1)} %tokens.1, ...), custom_call_target="tpu_custom_call" | custom-call | tf_op jit(solution)/shard_map/forward/pallas_call | solution.py:617
  144.4 1.9 slice.128
  146.3 1.2 convert_bitcast_fusion.segs
  147.5 1.6 fusion.14
  149.1 5.3 %fusion.17 = f32[512,1024]{1,0:T(8,128)S(1)} fusion(bf16[512,2048]{1,0:T(8,128)(2,1)} %bitcast.130, bf16[2048,1024]{1,0:T(8,128)(2,1)} %bitcast.126), kind=kOutput, calls=%fused_computation.62 | convolution fusion | flops 2147483648 | bytes 8388608 | tf_op jit(solution)/shard_map/dot_general | solution.py:1074
  154.4 3.9 convolution_convert_fusion.4
  158.3 3.5 convert_reduce_fusion
  161.9 4.8 %convolution_convert_fusion = bf16[2048,1024]{1,0:T(8,128)(2,1)} fusion(bf16[512,2048]{1,0:T(8,128)(2,1)S(1)} %bitcast.133, f32[512,1024]{1,0:T(8,128)S(1)} %fusion.17, f32[1024]{0:T(1024)S(1)} %bitcast.139), kind=kOutput, calls=%fused_computation.1 | convolution fusion | flops 2154823680 | bytes 8392704 | tf_op jit(solution)/shard_map/dot_general | solution.py:1074
  166.7 3.7 convolution_convert_fusion.3
  170.4 4.4 %convolution_convert_fusion.1 = bf16[2048,1024]{1,0:T(8,128)(2,1)} fusion(bf16[512,2048]{1,0:T(8,128)(2,1)S(1)} %bitcast.131, bf16[512,1024]{1,0:T(8,128)(2,1)S(1)} %get-tuple-element.89), kind=kOutput, calls=%fused_computation.2 | convolution fusion | flops 2149580800 | bytes 7340032 | tf_op jit(solution)/shard_map/dot_general | solution.py:1074
  175.4 0.7 slice.151
  177.0 39.5 %turn.1 = (bf16[64,2048]{1,0:T(8,128)(2,1)}, f32[64,2048]{1,0:T(8,128)}, bf16[4,2,64,2048]{3,2,1,0:T(8,128)(2,1)}, f32[8,2048]{1,0:T(8,128)}) custom-call(bf16[4,2,64,2048]{3,2,1,0:T(8,128)(2,1)} %bitcast.105, bf16[4,2,64,2048]{3,2,1,0:T(8,128)(2,1)} %bitcast.106, f32[64,2048]{1,0:T(8,128)} %get-tuple-element.64.x1, bf16[64,2048]{1,0:T(8,128)(2,1)} %cot.3, ...), custom_call_target="tpu_custom_call" | custom-call | tf_op jit(solution)/shard_map/turn/pallas_call | solution.py:798
  216.5 3.2 convolution_convert_fusion.7
  219.7 1.8 convolution_convert_fusion.5
  221.6 64.5 %scatter_weights.1 = (f32[64,2048]{1,0:T(8,128)}, f32[64,2048]{1,0:T(8,128)}, f32[64,512]{1,0:T(8,128)}) custom-call(bf16[4,2,4,64,1024]{4,3,2,1,0:T(8,128)(2,1)} %bitcast.102, bf16[4,2,4,64,1024]{4,3,2,1,0:T(8,128)(2,1)} %bitcast.101, bf16[4,2,4,64,256]{4,3,2,1,0:T(8,128)(2,1)} %bitcast.112), custom_call_target="tpu_custom_call" | custom-call | tf_op jit(solution)/shard_map/scatter_weights/pallas_call | solution.py:849
  286.1 3.3 copy.54
  289.4 8.5 %copy.64 = bf16[2,32,256,128]{3,0,2,1:T(2,128)(2,1)} copy(bf16[2,32,256,128]{3,2,1,0:T(8,128)(2,1)} %bitcast.100) | data formatting | bytes 8388608 | tf_op jit(solution)/shard_map/reshape | solution.py:1101
  297.9 7.6 %reshape.273.kv = bf16[32,256,256]{2,1,0:T(8,128)(2,1)} reshape(bf16[32,256,2,128]{3,2,1,0:T(2,128)(2,1)} %bitcast.97) | data formatting | bytes 8388608 | tf_op jit(solution)/shard_map/reshape | solution.py:1101
  305.5 16.5 %attend_back.1 = (bf16[2,256,256]{2,1,0:T(8,128)(2,1)}, bf16[2,10,256,256]{3,2,1,0:T(8,128)(2,1)}) custom-call(s32[32]{0:T(128)} %convert_bitcast_fusion.segs, s32[18]{0:T(128)} %parents.3, bf16[2,256,256]{2,1,0:T(8,128)(2,1)} %bitcast.115, bf16[32,256,256]{2,1,0:T(8,128)(2,1)} %reshape.273.kv, bf16[2,256,256]{2,1,0:T(8,128)(2,1)} %bitcast.116, ...), custom_call_target="tpu_custom_call" | custom-call | tf_op jit(solution)/shard_map/attend_back/pallas_call | solution.py:711
  322.0 39.0 %scatter_kv.1 = bf16[2,256,256]{2,1,0:T(8,128)(2,1)} custom-call(s32[32]{0:T(128)} %convert_bitcast_fusion.segs, s32[18]{0:T(128)} %parents.3, bf16[2,10,256,256]{3,2,1,0:T(8,128)(2,1)} %get-tuple-element.76.slots), custom_call_target="tpu_custom_call" | custom-call | tf_op jit(solution)/shard_map/scatter_kv/pallas_call | solution.py:920
  361.0 1.0 convert_reduce_fusion.2
  362.2 1.7 fusion.18
  364.7 0.8 select_maximum_fusion.small
  366.2 2.1 convolution_convert_fusion.2
  368.3 1.8 convolution_convert_fusion.6
  370.1 2.5 fusion.7.from_kv
  372.5 36.5 %closing.1 = (f32[64,2048]{1,0:T(8,128)}, f32[64,512]{1,0:T(8,128)}, f32[8,256]{1,0:T(8,128)}, f32[2,24,256]{2,1,0:T(8,128)}) custom-call(bf16[4,2,64,2048]{3,2,1,0:T(8,128)(2,1)} %bitcast.99, bf16[64,2048]{1,0:T(8,128)(2,1)} %tokens.1, f32[64,2048]{1,0:T(8,128)} %get-tuple-element.75.dx1, f32[64,2048]{1,0:T(8,128)} %fusion.7.from_kv, ...), custom_call_target="tpu_custom_call" | custom-call | tf_op jit(solution)/shard_map/closing/pallas_call | solution.py:1020
  409.1 1.3 slice.142
  410.3 0.7 fusion.15
  411.0 1.3 slice_bitcast_fusion
  412.8 0.8 constant_dynamic-slice_fusion
  415.4 0.7 copy.74
  416.1 1.9 copy.75
  418.0 1.6 copy.76
  419.5 0.8 copy.77
  420.3 0.7 copy.78
  421.0 0.8 copy.79
  (85 shorter events, 7.8 us)
Async XLA Ops:
  7.2 362.9 %all-gather.2.cloned.1.call-start = ((), (), s32[]{:S(2)}) async-start(), calls=%async_computation | async-start | bytes 1572864 | tf_op jit(solution)/shard_map/all_gather | solution.py:1095
  149.1 5.3 %copy-start.11 = (bf16[4,2,4,64,1024]{4,3,2,1,0:T(8,128)(2,1)S(1)}, bf16[4,2,4,64,1024]{4,3,2,1,0:T(8,128)(2,1)}, u32[]{:S(2)}) copy-start(bf16[4,2,4,64,1024]{4,3,2,1,0:T(8,128)(2,1)} %get-tuple-element.62) | copy-start | bytes 12582916
  149.1 5.3 %copy-start.16 = (f32[8,128]{1,0:T(8,128)S(1)}, f32[8,128]{1,0:T(8,128)}, u32[]{:S(2)}) copy-start(f32[8,128]{1,0:T(8,128)} %get-tuple-element.61) | copy-start | bytes 12292
  154.4 3.9 copy-start.13
  161.9 4.8 %copy-start.10 = (bf16[4,2,4,64,1024]{4,3,2,1,0:T(8,128)(2,1)S(1)}, bf16[4,2,4,64,1024]{4,3,2,1,0:T(8,128)(2,1)}, u32[]{:S(2)}) copy-start(bf16[4,2,4,64,1024]{4,3,2,1,0:T(8,128)(2,1)} %get-tuple-element.60) | copy-start | bytes 12582916
  166.7 3.7 copy-start.12
  170.4 5.8 %copy-start.9 = (bf16[4,4]{1,0:T(4,128)(2,1)S(1)}, bf16[4,4]{1,0:T(4,128)(2,1)}, u32[]{:S(2)}) copy-start(bf16[4,4]{1,0:T(4,128)(2,1)} %param.30) | copy-start | bytes 100
  170.4 6.4 %copy-start.2 = (bf16[4,2,4,80,256]{4,3,2,1,0:T(8,128)(2,1)S(1)}, bf16[4,2,4,80,256]{4,3,2,1,0:T(8,128)(2,1)}, u32[]{:S(2)}) copy-start(bf16[4,2,4,80,256]{4,3,2,1,0:T(8,128)(2,1)} %get-tuple-element.74) | copy-start | bytes 3932164
  176.9 39.5 %copy-start.15 = (bf16[4,2,4,64,256]{4,3,2,1,0:T(8,128)(2,1)S(1)}, bf16[4,2,4,64,256]{4,3,2,1,0:T(8,128)(2,1)}, u32[]{:S(2)}) copy-start(bf16[4,2,4,64,256]{4,3,2,1,0:T(8,128)(2,1)} %get-tuple-element.71) | copy-start | bytes 3145732
  216.5 3.2 copy-start.5
  216.5 3.2 copy-start.14
  322.0 40.0 %copy-start.1 = (bf16[2,256,256]{2,1,0:T(8,128)(2,1)S(1)}, bf16[2,256,256]{2,1,0:T(8,128)(2,1)}, u32[]{:S(2)}) copy-start(bf16[2,256,256]{2,1,0:T(8,128)(2,1)} %get-tuple-element.73) | copy-start | bytes 786436
  362.2 3.4 copy-start.6
  364.7 3.6 copy-start
  372.5 42.9 %copy-start.7 = (bf16[64,2048]{1,0:T(8,128)(2,1)S(1)}, bf16[64,2048]{1,0:T(8,128)(2,1)}, u32[]{:S(2)}) copy-start(bf16[64,2048]{1,0:T(8,128)(2,1)} %get-tuple-element.127) | copy-start | bytes 786436
  409.0 10.5 %copy-start.4 = (f32[64,2048]{1,0:T(8,128)S(1)}, f32[64,2048]{1,0:T(8,128)}, u32[]{:S(2)}) copy-start(f32[64,2048]{1,0:T(8,128)} %get-tuple-element.130) | copy-start | bytes 1572868
  409.0 11.3 %copy-start.8 = (f32[64,512]{1,0:T(8,128)S(1)}, f32[64,512]{1,0:T(8,128)}, u32[]{:S(2)}) copy-start(f32[64,512]{1,0:T(8,128)} %get-tuple-element.131) | copy-start | bytes 393220
  409.1 11.9 %copy-start.3 = (f32[64,2048]{1,0:T(8,128)S(1)}, f32[64,2048]{1,0:T(8,128)}, u32[]{:S(2)}) copy-start(f32[64,2048]{1,0:T(8,128)} %get-tuple-element.132) | copy-start | bytes 1572868
Sparse Core Ops, SparseCore 0:
  146.4 11.1 all-gather.1

commit v3 on v2

--- a/solution.py
+++ b/solution.py
@@ -116,43 +116,57 @@
     net.got(out.at[yo, 1 - c, hi], k[8])
 
 
-def group_scatter(net, part, from_core, held, from_half, from_full, total, make=None):
+def group_scatter(net, part, acc, from_half, from_full, total, make=None):
     y, c, yu, yd, yo = net.y, net.c, net.yu, net.yd, net.yo
     k = [net.slot() for _ in range(8)]
     n = part.shape[2]
     half = n // 2
     lo, hi = pl.ds(0, half), pl.ds(half, half)
-    for i, d in enumerate((yo, yu, yd, y)):
+
+    sent = []
+
+    def send(src, dst, i, name):
+        sent.append(net.copy(src, dst, i, name))
+        sent[-1].start()
+
+    def start(i, d):
         if make is not None:
             make(i, d)
-        net.send(part.at[d, 1 - c], from_core.at[d], k[i], "c")
+        send(part.at[d, 1 - c], acc.at[d], k[i], "c")
 
     def core_sum(i, d):
-        net.got(from_core.at[d], k[i])
-        held[d] = (part[d, c].astype(F32) + from_core[d].astype(F32)).astype(BF16)
-
+        net.got(acc.at[d], k[i])
+        acc[d] = acc[d] + part[d, c]
+
+    for i, d in enumerate((yo, yu, yd)):
+        start(i, d)
     yield
     core_sum(0, yo)
-    net.send(held.at[yo, lo], from_half.at[0], k[4], "yu")
-    net.send(held.at[yo, hi], from_half.at[1], k[5], "yd")
+    send(acc.at[yo, lo], from_half.at[0], k[4], "yu")
+    send(acc.at[yo, hi], from_half.at[1], k[5], "yd")
     core_sum(1, yu)
     core_sum(2, yd)
     yield
     net.got(from_half.at[0], k[4])
-    held[yu, lo] = (held[yu, lo].astype(F32) + from_half[0].astype(F32)).astype(BF16)
-    net.send(held.at[yu], from_full.at[0], k[6], "yu")
+    acc[yu, lo] = acc[yu, lo] + from_half[0]
+    send(acc.at[yu], from_full.at[0], k[6], "yu")
     net.got(from_half.at[1], k[5])
-    held[yd, hi] = (held[yd, hi].astype(F32) + from_half[1].astype(F32)).astype(BF16)
-    net.send(held.at[yd], from_full.at[1], k[7], "yd")
-    core_sum(3, y)
-    yield
+    acc[yd, hi] = acc[yd, hi] + from_half[1]
+    send(acc.at[yd], from_full.at[1], k[7], "yd")
+    yield
+    start(3, y)
+    yield
+    net.got(acc.at[y], k[3])
+    mine = part[y, c].astype(F32) + acc[y].astype(F32)
     net.got(from_full.at[0], k[6])
     net.got(from_full.at[1], k[7])
-    total(held[y].astype(F32) + from_full[0].astype(F32) + from_full[1].astype(F32))
+    for one in sent:
+        one.wait_send()
+    total(mine + from_full[0].astype(F32) + from_full[1].astype(F32))
 
 
 def scatter_scratch(n, w):
-    return [VMEM((4, n, w), BF16), VMEM((4, n, w), BF16), VMEM((2, n // 2, w), BF16), VMEM((2, n, w), BF16)]
+    return [VMEM((4, n, w), BF16), VMEM((2, n // 2, w), BF16), VMEM((2, n, w), BF16)]
 
 
 BOTH = slice(None)
@@ -210,10 +224,10 @@
 def add_into(dst, *others):
     for index in itertools.product(*[range(n) for n in dst.shape[:-2]]):
         at = index + (slice(None), slice(None))
-        total = dst[at].astype(F32)
+        total = dst[at]
         for other in others:
-            total = total + other[at].astype(F32)
-        dst[at] = total.astype(dst.dtype)
+            total = total + other[at]
+        dst[at] = total
 
 
 def plane_scatter(net, g, tmp):
@@ -658,69 +672,6 @@
     )(tokens, cotangent, pack, biases, parents, w_query, w_out, w_up, w_down)
 
 
-def block_place(segs, parents, block):
-    seg = segs[block]
-    parent = parents[seg]
-    trunk = parents[parent]
-    parent_block = jnp.int32(16)
-    for b in range(16, 32):
-        parent_block = jnp.where(segs[b] == parent, b, parent_block)
-    return trunk, parent_block, seg >= 10, seg >= 2
-
-
-def attend_back(q, kv, o, go, log_sum, segs, parents):
-    def kernel(segs, parents, q, kv, o, go, log_sum, dq, dkv):
-        z, x = lax.axis_index("z"), lax.axis_index("x")
-        lane = lax.broadcasted_iota(jnp.int32, (256, 512), 1) & 255
-        row = lax.broadcasted_iota(jnp.int32, (256, 512), 0)
-        for b in range(2):
-            block = z * 8 + b * 4 + x
-            trunk, parent_block, leaf, branch = block_place(segs, parents, block)
-
-            def stacked(ref):
-                return jnp.concatenate([ref[b, :, :128], ref[b, :, 128:]], axis=0)
-
-            both, grad = stacked(q), stacked(go)
-            logs = log_sum[b, 0:1]
-            inner = jnp.sum((grad.astype(F32) * stacked(o).astype(F32)).T, axis=0, keepdims=True)
-
-            def one(i, key_block, mask, acc):
-                key, value = kv[key_block, :, :128], kv[key_block, :, 128:]
-                nt = (((1,), (1,)), ((), ()))
-                s = lax.dot_general(key, both, nt, preferred_element_type=F32) * 128**-0.5
-                p = jnp.where(mask, jnp.exp(jnp.minimum(s - logs, 1.0)), 0.0)
-                dp = lax.dot_general(value, grad, nt, preferred_element_type=F32)
-                ds = (p * (dp - inner)).astype(BF16)
-                dk = jnp.dot(ds, both, preferred_element_type=F32) * 128**-0.5
-                dv = jnp.dot(p.astype(BF16), grad, preferred_element_type=F32)
-                dkv[b, i, :, :128] = dk.astype(BF16)
-                dkv[b, i, :, 128:] = dv.astype(BF16)
-                return acc + lax.dot_general(key, ds, (((0,), (0,)), ((), ())), preferred_element_type=F32)
-
-            def trunk_one(i, acc):
-                gap = (block - trunk * 8 - i) * 256
-                return one(i, trunk * 8 + i, row - lane <= gap, acc)
-
-            acc = lax.fori_loop(0, 8, trunk_one, jnp.zeros((128, 512), F32))
-            acc = one(8, parent_block, jnp.broadcast_to(leaf, (256, 512)), acc)
-            acc = one(9, block, (row <= lane) & branch, acc)
-            grad_q = (acc * 128**-0.5).T.astype(BF16)
-            dq[b, :, :128] = grad_q[:256]
-            dq[b, :, 128:] = grad_q[256:]
-
-    return pl.pallas_call(
-        kernel,
-        out_shape=(
-            jax.ShapeDtypeStruct((2, 256, 256), BF16),
-            jax.ShapeDtypeStruct((2, 10, 256, 256), BF16),
-        ),
-        in_specs=[INS, INS, INV, INV, INV, INV, INV],
-        out_specs=(INV, INV),
-        compiler_params=pltpu.CompilerParams(vmem_limit_bytes=56 << 20),
-        name="attend_back",
-    )(segs, parents, q, kv, o, go, log_sum)
-
-
 def normed(values):
     centred = values - jnp.mean(values, axis=-1, keepdims=True)
     inverse = lax.rsqrt(jnp.mean(centred * centred, axis=-1, keepdims=True) + EPS)
@@ -758,208 +709,438 @@
     best[1 - net.yh] = got[6]
 
 
-def turn(mlp, back, x1, cotangent, gain, down_bias):
-    def kernel(mlp, back, x1, cot, gain, bias, output, dx1, dz, sums, own, local, *rest):
-        first, second, (ss, rs) = rest[:4], rest[4:8], rest[8:]
-        net = Net(ss, rs)
-        net.barrier(RING)
-
-        def gradient():
-            def total(summed):
-                norm, inverse = normed(x1[...])
-                grad = cot[...].astype(F32) + norm_back(summed, norm, inverse, gain[...])
-                dx1[...] = grad
-                rounded = grad.astype(BF16)
-                own[...] = rounded
-                parts = [
-                    jnp.sum(v, axis=0, keepdims=True)
-                    for v in (summed * norm, summed, rounded.astype(F32), cot[...].astype(F32))
-                ]
-                zero = jnp.zeros((2, parts[0].shape[1]), F32)
-                sums[...] = jnp.concatenate([zero] + parts + [zero], axis=0)
-
-            yield from group_scatter(net, back, *first, total)
-            me = pltpu.make_async_copy(own, dz.at[net.y, net.c], local)
-            me.start()
-            yield from group_gather(net, own, dz)
-            me.wait()
-
-        def forward():
-            def total(summed):
-                output[...] = (x1[...] + (summed + bias[...])).astype(BF16)
-
-            yield
-            yield from group_scatter(net, mlp, *second, total)
-
-        run_all(gradient(), forward())
-        net.finish()
-
-    n, d = cotangent.shape
-    return pl.pallas_call(
-        kernel,
-        out_shape=(
-            jax.ShapeDtypeStruct((n, d), BF16),
-            jax.ShapeDtypeStruct((n, d), F32),
-            jax.ShapeDtypeStruct((4, 2, n, d), BF16),
-            jax.ShapeDtypeStruct((8, d), F32),
-        ),
-        in_specs=[INV] * 6,
-        out_specs=(INV, INV, ANY, INV),
-        scratch_shapes=[VMEM((n, d), BF16), pltpu.SemaphoreType.DMA]
-        + scatter_scratch(n, d)
-        + scatter_scratch(n, d)
-        + sems(9 + 8 + 8),
-        compiler_params=params(5),
-        name="turn",
-    )(mlp, back, x1, cotangent, gain, down_bias)
-
-
-def weight_scatter(net, g, tmp, swap, out):
+def weight_scatter(net, g, tmp, out):
     z, yh, x = net.z, net.yh, net.x
     w = g.shape[-1]
     k = net.slot()
     yield from plane_scatter(net, column_view(g), tmp)
-    net.send(g.at[z, 1 - yh, x], swap, k, "yo")
-    out[:, pl.ds(pl.multiple_of(yh * w, 128), w)] = g[z, yh, x].astype(F32)
-    yield
-    net.got(swap, k)
-    out[:, pl.ds(pl.multiple_of((1 - yh) * w, 128), w)] = swap[...].astype(F32)
-
-
-def scatter_weights(grads, cid):
-    count = len(grads)
-
-    def kernel(*refs):
-        g, outs = refs[:count], refs[count : 2 * count]
-        scratch, (ss, rs) = refs[2 * count : -2], refs[-2:]
+    mine = out.at[:, pl.ds(pl.multiple_of(yh * w, 128), w)]
+    net.send(g.at[z, 1 - yh, x], mine, k, "yo")
+    out[:, pl.ds(pl.multiple_of(yh * w, 128), w)] = g[z, yh, x]
+    yield
+    net.got(out.at[:, pl.ds(pl.multiple_of((1 - yh) * w, 128), w)], k)
+
+
+def smooth_gate(u):
+    scale = 0.7978845608028654
+    square = u * u
+    t = jnp.tanh(scale * u * (1.0 + 0.044715 * square))
+    half = 0.5 * (1.0 + t)
+    slope = half + 0.5 * u * (1.0 - t * t) * scale * (1.0 + 0.134145 * square)
+    return u * half, slope
+
+
+def piece(ref, which, zz, yy, xx):
+    return jnp.concatenate(
+        [ref[zz, yy, xx, :, (which * 4 + r) * 128 : (which * 4 + r + 1) * 128] for r in range(4)], axis=0
+    )
+
+
+def put_piece(ref, which, zz, yy, xx, value):
+    for r in range(4):
+        ref[zz, yy, xx, :, (which * 4 + r) * 128 : (which * 4 + r + 1) * 128] = value[r * 64 : (r + 1) * 64]
+
+
+def attend_back(z, x, q, kv, o, go, log_sum, segs, parents, grad, lone, dq_sum, dq):
+    lane = (lax.broadcasted_iota(jnp.int32, (256, 512), 1) & 255).astype(F32)
+    row = lax.broadcasted_iota(jnp.int32, (256, 512), 0).astype(F32)
+    places = [place_of(segs, parents, z * 8 + b * 4 + x) for b in range(2)]
+
+    def stacked(ref, b):
+        return jnp.concatenate([ref[b * 256 : b * 256 + 256, :128], ref[b * 256 : b * 256 + 256, 128:]], axis=0)
+
+    logs, inner = [], []
+    for b in range(2):
+        logs.append(log_sum[b, 0:1])
+        inner.append(
+            jnp.sum((stacked(go, b).astype(F32) * stacked(o, b).astype(F32)).T, axis=0, keepdims=True)
+        )
+
+    def one(b, key, value, masked, first):
+        both, up = stacked(q, b), stacked(go, b)
+        s = masked(lax.dot_general(key, both, NT, preferred_element_type=F32) * SCALE)
+        p = jnp.exp(s - logs[b])
+        dp = lax.dot_general(value, up, NT, preferred_element_type=F32)
+        ds = (p * (dp - inner[b])).astype(BF16)
+        more = lax.dot_general(key, ds, TN, preferred_element_type=F32)
+        dq_sum[b] = more if first else dq_sum[b] + more
+        dk = jnp.dot(ds, both, preferred_element_type=F32) * SCALE
+        dv = jnp.dot(p.astype(BF16), up, preferred_element_type=F32)
+        return dk.astype(BF16), dv.astype(BF16)
+
+    for b in range(2):
+        trunk, leaf, branch, above = places[b]
+        lone[b, 0, 0], lone[b, 0, 1] = one(
+            b,
+            piece(kv, 0, z, b, x),
+            piece(kv, 1, z, b, x),
+            lambda s: jnp.where(row <= lane, s, NEG) + (branch - 1.0) * 1e30,
+            True,
+        )
+        key, value = (
+            sum(piece(kv, w, 2 + j // 8, j // 4 % 2, j % 4) * wide(above[j]) for j in range(16)) for w in range(2)
+        )
+        lone[b, 1, 0], lone[b, 1, 1] = one(b, key, value, lambda s: s + (leaf - 1.0) * 1e30, False)
+    yield
+
+    for j in range(16):
+        own = [
+            wide((z * 8 + b * 4 + x == 16 + j).astype(F32) * jnp.ones((1, 1), F32)) for b in range(2)
+        ]
+        for w in range(2):
+            value = sum(lone[b, 0, w] * own[b] + lone[b, 1, w] * wide(places[b][3][j]) for b in range(2))
+            put_piece(grad, w, 2 + j // 8, j // 4 % 2, j % 4, value)
+
+    def trunk_one(i, carry):
+        yy, xx = i // 4, i % 4
+        totals = None
+        for b in range(2):
+            trunk = places[b][0]
+            second = wide(trunk)
+            first = 1 - second
+            key, value = (piece(kv, w, 0, yy, xx) * first + piece(kv, w, 1, yy, xx) * second for w in range(2))
+            start = (z * 8 + b * 4 + x).astype(F32) - 8.0 * trunk
+            gap = (start - i.astype(F32)) * 256.0
+            dk, dv = one(b, key, value, lambda s: jnp.where(row - lane <= gap, s, NEG), False)
+            parts = [dk * first, dv * first, dk * second, dv * second]
+            totals = parts if totals is None else [t + p for t, p in zip(totals, parts)]
+        for t in range(2):
+            for w in range(2):
+                put_piece(grad, w, t, yy, xx, totals[2 * t + w])
+        return carry
+
+    lax.fori_loop(0, 4, trunk_one, 0)
+    yield
+    lax.fori_loop(4, 8, trunk_one, 0)
+    for b in range(2):
+        rows = (dq_sum[b] * SCALE).T.astype(BF16)
+        dq[b * 256 : b * 256 + 256, :128] = rows[:256]
+        dq[b * 256 : b * 256 + 256, 128:] = rows[256:]
+
+
+def spread(net, names, src, dst, k):
+    for i, name in enumerate(names):
+        net.send(src, dst.at[i], k[i], name)
+
+
+def all_sums(net, mine, near, far):
+    k = [net.slot() for _ in range(6)]
+    spread(net, ("xu", "xd", "xo"), mine.at[0], near, k)
+    yield
+    for i in range(3):
+        net.got(near.at[i], k[i])
+    mine[1] = mine[0] + near[0] + near[1] + near[2]
+    spread(net, ("zu", "zd", "zo"), mine.at[1], far, k[3:])
+    yield
+    for i in range(3):
+        net.got(far.at[i], k[3 + i])
+    mine[2] = mine[1] + far[0] + far[1] + far[2]
+
+
+def backward(tokens, cotangent, parents, cot_all, h2, wu, wd, wq, wo, packs, h1, q, kv, o, log_sum, x1, vec, ub):
+    def kernel(tok, cot, parents, cot_in, h2_in, wu_in, wd_in, wq_in, wo_in, packs_in, h1_in, q, kv_in, o, log_sum,
+               x1, vec, ub_in,
+               output, grad_input, up_out, down_out, wo_out, wq_out, vec_out, bias_out, kv_out, vb_out,
+               h2, cots, wu, wd, wq, wo, packs, adu, us, das, part, part_mlp, gu, gd, gwo, gq, own, dz, dx1, sums, go,
+               lone, dq_sum, dq, dkv_from, dkv, gkv, gkv_z, gkv_x, bias, bias_x, bias_z, vecs, vec_z, vec_x,
+               local, *rest):
+        *scratch, ss, rs = rest
+        first, second, tmp_u, tmp_d, tmp_o, tmp_q, tmp_k = (
+            scratch[:3],
+            scratch[3:6],
+            scratch[6:14],
+            scratch[14:22],
+            scratch[22:30],
+            scratch[30:38],
+            scratch[38:46],
+        )
         net = Net(ss, rs)
-        net.barrier(PLANE + ("yo",))
-        run_all(
-            *[
-                weight_scatter(net, g[i], scratch[9 * i : 9 * i + 8], scratch[9 * i + 8], outs[i])
-                for i in range(count)
-            ]
-        )
-        net.finish()
-
-    scratch = []
-    for one in grads:
-        n, w = one.shape[-2:]
-        scratch += plane_scratch(n, w // 2) + [VMEM((n, w), BF16)]
-    return pl.pallas_call(
-        kernel,
-        out_shape=tuple(jax.ShapeDtypeStruct((g.shape[-2], 2 * g.shape[-1]), F32) for g in grads),
-        in_specs=[INV] * count,
-        out_specs=(INV,) * count,
-        scratch_shapes=scratch + sems(17 * count),
-        compiler_params=params(cid),
-        name="scatter_weights",
-    )(*grads)
-
-
-def scatter_kv(slots, segs, parents):
-    def kernel(segs, parents, slots, out, full, from_core, held, ring, *rest):
-        tmp, (ss, rs) = rest[:8], rest[8:]
-        net = Net(ss, rs)
-        z, x, c, y = net.z, net.x, net.c, net.y
-        net.barrier(PLANE + RING + ("yo",))
-        for b in range(2):
-            block = z * 8 + b * 4 + x
-            trunk, parent_block, leaf, branch = block_place(segs, parents, block)
-
-            def place(kb, carry):
-                slot = jnp.where(kb < 16, kb & 7, jnp.where(kb == block, 9, 8))
-                valid = jnp.where(
-                    kb < 16,
-                    (kb >> 3) == trunk,
-                    ((kb == block) & branch) | ((kb == parent_block) & leaf),
+        z, yh, x, yl, c, y = net.z, net.yh, net.x, net.yl, net.c, net.y
+
+        def columns(ref, j):
+            return ref.at[:, :, :, :, pl.ds(j * 256, 256)]
+
+        def load(src, dst, i):
+            one = pltpu.make_async_copy(src, dst, local.at[i])
+            one.start()
+            return one
+
+        load(h2_in, h2, 0)
+        load(columns(wu_in, 0), columns(wu, 0), 2)
+        load(cot_in, cots, 1)
+        load(columns(wd_in, 0), columns(wd, 0), 6)
+        for j in range(1, 4):
+            load(columns(wu_in, j), columns(wu, j), 2 + j)
+            load(columns(wd_in, j), columns(wd, j), 6 + j)
+        loads = [load(wo_in, wo, 10), load(wq_in.at[:, :, :, pl.ds(0, 64)], wq, 11)]
+        loads.append(load(packs_in.at[:, :, :, :, :, pl.ds(0, 16)], packs, 12))
+        net.barrier(PLANE + RING + ("yo", "xo", "zo"))
+        pltpu.make_async_copy(h2_in, h2, local.at[0]).wait()
+        pltpu.make_async_copy(cot_in, cots, local.at[1]).wait()
+
+        def hidden(j, carry):
+            at = pl.ds(pl.multiple_of(j * 256, 256), 256)
+            there = pl.ds(0, 4), pl.ds(0, 2), pl.ds(0, 4), pl.ds(0, 64), at
+            pltpu.make_async_copy(wu_in.at[there], wu.at[there], local.at[2 + j]).wait()
+            us[...] = jnp.dot(
+                h2[...].reshape(512, 2048), wu[there].reshape(2048, 256), preferred_element_type=F32
+            )
+            pltpu.make_async_copy(wd_in.at[there], wd.at[there], local.at[6 + j]).wait()
+            das[...] = jnp.dot(
+                cots[...].reshape(512, 2048), wd[there].reshape(2048, 256), preferred_element_type=F32
+            )
+            bias_row = jnp.concatenate([ub_in[pl.ds(2 * j, 1)], ub_in[pl.ds(2 * j + 1, 1)]], axis=1)
+
+            def gate(i, total):
+                rows = pl.ds(pl.multiple_of(i * 64, 64), 64)
+                value, slope = smooth_gate(us[rows] + bias_row)
+                adu[0, rows, at] = value.astype(BF16)
+                du = (das[rows] * slope).astype(BF16)
+                adu[1, rows, at] = du
+                return total + jnp.sum(du.astype(F32), axis=0, keepdims=True)
+
+            total = lax.fori_loop(0, 8, gate, jnp.zeros((1, 256), F32))
+            bias[0, pl.ds(2 * j, 1)] = total[:, :128]
+            bias[0, pl.ds(2 * j + 1, 1)] = total[:, 128:]
+            return carry
+
+        lax.fori_loop(0, 4, hidden, 0)
+
+        def projected(dst, d, rows, weight):
+            def column(j, carry):
+                out = lax.dot_general(rows, weight(j), NT, preferred_element_type=F32).astype(BF16)
+                at = pl.ds(pl.multiple_of(j * 512, 512), 512)
+                dst[d, 0, :, at] = out[:64]
+                dst[d, 1, :, at] = out[64:]
+                return carry
+
+            lax.fori_loop(0, 4, column, 0)
+
+        def ring_rows(d):
+            return pl.ds(pl.multiple_of(d * 128, 128), 128)
+
+        def make_two(i, d):
+            projected(part, d, adu[1, ring_rows(d)], lambda j: wu[j].reshape(512, 1024))
+
+        def total_two(summed):
+            norm, inverse = normed(x1[...])
+            grad = cot[...].astype(F32) + norm_back(summed, norm, inverse, vec[2:3])
+            dx1[...] = grad
+            rounded = grad.astype(BF16)
+            own[...] = rounded
+            values = (summed * norm, summed, rounded.astype(F32), cot[...].astype(F32))
+            for i, v in enumerate(values):
+                sums[2 + i : 3 + i] = jnp.sum(v, axis=0, keepdims=True)
+
+        def outer(dst, left, right):
+            def block(j, carry):
+                out = lax.dot_general(left(j), right, TN, preferred_element_type=F32)
+                dst[j] = out.astype(BF16).reshape(2, 4, 64, right.shape[1])
+                return carry
+
+            lax.fori_loop(0, 4, block, 0)
+
+        def wide_outer(dst, left, which):
+            def block(i, carry):
+                j, w = i // 2, i % 2
+                at = pl.ds(pl.multiple_of(w * 512, 512), 512)
+                out = lax.dot_general(
+                    left[:, :, :, pl.ds(pl.multiple_of(j * 512, 512), 512)].reshape(512, 512),
+                    adu[which, :, at],
+                    TN,
+                    preferred_element_type=F32,
                 )
-                value = jnp.where(valid, slots[b, slot], jnp.zeros((256, 256), BF16))
-                at = (kb >> 3, (kb >> 2) & 1, kb & 3)
-                if b == 0:
-                    full[at] = value
-                else:
-                    full[at] = full[at] + value
+                dst[j, :, :, :, at] = out.astype(BF16).reshape(2, 4, 64, 512)
                 return carry
 
-            lax.fori_loop(0, 32, place, 0)
-        k = [net.slot() for _ in range(8)]
-        net.send(full.at[:, 1 - c], from_core, k[0], "c")
-        net.got(from_core, k[0])
-        for zz in range(4):
-            for xx in range(4):
-                held[zz, xx] = (full[zz, c, xx].astype(F32) + from_core[zz, xx].astype(F32)).astype(BF16)
+            lax.fori_loop(0, 8, block, 0)
+
+        rows_two = group_scatter(net, part, *first, total_two, make_two)
+        next(rows_two)
+        wide_outer(gd, cots, 0)
+        down = weight_scatter(net, gd, tmp_d, down_out)
+        next(down)
+        next(rows_two)
+        wide_outer(gu, h2, 1)
+        up = weight_scatter(net, gu, tmp_u, up_out)
+        next(up)
+        next(rows_two)
+        for d in range(4):
+            projected(part_mlp, d, adu[0, d * 128 : d * 128 + 128], lambda j: wd[j].reshape(512, 1024))
+        keep = [
+            load(kv_in.at[w, :, :, :, pl.ds(r * 64, 64)], wd.at[:, :, :, :, pl.ds((w * 4 + r) * 128, 128)], 13 + 4 * w + r)
+            for w in range(2)
+            for r in range(4)
+        ]
+        next(rows_two)
+        next(rows_two, None)
+        me = load(own, dz.at[y, c], 23)
+        spreading = group_gather(net, own, dz)
+        next(spreading)
+        late = [load(h1_in.at[:, pl.ds(w * 1024, 1024)], adu.at[w], 21 + w) for w in range(2)]
+        next(spreading)
+        next(down)
+        next(spreading)
+        next(up)
+        for _ in spreading:
+            pass
+        me.wait()
+        loads[0].wait()
+        go[...] = jnp.dot(
+            dz[...].reshape(512, 2048), wo[...].reshape(2048, 256), preferred_element_type=F32
+        ).astype(BF16)
+
+        def total_out(summed):
+            output[...] = (x1[...] + (summed + vec[5:6])).astype(BF16)
+
+        rows_out = group_scatter(net, part_mlp, *second, total_out)
+        next(rows_out)
+        for one in keep:
+            one.wait()
+        steps = attend_back(z, x, q, wd, o, go, log_sum, vec[8:9, 0:128], parents[0:1], wu, lone, dq_sum, dq)
+        next(steps)
+        next(rows_out)
+        next(steps)
+        next(rows_out)
+        next(down)
+        next(up)
+        next(steps, None)
+        next(rows_out)
+        next(rows_out, None)
+
+        kc = [net.slot() for _ in range(4)]
+        theirs = pl.ds(pl.multiple_of((1 - c) * 512, 512), 512)
+        for i in range(4):
+            net.send(wu.at[:, :, i, :, theirs], cots.at[:, :, :, pl.ds(i * 512, 512)], kc[i], "c")
+        for one in loads[1:] + late:
+            one.wait()
+
+        def make_one(i, d):
+            if i == 3:
+                lower = lax.dot_general(
+                    dkv[y], packs[...].reshape(2048, 128), NT, preferred_element_type=F32
+                )
+                upper = lax.dot_general(
+                    dq[ring_rows(d)], wq[...].reshape(2048, 256), NT, preferred_element_type=F32
+                )
+                out = (lower + upper).astype(BF16)
+                h2[d, 0] = out[:64]
+                h2[d, 1] = out[64:]
+            else:
+                projected(h2, d, dq[ring_rows(d)], lambda j: wq[j].reshape(512, 256))
+
+        def total_one(summed):
+            norm, inverse = normed(tok[...].astype(F32))
+            grad_input[...] = dx1[...] + norm_back(summed, norm, inverse, vec[0:1])
+            sums[0:1] = jnp.sum(summed * norm, axis=0, keepdims=True)
+            sums[1:2] = jnp.sum(summed, axis=0, keepdims=True)
+            sums[6:8] = jnp.zeros((2, 2048), F32)
+            vecs[y, c] = sums[...]
+
+        rows_one = group_scatter(net, h2, *first, total_one, make_one)
+        next(rows_one)
+        ours = pl.ds(pl.multiple_of(c * 512, 512), 512)
+        for i in range(4):
+            net.got(cots.at[:, :, :, pl.ds(i * 512, 512)], kc[i])
+
+            def core_sum(j, carry):
+                zz, yy = j // 2, j % 2
+                wu[zz, yy, i, :, ours] = wu[zz, yy, i, :, ours] + cots[zz, yy, :, i * 512 : i * 512 + 512]
+                return carry
+
+            lax.fori_loop(0, 8, core_sum, 0)
 
         def view(zz, half, xx, part):
-            rows = pl.ds(0, 256) if half == BOTH else pl.ds(128 * half, 128)
-            return held.at[zz, xx, rows, pl.ds(part * 128, 128)]
-
-        run_all(plane_scatter(net, view, tmp))
-        mine = held.at[z, x]
-
-        def rows(yy):
-            return pl.ds(pl.multiple_of(yy * 64, 64), 64)
-
+            at = ours if half == BOTH else pl.ds(pl.multiple_of(c * 512 + 256 * half, 256), 256)
+            return wu.at[zz, part, xx, :, at]
+
+        keys = plane_scatter(net, view, tmp_k)
+        next(keys)
+        next(rows_one)
+        outer(gq, lambda j: adu[j // 2, :, pl.ds(pl.multiple_of((j % 2) * 512, 512), 512)], dq[...])
+        bias[0, 8:9] = jnp.sum(dq[:, :128].astype(F32), axis=0, keepdims=True)
+        bias[0, 9:10] = jnp.sum(dq[:, 128:].astype(F32), axis=0, keepdims=True)
+        bias[0, 10:16] = jnp.zeros((6, 128), F32)
+        next(keys)
+        query = weight_scatter(net, gq, tmp_q, wq_out)
+        next(query)
+        small = all_sums(net, bias, bias_x, bias_z)
+        next(small)
+        next(rows_one)
+        outer(gwo, lambda j: dz[:, :, :, pl.ds(pl.multiple_of(j * 512, 512), 512)].reshape(512, 512), o[...])
+        next(keys)
+        project = weight_scatter(net, gwo, tmp_o, wo_out)
+        next(project)
+        next(down)
+        next(up)
+        next(query)
+        next(small)
+        next(keys)
+        next(project)
+        for _ in keys:
+            pass
+
+        def ring_piece(ref, d):
+            at = pl.ds(pl.multiple_of(c * 512 + lax.rem(d, 2) * 256, 256), 256)
+            return ref.at[z, d // 2, x, :, at]
+
+        kr = [net.slot() for _ in range(7)]
         for i, (name, d) in enumerate((("yu", net.yu), ("yd", net.yd), ("yo", net.yo))):
-            net.send(mine.at[rows(d)], ring.at[i], k[1 + i], name)
+            net.send(ring_piece(wu, d), dkv_from.at[i], kr[i], name)
+        next(query)
+        next(project)
         for i in range(3):
-            net.got(ring.at[i], k[1 + i])
-        own = held[z, x, rows(y)].astype(F32)
+            net.got(dkv_from.at[i], kr[i])
+        mine = ring_piece(wu, y)[...].astype(F32)
         for i in range(3):
-            own = own + ring[i].astype(F32)
-        out[c, rows(y)] = own.astype(BF16)
-        view = out.at[c, rows(y)]
+            mine = mine + dkv_from[i].astype(F32)
+        mine = mine.astype(BF16)
+        dkv[y] = jnp.concatenate([mine[:, :128], mine[:, 128:]], axis=0)
         for i, name in enumerate(("yu", "yd", "yo")):
-            net.send(view, view, k[4 + i], name)
+            net.send(dkv.at[y], dkv.at[y], kr[3 + i], name)
+        next(rows_one)
+        next(down)
+        next(up)
+        next(small, None)
         for i, d in enumerate((net.yd, net.yu, net.yo)):
-            net.got(out.at[c, rows(d)], k[4 + i])
-        net.send(out.at[c], out.at[c], k[7], "c")
-        net.got(out.at[1 - c], k[7])
-        net.finish()
-
-    return pl.pallas_call(
-        kernel,
-        out_shape=jax.ShapeDtypeStruct((2, 256, 256), BF16),
-        in_specs=[INS, INS, INV],
-        out_specs=INV,
-        scratch_shapes=[
-            VMEM((4, 2, 4, 256, 256), BF16),
-            VMEM((4, 4, 256, 256), BF16),
-            VMEM((4, 4, 256, 256), BF16),
-            VMEM((3, 64, 256), BF16),
-            VMEM((2, 4, 128, 128), BF16),
-            VMEM((2, 4, 128, 128), BF16),
-            VMEM((2, 4, 256, 128), BF16),
-            VMEM((2, 4, 256, 128), BF16),
-            VMEM((2, 128, 128), BF16),
-            VMEM((2, 128, 128), BF16),
-            VMEM((2, 256, 128), BF16),
-            VMEM((2, 256, 128), BF16),
-        ]
-        + sems(16 + 8),
-        compiler_params=params(6),
-        name="scatter_kv",
-    )(segs, parents, slots)
-
-
-def closing(back, tokens, dx1, from_kv, gain, sums, grad_q, small):
-    def kernel(back, tokens, dx1, from_kv, gain, sums, gq, small, grad_input, out_q, vec, small_out,
-               vecs, vec_z, vec_x, lone, small_z, small_x, small_y, swap, *rest):
-        first, tmp, (ss, rs) = rest[:4], rest[4:12], rest[12:]
-        net = Net(ss, rs)
-        z, yh, x, y, c = net.z, net.yh, net.x, net.y, net.c
-        net.barrier(PLANE + RING + ("yo", "xo", "zo"))
-
-        def rows():
-            def total(summed):
-                grad = summed + from_kv[...]
-                norm, inverse = normed(tokens[...].astype(F32))
-                grad_input[...] = dx1[...] + norm_back(grad, norm, inverse, gain[...])
-                one = jnp.sum(grad * norm, axis=0, keepdims=True)
-                two = jnp.sum(grad, axis=0, keepdims=True)
-                vecs[y, c] = jnp.concatenate([one, two, sums[2:8]], axis=0)
-
-            yield from group_scatter(net, back, *first, total)
+            net.got(dkv.at[d], kr[3 + i])
+
+        every = dkv[...].reshape(512, 128)
+        value_sum = jnp.broadcast_to(jnp.sum(every.astype(F32), axis=0, keepdims=True), (8, 128))
+        for j in range(4):
+            at = pl.ds(pl.multiple_of((j % 2) * 512 + yh * 256, 256), 256)
+            out = lax.dot_general(adu[j // 2, :, at], every, TN, preferred_element_type=F32).reshape(4, 2, 32, 128)
+            for i in range(4):
+                gkv[j, i, 0:32] = jnp.where(yl == 0, out[i, 0], out[i, 1])
+                gkv[j, i, 32:40] = value_sum
+
+        def key_value():
+            k = [net.slot() for _ in range(7)]
+            for i, (name, d) in enumerate((("zu", net.zu), ("zd", net.zd), ("zo", net.zo))):
+                net.send(gkv.at[d], gkv_z.at[i], k[i], name)
+            yield
+            for i in range(3):
+                net.got(gkv_z.at[i], k[i])
+            for i in range(4):
+                gkv_x[i] = gkv[z, i] + gkv_z[0, i] + gkv_z[1, i] + gkv_z[2, i]
+            for i, (name, d) in enumerate((("xu", net.xu), ("xd", net.xd), ("xo", net.xo))):
+                net.send(gkv_x.at[d], gkv_x.at[4 + i], k[3 + i], name)
+            yield
+            for i in range(3):
+                net.got(gkv_x.at[4 + i], k[3 + i])
+            total = gkv_x[x] + gkv_x[4] + gkv_x[5] + gkv_x[6]
+            gkv_x[7, 0:16] = jnp.where(c == 0, total[0:16], total[16:32])
+            gkv_x[7, 16:32] = jnp.where(c == 0, total[16:32], total[0:16])
+            gkv_x[7, 32:40] = total[32:40]
+            net.send(gkv_x.at[7, pl.ds(16, 24)], gkv_x.at[8, pl.ds(16, 24)], k[6], "c")
+            yield
+            net.got(gkv_x.at[8, pl.ds(16, 24)], k[6])
+            here, there = gkv_x[7, 0:16], gkv_x[8, 16:32]
+            kv_out[:, 0:128] = jnp.where(c == 0, here, there)
+            kv_out[:, 128:256] = jnp.where(c == 0, there, here)
+            vb_out[...] = jnp.where(c == 0, gkv_x[8, 32:40], gkv_x[7, 32:40])
+
+        def vectors():
             k = [net.slot() for _ in range(13)]
             at = vecs.at[y, c]
             for i, name in enumerate(("yu", "yd", "yo", "c")):
@@ -983,66 +1164,99 @@
                 net.got(vec_z.at[4 + i], k[7 + i])
             acc = vec_z[z] + vec_z[4] + vec_z[5] + vec_z[6]
             vec_x[0] = jnp.where(yh == 0, acc[:, :256], acc[:, 256:])
-            for i, name in enumerate(("xu", "xd", "xo")):
-                net.send(vec_x.at[0], vec_x.at[1 + i], k[10 + i], name)
+            spread(net, ("xu", "xd", "xo"), vec_x.at[0], vec_x.at[pl.ds(1, 3)], k[10:])
             yield
             for i in range(3):
                 net.got(vec_x.at[1 + i], k[10 + i])
-            vec[...] = vec_x[0] + vec_x[1] + vec_x[2] + vec_x[3]
-
-        def small_sums():
-            k = [net.slot() for _ in range(7)]
-            for i, (name, d) in enumerate((("zu", net.zu), ("zd", net.zd), ("zo", net.zo))):
-                net.send(small.at[d], small_z.at[i], k[i], name)
+            vec_out[...] = vec_x[0] + vec_x[1] + vec_x[2] + vec_x[3]
+
+        def partner_bias():
+            k = net.slot()
+            net.send(bias.at[2], bias_out.at[1], k, "yo")
+            bias_out[0] = bias[2]
             yield
-            for i in range(3):
-                net.got(small_z.at[i], k[i])
-            for xx in range(4):
-                small_x[xx] = small[z, xx] + small_z[0, xx] + small_z[1, xx] + small_z[2, xx]
-            for i, (name, d) in enumerate((("xu", net.xu), ("xd", net.xd), ("xo", net.xo))):
-                net.send(small_x.at[d], small_x.at[4 + i], k[3 + i], name)
-            yield
-            for i in range(3):
-                net.got(small_x.at[4 + i], k[3 + i])
-            lone[...] = small_x[x] + small_x[4] + small_x[5] + small_x[6]
-            net.send(lone, small_y, k[6], "yo")
-            yield
-            net.got(small_y, k[6])
-            small_out[0] = lone[...]
-            small_out[1] = small_y[...]
-
-        run_all(rows(), weight_scatter(net, gq, tmp, swap, out_q), small_sums())
+            net.got(bias_out.at[1], k)
+
+        last = key_value()
+        next(last)
+        next(rows_one, None)
+        run_all(vectors(), last, partner_bias(), query, project, down, up)
         net.finish()
 
     n, d = tokens.shape
-    w = grad_q.shape[-1]
-    tile = small.shape[-2:]
+
+    def bf(*shape):
+        return jax.ShapeDtypeStruct(shape, BF16)
+
+    def f32(*shape):
+        return jax.ShapeDtypeStruct(shape, F32)
+
     return pl.pallas_call(
         kernel,
         out_shape=(
-            jax.ShapeDtypeStruct((n, d), F32),
-            jax.ShapeDtypeStruct((n, 2 * w), F32),
-            jax.ShapeDtypeStruct((8, 256), F32),
-            jax.ShapeDtypeStruct((2,) + tile, F32),
+            bf(n, d),
+            f32(n, d),
+            bf(n, d),
+            bf(n, d),
+            bf(n, 512),
+            bf(n, 512),
+            f32(8, 256),
+            f32(2, 16, 128),
+            f32(16, 256),
+            f32(8, 128),
         ),
-        in_specs=[INV] * 8,
-        out_specs=(INV,) * 4,
+        in_specs=[INV, INV, INV] + [ANY] * 8 + [INV, ANY] + [INV] * 5,
+        out_specs=(INV,) * 10,
         scratch_shapes=[
+            VMEM((4, 2, n, d), BF16),
+            VMEM((4, 2, n, d), BF16),
+            VMEM((4, 2, 4, n, 1024), BF16),
+            VMEM((4, 2, 4, n, 1024), BF16),
+            VMEM((4, 2, 4, n, 256), BF16),
+            VMEM((4, 2, 4, n, 256), BF16),
+            VMEM((4, 2, 4, 2, 2, 16, 128), BF16),
+            VMEM((2, 512, 1024), BF16),
+            VMEM((512, 256), F32),
+            VMEM((512, 256), F32),
+            VMEM((4, 2, n, d), BF16),
+            VMEM((4, 2, n, d), BF16),
+            VMEM((4, 2, 4, n, 1024), BF16),
+            VMEM((4, 2, 4, n, 1024), BF16),
+            VMEM((4, 2, 4, n, 256), BF16),
+            VMEM((4, 2, 4, n, 256), BF16),
+            VMEM((n, d), BF16),
+            VMEM((4, 2, n, d), BF16),
+            VMEM((n, d), F32),
+            VMEM((8, d), F32),
+            VMEM((512, 256), BF16),
+            VMEM((2, 2, 2, 256, 128), BF16),
+            VMEM((2, 128, 512), F32),
+            VMEM((512, 256), BF16),
+            VMEM((3, 64, 256), BF16),
+            VMEM((4, 128, 128), BF16),
+            VMEM((4, 4, 40, 128), F32),
+            VMEM((3, 4, 40, 128), F32),
+            VMEM((9, 40, 128), F32),
+            VMEM((3, 16, 128), F32),
+            VMEM((3, 16, 128), F32),
+            VMEM((3, 16, 128), F32),
             VMEM((4, 2, 8, d), F32),
             VMEM((7, 8, 512), F32),
             VMEM((4, 8, 256), F32),
-            VMEM(tile, F32),
-            VMEM((3, 4) + tile, F32),
-            VMEM((7,) + tile, F32),
-            VMEM(tile, F32),
-            VMEM((n, w), BF16),
+            pltpu.SemaphoreType.DMA((24,)),
         ]
         + scatter_scratch(n, d)
-        + plane_scratch(n, w // 2)
-        + sems(8 + 13 + 7 + 17),
-        compiler_params=params(7),
-        name="closing",
-    )(back, tokens, dx1, from_kv, gain, sums, grad_q, small)
+        + scatter_scratch(n, d)
+        + plane_scratch(n, 512)
+        + plane_scratch(n, 512)
+        + plane_scratch(n, 128)
+        + plane_scratch(n, 128)
+        + [VMEM(s, BF16) for s in ((2, 4, n, 256), (2, 4, n, 256), (2, 4, n, 512), (2, 4, n, 512))]
+        + [VMEM(s, BF16) for s in ((2, n, 256), (2, n, 256), (2, n, 512), (2, n, 512))]
+        + sems(200),
+        compiler_params=params(2, 62 << 20),
+        name="backward",
+    )(tokens, cotangent, parents, cot_all, h2, wu, wd, wq, wo, packs, h1, q, kv, o, log_sum, x1, vec, ub)
 
 
 def local(
@@ -1068,10 +1282,7 @@
 ):
     z, yh, x, yl, c = (lax.axis_index(a) for a in AXES)
     tp = yl * 2 + c
-    d = tokens.shape[1]
-
-    def dot(left, right, dims):
-        return lax.dot_general(left, right, ((dims[:1], dims[1:]), ((), ())), preferred_element_type=F32)
+    dp = (z * 2 + yh) * 4 + x
 
     def row(values):
         return jnp.tile(values.astype(BF16).reshape(1, -1), (1, 128 // values.size))
@@ -1083,94 +1294,42 @@
     ubt = jnp.pad(jnp.tile(up_bias.T, (1, 32)).reshape(2, 8, 128), ((0, 0), (0, 8), (0, 0)))
     biases = jnp.concatenate([qbt, ubt], axis=2)
     ancestors = jnp.pad(jnp.broadcast_to(parents.astype(F32)[None], (8, 18)), ((0, 0), (0, 110)))
-    (cot_all, h2, wu, wd, wq, wo, packs, h1, q, kv6, o_rows, log_sum, x1, best, vec, ub) = forward(
+    (cot_all, h2, wu, wd, wq, wo, packs, h1, q, kv, o, log_sum, x1, best, vec, ub) = forward(
         tokens, cotangent, pack, biases, ancestors, w_query, w_out, w_up, w_down
     )
-    cot_all = cot_all.reshape(512, d)
-    wq = wq[:, :, :, :64].reshape(d, -1)
-    wo = wo.reshape(d, -1)
-    wu = wu.reshape(d, -1)
-    wd = wd.reshape(d, -1)
-    h2 = h2.reshape(512, d)
-    w_kv = lax.all_gather(packs[..., :16, :].reshape(d, 128), "c", axis=1, tiled=True)
-    gain1, shift1, gain2, shift2, bias_out, bias_down = (vec[i : i + 1] for i in range(6))
-    segs = vec[8, :32].astype(jnp.int32)
-    ub = ub.reshape(1, 1024)
-    q_blocks = q.reshape(2, 256, 256)
-    o = o_rows.reshape(2, 256, 256)
-    kv_all = kv6.reshape(2, 32, 256, 128).transpose(1, 2, 0, 3).reshape(32, 256, 256)
+    output, grad_input, up_sum, down_sum, out_sum, query_sum, vec_sum, bias_sum, keyval_sum, vb_sum = backward(
+        tokens, cotangent, ancestors, cot_all, h2, wu, wd, wq, wo, packs, h1, q, kv, o, log_sum, x1, vec, ub
+    )
     limit = tau[0]
     head_max = best.reshape(4, 8, 128)[:, 0, 0]
     factor = limit / jnp.maximum(head_max, limit)
     clipped_query = (w_query.astype(F32) * jnp.repeat(factor, 128)[None, :]).astype(BF16)
     clipped_bias = (query_bias.astype(F32) * factor[None, :]).astype(BF16)
 
-    def gate(values):
-        return jax.nn.gelu(values, approximate=True)
-
-    u = dot(h2, wu, (1, 0)) + ub
-    a, gate_back = jax.vjp(gate, u)
-    a = a.astype(BF16)
-    mlp = dot(a, wd, (1, 1)).astype(BF16).reshape(4, 2, 64, d)
-    du = gate_back(dot(cot_all, wd, (1, 0)))[0].astype(BF16)
-    grad_ub = jnp.sum(du.astype(F32), axis=0)
-    grad_down = dot(cot_all, a, (0, 0)).astype(BF16)
-    grad_up = dot(h2, du, (0, 0)).astype(BF16)
-    back2 = dot(du, wu, (1, 1)).astype(BF16).reshape(4, 2, 64, d)
-    output, dx1, dz, sums = turn(mlp, back2, x1, cotangent, gain2, bias_down)
-    dz = dz.reshape(512, d)
-    go = dot(dz, wo, (1, 0)).astype(BF16).reshape(2, 256, 256)
-    grad_out = dot(dz, o_rows, (0, 0)).astype(BF16)
-    up_sum, down_sum, out_sum = scatter_weights(
-        [v.reshape(4, 2, 4, 64, -1) for v in (grad_up, grad_down, grad_out)], 8
-    )
-    dq, slots = attend_back(q_blocks, kv_all, o, go, log_sum, segs, parents)
-    dq = dq.reshape(512, 256)
-    dkv = scatter_kv(slots, segs, parents).reshape(512, 256)
-    back1 = dot(dq, wq, (1, 1)).astype(BF16).reshape(4, 2, 64, d)
-    grad_q = dot(h1, dq, (0, 0)).astype(BF16).reshape(4, 2, 4, 64, 256)
-    grad_kv = dot(h1, dkv, (0, 0)).reshape(4, 2, 4, 4, 16, 256)
-    grad_kv = lax.dynamic_index_in_dim(lax.dynamic_index_in_dim(grad_kv, yh, 1, False), tp, 2, False)
-    dkv_own = lax.dynamic_slice_in_dim(dkv, yh * 256 + tp * 64, 64, 0)
-    from_kv = dot(dkv_own, w_kv, (1, 1))
-    gqb = jnp.sum(dq.astype(F32), axis=0).reshape(2, 128).T.reshape(4, 2, 4, 8)
-    gub = grad_ub.reshape(8, 128).T.reshape(4, 2, 4, 32)
-    gvb = jnp.sum(dkv[:, 128:].astype(F32), axis=0).reshape(4, 2, 4, 4)
-    gvb = lax.dynamic_index_in_dim(lax.dynamic_index_in_dim(gvb, yh, 1, False), tp, 2, False)
-    bias_rows = jnp.concatenate([gqb, gub], axis=3).transpose(0, 2, 1, 3)
-    bias_rows = jnp.pad(bias_rows, ((0, 0), (0, 0), (0, 1), (0, 256 - 40)))
-    bias_rows = bias_rows.at[:, :, 2, 0].set(gvb)
-    bias_rows = jnp.pad(bias_rows, ((0, 0), (0, 0), (0, 5), (0, 0)))
-    small_grads = jnp.concatenate([grad_kv, bias_rows], axis=2)
-    grad_input, query_sum, vec, small_sum = closing(
-        back1, tokens, dx1, from_kv, gain1, sums, grad_q, small_grads
-    )
-    keyval_sum = small_sum[0, :16]
-    valueb_sum = small_sum[0, 18, :1]
-    own_bias = lax.dynamic_index_in_dim(small_sum[0, 16:18, :40], yh, 0, False)
-    oth_bias = lax.dynamic_index_in_dim(small_sum[1, 16:18, :40], yh, 0, False)
-    first = jnp.where(yh == 0, own_bias, oth_bias)
-    second = jnp.where(yh == 0, oth_bias, own_bias)
-    qbias_sum = jnp.concatenate([first[:8].reshape(4, 2), second[:8].reshape(4, 2)], axis=1)
-    ubias_sum = jnp.concatenate([first[8:].reshape(4, 8), second[8:].reshape(4, 8)], axis=1)
-    vec = lax.dynamic_slice(vec, (jnp.int32(0), x * 64 + tp * 16), (6, 16))
+    own = lax.dynamic_slice(bias_sum, (jnp.int32(0), jnp.int32(0), dp * 4), (2, 10, 4))
+    low = jnp.where(yh == 0, own[0], own[1])
+    high = jnp.where(yh == 0, own[1], own[0])
+    qbias_sum = jnp.concatenate([low[8:10], high[8:10]], axis=0).T
+    ubias_sum = jnp.concatenate([low[:8], high[:8]], axis=0).T
+    valueb_sum = lax.dynamic_slice(vb_sum, (jnp.int32(0), dp * 4 + tp), (1, 1)).reshape(1)
+    vec_sum = lax.dynamic_slice(vec_sum, (jnp.int32(0), x * 64 + tp * 16), (6, 16))
     return (
         output,
         grad_input,
-        query_sum,
-        up_sum,
-        out_sum,
-        down_sum,
+        query_sum.astype(F32),
+        up_sum.astype(F32),
+        out_sum.astype(F32),
+        down_sum.astype(F32),
         qbias_sum,
         ubias_sum,
         keyval_sum,
         valueb_sum,
-        vec[0],
-        vec[1],
-        vec[2],
-        vec[3],
-        vec[4],
-        vec[5],
+        vec_sum[0],
+        vec_sum[1],
+        vec_sum[2],
+        vec_sum[3],
+        vec_sum[4],
+        vec_sum[5],
         clipped_query,
         clipped_bias,
     )

time: 434 us -> 305 us (0.70); the launches traced: 429 us -> 305 us
  Pallas kernels: 322 us -> 277 us
  matrix products: 38.5 us -> 0 us
  local copies, waits for them, and re-layouts: 43.9 us -> 13.5 us
  between operations: 15.9 us -> 2.11 us
    pallas_call x5 -> x1, Pallas kernels: 196 us -> 152 us  [backward(): pl.pallas_call(kernel, out_shape=(bf(n, d), f32(n, d), bf(n, d), bf(n, d)...]
    dot_general x12 -> x0, matrix products: 38.5 us -> none  [dot(): lax.dot_general(left, right, ((dims[:1], dims[1:]), ((), ())), preferred_...]
    reshape x7 -> x0, local copies, waits for them, and re-layouts: 16.4 us -> none  [the longest x2 16.1 us: local(): kv6.reshape(2, 32, 256, 128).transpose(1, 2, 0, 3).reshape(32, 256, 256)]
    slice x11 -> x5, local copies, waits for them, and re-layouts: 5.95 us -> 0.18 us  [the longest x4 0.17 us: local(): ubias_sum = jnp.concatenate([low[:8], high[:8]], axis=0).T]
    convert_element_type x1 -> x4, other arithmetic: 1.19 us -> 6.56 us  [the longest x1 1.78 us: local(): up_sum.astype(F32)]
  transfers between devices with their start and end apart: 1 -> 0, of which waited for: 0 -> 0; matrix products, arithmetic and copies ran while one was open for 15% -> 0% of each run, Pallas kernels for 37% -> 0%
where the time goes in v3:
time: 305 us
  Pallas kernels  277 us (91%)
  local copies, waits for them, and re-layouts  13.5 us (4%)
  other arithmetic  11.9 us (4%)
    pallas_call x1, Pallas kernels, backward(): pl.pallas_call(kernel, out_shape=(bf(n, d), f32(n, d), bf(n, d), bf(n, d)...  152 us
    pallas_call x1, Pallas kernels, forward(): pl.pallas_call(kernel, out_shape=(rows, rows, bf(4, 2, 4, n, 1024), bf(4,...  126 us

profile of v3, /device:TPU:0, one launch (start us, length us, event | category | flops | bytes accessed | tf_op | source)
XLA Modules:
  0.0 304.9 jit_solution(725252391305971459)
XLA Ops:
  0.7 0.7 fusion.3
  1.4 0.7 tile.80
  2.0 0.1 tile.81
  2.1 0.7 tile.82
  2.8 0.1 tile.83
  2.9 0.7 tile.84
  3.5 0.1 tile.85
  3.6 0.7 tile.86
  4.3 0.1 tile.87
  4.4 0.7 tile.88
  5.0 0.1 tile.89
  5.1 0.7 tile.90
  5.8 0.1 tile.91
  6.5 0.7 convert.3
  7.3 0.1 concatenate.18
  7.3 0.1 concatenate.19
  7.4 0.6 pad_maximum_fusion.pack
  8.0 0.7 convert_element_type.34
  8.7 0.6 pad.15.parents
  9.3 0.7 tile.98
  10.0 0.1 tile.99
  10.1 0.1 copy.44
  10.1 0.8 copy.43
  10.9 0.1 tile.97
  11.0 0.6 fusion.2.biases
  11.7 125.6 %forward.1 = (bf16[4,2,64,2048]{3,2,1,0:T(8,128)(2,1)}, bf16[4,2,64,2048]{3,2,1,0:T(8,128)(2,1)}, bf16[4,2,4,64,1024]{4,3,2,1,0:T(8,128)(2,1)}, bf16[4,2,4,64,10...) custom-call(bf16[64,2048]{1,0:T(8,128)(2,1)} %tok.3, ...), custom_call_target="tpu_custom_call" | custom-call | tf_op jit(solution)/shard_map/forward/pallas_call | solution.py:631
  137.3 151.8 %backward.1 = (bf16[64,2048]{1,0:T(8,128)(2,1)}, f32[64,2048]{1,0:T(8,128)}, bf16[64,2048]{1,0:T(8,128)(2,1)}, bf16[64,2048]{1,0:T(8,128)(2,1)}, bf16[64,512]{1,...) custom-call(bf16[64,2048]{1,0:T(8,128)(2,1)} %tok.3, ...), custom_call_target="tpu_custom_call" | custom-call | tf_op jit(solution)/shard_map/backward/pallas_call | solution.py:1194
  289.1 0.0 copy-start.1
  289.2 0.9 dynamic-slice_select_fusion.1
  290.0 0.1 copy.46
  290.1 0.1 copy.45
  290.2 0.7 maximum_bitcast_fusion.1
  290.9 0.7 copy.48
  291.5 1.8 convert_element_type.36
  293.3 1.8 convert_element_type.38
  295.1 1.5 convert_element_type.35
  296.6 1.5 convert_element_type.37
  298.1 1.3 constant_dynamic-slice_fusion.1
  299.4 0.1 constant_dynamic-slice_fusion
  299.4 0.5 slice_bitcast_fusion.2
  300.0 0.7 slice.87
  300.7 0.1 copy.49
  301.5 0.1 broadcast_bitcast_fusion
  301.5 0.6 multiply_convert_fusion
  302.2 0.6 multiply_convert_fusion.1
  302.7 0.7 copy.55
  303.4 0.8 copy.56
  304.2 0.6 copy.57
  (21 shorter events, 0.1 us)
Async XLA Ops:
  289.1 10.3 %copy-start.5 = (f32[8,256]{1,0:T(8,128)S(1)}, f32[8,256]{1,0:T(8,128)}, u32[]{:S(2)}) copy-start(f32[8,256]{1,0:T(8,128)} %get-tuple-element.68) | copy-start | bytes 24580
  289.1 12.4 %copy-start.1 = (bf16[64,512]{1,0:T(8,128)(2,1)S(1)}, bf16[64,512]{1,0:T(8,128)(2,1)}, u32[]{:S(2)}) copy-start(bf16[64,512]{1,0:T(8,128)(2,1)} %wq_in.1) | copy-start | bytes 196612
  289.1 13.1 %copy-start.4 = (bf16[4,4]{1,0:T(4,128)(2,1)S(1)}, bf16[4,4]{1,0:T(4,128)(2,1)}, u32[]{:S(2)}) copy-start(bf16[4,4]{1,0:T(4,128)(2,1)} %param.28) | copy-start | bytes 100
  289.1 13.6 %copy-start.2 = (bf16[64,2048]{1,0:T(8,128)(2,1)S(1)}, bf16[64,2048]{1,0:T(8,128)(2,1)}, u32[]{:S(2)}) copy-start(bf16[64,2048]{1,0:T(8,128)(2,1)} %get-tuple-element.136) | copy-start | bytes 786436
  289.1 14.3 %copy-start = (f32[64,2048]{1,0:T(8,128)S(1)}, f32[64,2048]{1,0:T(8,128)}, u32[]{:S(2)}) copy-start(f32[64,2048]{1,0:T(8,128)} %get-tuple-element.137) | copy-start | bytes 1572868
  289.1 15.1 %copy-start.3 = (f32[16,256]{1,0:T(8,128)S(1)}, f32[16,256]{1,0:T(8,128)}, u32[]{:S(2)}) copy-start(f32[16,256]{1,0:T(8,128)} %get-tuple-element.144) | copy-start | bytes 49156

commit v4 on v3

--- a/solution.py
+++ b/solution.py
@@ -49,6 +49,7 @@
 
     def slot(self):
         self.count += 1
+        assert self.count <= self.send_sems.shape[0]
         return self.count - 1
 
     def copy(self, src, dst, k, name):
@@ -172,53 +173,72 @@
 BOTH = slice(None)
 
 
-def plane_gather(net, o):
+def plane_gather(net, o, theirs=None):
     z, x, xu, xd, xo, zu, zd, zo = net.z, net.x, net.xu, net.xd, net.xo, net.zu, net.zd, net.zo
     k = [net.slot() for _ in range(16)]
     every = slice(None)
-
-    def send(view, i, name):
-        net.send(view, view, k[i], name)
-
-    def got(view, i):
-        net.got(view, k[i])
-
-    send(o(z, BOTH, x, 0), 0, "xu")
-    send(o(z, BOTH, x, 0), 1, "xd")
-    send(o(z, BOTH, x, 1), 2, "zu")
-    send(o(z, BOTH, x, 1), 3, "zd")
-    yield
-    got(o(z, BOTH, xd, 0), 0)
-    send(o(z, 0, xd, 0), 4, "xu")
-    got(o(zd, BOTH, x, 1), 2)
-    send(o(zd, 0, x, 1), 6, "zu")
-    got(o(z, BOTH, xu, 0), 1)
-    send(o(z, 1, xu, 0), 5, "xd")
-    got(o(zu, BOTH, x, 1), 3)
-    send(o(zu, 1, x, 1), 7, "zd")
-    yield
-    got(o(z, 0, xo, 0), 4)
-    got(o(z, 1, xo, 0), 5)
-    send(o(z, BOTH, every, 0), 8, "zu")
-    send(o(z, BOTH, every, 0), 9, "zd")
-    got(o(zo, 0, x, 1), 6)
-    got(o(zo, 1, x, 1), 7)
-    send(o(every, BOTH, x, 1), 10, "xu")
-    send(o(every, BOTH, x, 1), 11, "xd")
-    yield
-    got(o(zd, BOTH, every, 0), 8)
-    send(o(zd, 0, every, 0), 12, "zu")
-    got(o(every, BOTH, xd, 1), 10)
-    send(o(every, 0, xd, 1), 14, "xu")
-    got(o(zu, BOTH, every, 0), 9)
-    send(o(zu, 1, every, 0), 13, "zd")
-    got(o(every, BOTH, xu, 1), 11)
-    send(o(every, 1, xu, 1), 15, "xd")
-    yield
-    got(o(zo, 0, every, 0), 12)
-    got(o(zo, 1, every, 0), 13)
-    got(o(every, 0, xo, 1), 14)
-    got(o(every, 1, xo, 1), 15)
+    relayed = []
+
+    def send(at, i, name):
+        net.send(o(*at), o(*at), k[i], name)
+
+    def got(at, i):
+        net.got(o(*at), k[i])
+
+    def relay(*at):
+        if theirs is not None:
+            slot = net.slot()
+            net.send(o(*at), o(*at), slot, "c")
+            relayed.append((at, slot))
+
+    send((z, BOTH, x, 0), 0, "xu")
+    send((z, BOTH, x, 0), 1, "xd")
+    send((z, BOTH, x, 1), 2, "zu")
+    send((z, BOTH, x, 1), 3, "zd")
+    relay(z, BOTH, x, 0)
+    relay(z, BOTH, x, 1)
+    yield
+    got((z, BOTH, xd, 0), 0)
+    send((z, 0, xd, 0), 4, "xu")
+    got((zd, BOTH, x, 1), 2)
+    send((zd, 0, x, 1), 6, "zu")
+    got((z, BOTH, xu, 0), 1)
+    send((z, 1, xu, 0), 5, "xd")
+    got((zu, BOTH, x, 1), 3)
+    send((zu, 1, x, 1), 7, "zd")
+    for at in ((z, BOTH, xd, 0), (zd, BOTH, x, 1), (z, BOTH, xu, 0), (zu, BOTH, x, 1)):
+        relay(*at)
+    yield
+    got((z, 0, xo, 0), 4)
+    got((z, 1, xo, 0), 5)
+    send((z, BOTH, every, 0), 8, "zu")
+    send((z, BOTH, every, 0), 9, "zd")
+    got((zo, 0, x, 1), 6)
+    got((zo, 1, x, 1), 7)
+    send((every, BOTH, x, 1), 10, "xu")
+    send((every, BOTH, x, 1), 11, "xd")
+    relay(z, BOTH, xo, 0)
+    relay(zo, BOTH, x, 1)
+    yield
+    got((zd, BOTH, every, 0), 8)
+    send((zd, 0, every, 0), 12, "zu")
+    got((every, BOTH, xd, 1), 10)
+    send((every, 0, xd, 1), 14, "xu")
+    got((zu, BOTH, every, 0), 9)
+    send((zu, 1, every, 0), 13, "zd")
+    got((every, BOTH, xu, 1), 11)
+    send((every, 1, xu, 1), 15, "xd")
+    for at in ((zd, BOTH, every, 0), (every, BOTH, xd, 1), (zu, BOTH, every, 0), (every, BOTH, xu, 1)):
+        relay(*at)
+    yield
+    got((zo, 0, every, 0), 12)
+    got((zo, 1, every, 0), 13)
+    relay(zo, BOTH, every, 0)
+    got((every, 0, xo, 1), 14)
+    got((every, 1, xo, 1), 15)
+    relay(every, BOTH, xo, 1)
+    for at, slot in relayed:
+        net.got(theirs(*at), slot)
 
 
 def add_into(dst, *others):
@@ -436,98 +456,130 @@
     return top
 
 
-def forward(tokens, cotangent, pack, biases, parents, w_query, w_out, w_up, w_down):
-    def kernel(tok, cot, pack, biases, parents, wq_in, wo_in, wu_in, wd_in,
-               cot_out, h2, wu, wd, wq_out, wo_out, pack_out, h1_out, q_out, kv_out, o, log_sum, x1, best, vec, ub,
-               tok_all, h1, packs, wq, wo, q, kv, scores, part, own, mine, got, local, *rest):
+def one_hot(rows, lanes, hit):
+    row = lax.broadcasted_iota(jnp.int32, (rows, lanes), 0)
+    lane = lax.broadcasted_iota(jnp.int32, (rows, lanes), 1)
+    return hit(row, lane).astype(F32).astype(BF16)
+
+
+def forward(tokens, cotangent, seg_ids, parents, vectors, query_bias, up_bias, w_keyval, w_query, w_out, w_up, w_down):
+    def kernel(tok, cot, seg_in, par_in, vec_in, qb_in, ub_in, wkv_in, wq_in, wo_in, wu_in, wd_in,
+               cot_out, h2, wu, wd, wq_out, wo_out, wkv_out, h1_out, q_out, kv_out, o, log_sum, x1, best, vec, ub,
+               tok_all, h1, wkv, wq, wo, q, kv, scores, part, own, mine, got, pack, pairs, halves, tiles, local,
+               *rest):
         *scratch, ss, rs = rest
         net = Net(ss, rs)
         z, yh, x, yl, c, y = net.z, net.yh, net.x, net.yl, net.c, net.y
         starts = [
             pltpu.make_async_copy(src, dst, local.at[i])
-            for i, (src, dst) in enumerate(
-                (
-                    (tok, tok_all.at[y, c]),
-                    (cot, cot_out.at[y, c]),
-                    (pack.at[c], packs.at[z, yh, x, yl, c]),
-                    (biases.at[yh], wq.at[z, yh, x, pl.ds(64, 16)]),
-                )
-            )
+            for i, (src, dst) in enumerate(((tok, tok_all.at[y, c]), (cot, cot_out.at[y, c])))
         ]
         for one in starts:
             one.start()
-        net.barrier(PLANE + RING + ("yo",))
-
-        def parameters():
-            k = [net.slot() for _ in range(4)]
-            pair = packs.at[z, yh, x, yl]
-            net.send(pack.at[1 - c], packs.at[z, yh, x, yl, c], k[0], "c")
-            yield
-            starts[2].wait()
-            net.got(packs.at[z, yh, x, yl, 1 - c], k[0])
-            for i, name in enumerate(("yu", "yd", "yo")):
-                net.send(pair, pair, k[1 + i], name)
-            yield
-            for i, d in enumerate((net.yd, net.yu, net.yo)):
-                net.got(packs.at[z, d // 2, x, lax.rem(d, 2)], k[1 + i])
-
-            def view(zz, half, xx, part):
-                return packs.at[zz, part, xx, pl.ds(0, 2) if half == BOTH else half]
-
-            yield from plane_gather(net, view)
-
-        def bias():
-            k = net.slot()
-            there = wq.at[z, yh, x, pl.ds(64, 16)]
-            net.send(biases.at[1 - yh], there, k, "yo")
-            yield
-            starts[3].wait()
-            net.got(wq.at[z, 1 - yh, x, pl.ds(64, 16)], k)
-
-        def query():
-            steps = weight_gather(net, wq_in, wq, local.at[4])
-            next(steps)
-            yield from bias()
-            yield from steps
-
-        later = Ticks(
-            weight_gather(net, wo_in, wo, local.at[5]),
-            weight_gather(net, wu_in, wu, local.at[6]),
-            weight_gather(net, wd_in, wd, local.at[7]),
-        )
-
-        def start_later():
-            yield
-            later.tick()
-
-        run_all(group_gather(net, tok, tok_all), parameters(), query(), start_later())
-        starts[0].wait()
+        row = lax.broadcasted_iota(jnp.int32, (16, 128), 0)
+        lane = lax.broadcasted_iota(jnp.int32, (16, 128), 1)
+        periodic = jnp.dot(vec_in[...], one_hot(16, 128, lambda r, l: l % 16 == r), preferred_element_type=F32)
+        first = jnp.dot(vec_in[...], one_hot(16, 128, lambda r, l: r == 0), preferred_element_type=F32)
+        tile = jnp.where(row < 6, periodic, first)
+        tile = jnp.where(row == 7, seg_in[0].astype(F32), tile).astype(BF16)
+        for i in range(2):
+            pack[i, 0:16] = wkv_in[:, i * 128 : (i + 1) * 128]
+            pack[i, 16:32] = tile
+        four = one_hot(4, 128, lambda r, l: l % 4 == r)
+        heads = lax.dot_general(qb_in[...], four, TN, preferred_element_type=F32)
+        units = lax.dot_general(ub_in[...], four, TN, preferred_element_type=F32)
+        blank = jnp.zeros((6, 128), F32)
+        for i in range(2):
+            halves[i] = jnp.concatenate([units[8 * i : 8 * i + 8], heads[2 * i : 2 * i + 2], blank], axis=0).astype(BF16)
+        pairs[yh, yl, c] = jnp.where(c == 0, pack[0], pack[1])
+        net.barrier(PLANE + RING + ("yo", "xo", "zo"))
+
+        query = weight_gather(net, wq_in, wq, local.at[4])
+        later = Ticks(weight_gather(net, wu_in, wu, local.at[6]), weight_gather(net, wd_in, wd, local.at[7]))
+        project_weight = weight_gather(net, wo_in, wo, local.at[5])
+        toks = group_gather(net, tok, tok_all)
+        ks = [net.slot() for _ in range(11)]
+        net.send(pack.at[1 - c], pairs.at[yh, yl, c], ks[0], "c")
+        net.send(halves.at[1 - yh], halves.at[2], ks[4], "yo")
+        next(query)
+        net.got(pairs.at[yh, yl, 1 - c], ks[0])
+        for i, name in enumerate(("yu", "yd", "yo")):
+            net.send(pairs.at[yh, yl], pairs.at[yh, yl], ks[1 + i], name)
+        next(toks)
+        next(query)
+        net.got(halves.at[2], ks[4])
+        here, there = jnp.where(yh == 0, halves[0], halves[1]), halves[2]
+        low, high = jnp.where(yh == 0, here, there), jnp.where(yh == 0, there, here)
+        tiles[z, x, 1] = jnp.where((lane // 16) % 2 == 0, low.astype(F32), high.astype(F32)).astype(BF16)
+        for i, d in enumerate((net.yd, net.yu, net.yo)):
+            net.got(pairs.at[d // 2, lax.rem(d, 2)], ks[1 + i])
+        merged = jnp.zeros((16, 128), F32)
+        for i in range(8):
+            high, tp = i // 4, i % 4
+            one = pairs[high, tp // 2, tp % 2, 16:32].astype(F32)
+            hit = (row < 6) & (lane // 16 == i)
+            hit = hit | ((row == 6) & (lane // 16 % 2 == high) & (lane % 4 == tp))
+            hit = hit | ((row == 7) & ((lane // 4) % 2 == high))
+            merged = jnp.where(hit, one, merged)
+            wkv[z, high, x, tp // 2, tp % 2] = pairs[high, tp // 2, tp % 2, 0:16]
+        tiles[z, x, 0] = merged.astype(BF16)
+        for i, name in enumerate(("xu", "xd", "xo")):
+            net.send(tiles.at[z, x], tiles.at[z, x], ks[5 + i], name)
+
+        def key_view(zz, half, xx, part):
+            return wkv.at[zz, part, xx, pl.ds(0, 2) if half == BOTH else half]
+
+        keyval = plane_gather(net, key_view)
+        next(keyval)
+        next(project_weight)
         later.tick()
-
-        lane = lax.broadcasted_iota(jnp.int32, (16, 128), 1)
-        values = jnp.zeros((16, 128), F32)
+        for i, d in enumerate((net.xd, net.xu, net.xo)):
+            net.got(tiles.at[z, d], ks[5 + i])
+        for i, name in enumerate(("zu", "zd", "zo")):
+            net.send(tiles.at[z], tiles.at[z], ks[8 + i], name)
+        next(keyval)
+        next(query)
+        next(toks)
+        next(keyval)
+        next(query)
+        next(project_weight)
+        later.tick()
+        next(toks)
+        next(keyval)
+        next(query)
+        next(project_weight)
+        for i, d in enumerate((net.zd, net.zu, net.zo)):
+            net.got(tiles.at[d], ks[8 + i])
+
+        value_bias = jnp.zeros((16, 128), F32)
+        biases = jnp.zeros((16, 128), F32)
         segs = jnp.zeros((16, 128), F32)
-        for j in range(16):
-            block = jnp.zeros((16, 128), F32)
-            for k in range(8):
-                dev = 8 * j + k
-                dp, tp = dev // 4, dev % 4
-                tile = packs[dp // 8, dp // 4 % 2, dp % 4, tp // 2, tp % 2, 16:32].astype(F32)
-                block = jnp.where(lane // 16 == k, tile, block)
-                values = jnp.where(lane == dev, tile, values)
-                if tp == 0:
-                    segs = jnp.where(lane == dp, tile, segs)
-            vec[:, j * 128 : (j + 1) * 128] = block
-        value_bias = values[6:7]
+        for zz in range(4):
+            come = [tiles[zz, xx, 0].astype(F32) for xx in range(4)]
+            turned = [pltpu.roll(one, 64, 1) for one in come]
+            for xx in range(4):
+                at = (lane // 32 == zz) & ((lane // 4) % 4 == xx)
+                value_bias = jnp.where(at, come[xx], value_bias)
+                biases = jnp.where(at, tiles[zz, xx, 1].astype(F32), biases)
+                segs = jnp.where((lane // 8 == zz) & (lane % 4 == xx), come[xx], segs)
+            for high in range(2):
+                for pair in range(2):
+                    even = come[2 * pair] if high == 0 else turned[2 * pair]
+                    odd = turned[2 * pair + 1] if high == 0 else come[2 * pair + 1]
+                    j = (zz * 2 + high) * 2 + pair
+                    vec[:, j * 128 : (j + 1) * 128] = jnp.where(lane < 64, even, odd)
+        value_bias = value_bias[6:7]
         segs = segs[7:8]
         vec[8:9, 0:128] = segs
-        query_bias = jnp.zeros((16, 256), F32)
-        lane = lax.broadcasted_iota(jnp.int32, (16, 256), 1) & 127
-        for dp in range(32):
-            tile = wq[dp // 8, dp // 4 % 2, dp % 4, 64:80].astype(F32)
-            query_bias = jnp.where(lane // 4 == dp, tile, query_bias)
-        ub[...] = query_bias[:8, 128:]
-        query_bias = jnp.concatenate([query_bias[0:1, :128], query_bias[1:2, :128]], axis=1)
+        ub[...] = biases[0:8]
+        query_bias = jnp.concatenate([biases[8:9], biases[9:10]], axis=1)
+        parent = jnp.zeros((1, 128), F32)
+        for i in range(18):
+            parent = jnp.where(lane[0:1] == i, par_in[i].astype(F32), parent)
+        vec[9:10, 0:128] = parent
+        for _ in toks:
+            pass
+        starts[0].wait()
 
         gain1, shift1 = vec[0:1], vec[1:2]
 
@@ -537,13 +589,18 @@
             return carry
 
         lax.fori_loop(0, 8, norm_rows, 0)
+        next(project_weight)
+        for _ in query:
+            pass
+        for _ in keyval:
+            pass
 
         def project(i, carry):
             rows = pl.ds(pl.multiple_of(i * 256, 256), 256)
             h = h1[rows]
-            weight = wq[:, :, :, :64].reshape(2048, 256)
+            weight = wq[...].reshape(2048, 256)
             q[rows] = (jnp.dot(h, weight, preferred_element_type=F32) + query_bias).astype(BF16)
-            weight = packs[:, :, :, :, :, :16].reshape(2048, 128)
+            weight = wkv[...].reshape(2048, 128)
             shift = value_bias * c.astype(F32)
             kv[c, z, i, x] = (jnp.dot(h, weight, preferred_element_type=F32) + shift).astype(BF16)
             return carry
@@ -554,41 +611,40 @@
             rows = pl.ds(0, 256) if half == BOTH else pl.ds(128 * half, 128)
             return kv.at[c, zz, part, xx, rows]
 
-        keys = plane_gather(net, view)
+        def their_view(zz, half, xx, part):
+            rows = pl.ds(0, 256) if half == BOTH else pl.ds(128 * half, 128)
+            return kv.at[1 - c, zz, part, xx, rows]
+
+        keys = plane_gather(net, view, their_view)
         cots = group_gather(net, cot, cot_out)
         next(keys)
         later.tick()
         next(cots)
         next(keys)
+        next(project_weight)
         next(keys)
         next(cots)
         next(keys)
         later.tick()
+        next(cots)
         for _ in keys:
             pass
-        k = net.slot()
-        net.send(kv.at[c], kv.at[c], k, "c")
-        next(cots)
-        net.got(kv.at[1 - c], k)
 
         saves = [
             pltpu.make_async_copy(src, dst, local.at[8 + i])
             for i, (src, dst) in enumerate(
-                ((wq, wq_out), (packs, pack_out), (h1, h1_out), (q, q_out), (kv, kv_out), (wo, wo_out))
+                ((wq, wq_out), (wkv, wkv_out), (h1, h1_out), (q, q_out), (kv, kv_out), (wo, wo_out))
             )
         ]
         for one in saves[:5]:
             one.start()
-        parent = parents[0:1]
         top = attend(0, z, x, q, kv, segs, parent, scores, o, log_sum)
-        next(later.steps[0], None)
         top = jnp.maximum(top, attend(1, z, x, q, kv, segs, parent, scores, o, log_sum))
         for h in range(2):
             mine[0, 8 * h : 8 * h + 8] = jnp.full((8, 128), jnp.max(top[:, h * 256 : (h + 1) * 256]), F32)
-        for _ in later.steps[0]:
+        for _ in project_weight:
             pass
         saves[5].start()
-        later.tick()
 
         def project_out(i, d):
             rows = o[pl.ds(pl.multiple_of(d * 128, 128), 128)]
@@ -598,19 +654,28 @@
                 part[d, 0, :, j * 512 : (j + 1) * 512] = out[:64]
                 part[d, 1, :, j * 512 : (j + 1) * 512] = out[64:]
 
-        def rows():
-            def total(summed):
-                value = tok[...].astype(F32) + (summed + vec[4:5])
-                x1[...] = value
-                own[...] = (normed(value)[0] * vec[2:3] + vec[3:4]).astype(BF16)
-
-            yield from group_scatter(net, part, *scratch, total, project_out)
-            me = pltpu.make_async_copy(own, h2.at[y, c], local.at[14])
-            me.start()
-            yield from group_gather(net, own, h2)
-            me.wait()
-
-        run_all(rows(), heads_max(net, mine, got, best))
+        def total(summed):
+            value = tok[...].astype(F32) + (summed + vec[4:5])
+            x1[...] = value
+            own[...] = (normed(value)[0] * vec[2:3] + vec[3:4]).astype(BF16)
+
+        rows = group_scatter(net, part, *scratch, total, project_out)
+        largest = heads_max(net, mine, got, best)
+        for _ in range(3):
+            next(rows)
+            next(largest)
+        next(rows)
+        later.tick()
+        next(rows, None)
+        me = pltpu.make_async_copy(own, h2.at[y, c], local.at[14])
+        me.start()
+        spreading = group_gather(net, own, h2)
+        next(spreading)
+        for _ in largest:
+            pass
+        for _ in spreading:
+            pass
+        me.wait()
         for _ in cots:
             pass
         later.tick()
@@ -635,9 +700,9 @@
             rows,
             bf(4, 2, 4, n, 1024),
             bf(4, 2, 4, n, 1024),
-            bf(4, 2, 4, 80, 256),
             bf(4, 2, 4, n, 256),
-            bf(4, 2, 4, 2, 2, 32, 128),
+            bf(4, 2, 4, n, 256),
+            bf(4, 2, 4, 2, 2, 16, 128),
             bf(512, d),
             bf(512, 256),
             bf(2, 4, 2, 4, 256, 128),
@@ -648,13 +713,13 @@
             f32(16, d),
             f32(8, 128),
         ),
-        in_specs=[INV, ANY, INV, INV, INV, ANY, ANY, ANY, ANY],
+        in_specs=[INV, INV, INS, INS] + [INV] * 8,
         out_specs=(ANY,) * 10 + (INV,) * 6,
         scratch_shapes=[
             VMEM((4, 2, n, d), BF16),
             VMEM((512, d), BF16),
-            VMEM((4, 2, 4, 2, 2, 32, 128), BF16),
-            VMEM((4, 2, 4, 80, 256), BF16),
+            VMEM((4, 2, 4, 2, 2, 16, 128), BF16),
+            VMEM((4, 2, 4, n, 256), BF16),
             VMEM((4, 2, 4, n, 256), BF16),
             VMEM((512, 256), BF16),
             VMEM((2, 4, 2, 4, 256, 128), BF16),
@@ -663,13 +728,17 @@
             VMEM((n, d), BF16),
             VMEM((5, 16, 128), F32),
             VMEM((7, 16, 128), F32),
+            VMEM((2, 32, 128), BF16),
+            VMEM((2, 2, 2, 32, 128), BF16),
+            VMEM((3, 16, 128), BF16),
+            VMEM((4, 4, 2, 16, 128), BF16),
             pltpu.SemaphoreType.DMA((15,)),
         ]
         + scatter_scratch(n, d)
-        + sems(160),
+        + sems(190),
         compiler_params=params(1),
         name="forward",
-    )(tokens, cotangent, pack, biases, parents, w_query, w_out, w_up, w_down)
+    )(tokens, cotangent, seg_ids, parents, vectors, query_bias, up_bias, w_keyval, w_query, w_out, w_up, w_down)
 
 
 def normed(values):
@@ -837,8 +906,8 @@
     mine[2] = mine[1] + far[0] + far[1] + far[2]
 
 
-def backward(tokens, cotangent, parents, cot_all, h2, wu, wd, wq, wo, packs, h1, q, kv, o, log_sum, x1, vec, ub):
-    def kernel(tok, cot, parents, cot_in, h2_in, wu_in, wd_in, wq_in, wo_in, packs_in, h1_in, q, kv_in, o, log_sum,
+def backward(tokens, cotangent, cot_all, h2, wu, wd, wq, wo, packs, h1, q, kv, o, log_sum, x1, vec, ub):
+    def kernel(tok, cot, cot_in, h2_in, wu_in, wd_in, wq_in, wo_in, packs_in, h1_in, q, kv_in, o, log_sum,
                x1, vec, ub_in,
                output, grad_input, up_out, down_out, wo_out, wq_out, vec_out, bias_out, kv_out, vb_out,
                h2, cots, wu, wd, wq, wo, packs, adu, us, das, part, part_mlp, gu, gd, gwo, gq, own, dz, dx1, sums, go,
@@ -872,8 +941,8 @@
         for j in range(1, 4):
             load(columns(wu_in, j), columns(wu, j), 2 + j)
             load(columns(wd_in, j), columns(wd, j), 6 + j)
-        loads = [load(wo_in, wo, 10), load(wq_in.at[:, :, :, pl.ds(0, 64)], wq, 11)]
-        loads.append(load(packs_in.at[:, :, :, :, :, pl.ds(0, 16)], packs, 12))
+        loads = [load(wo_in, wo, 10), load(wq_in, wq, 11)]
+        loads.append(load(packs_in, packs, 12))
         net.barrier(PLANE + RING + ("yo", "xo", "zo"))
         pltpu.make_async_copy(h2_in, h2, local.at[0]).wait()
         pltpu.make_async_copy(cot_in, cots, local.at[1]).wait()
@@ -961,10 +1030,16 @@
         down = weight_scatter(net, gd, tmp_d, down_out)
         next(down)
         next(rows_two)
+        next(rows_two)
+        next(rows_two)
+        next(rows_two, None)
+        me = load(own, dz.at[y, c], 23)
+        spreading = group_gather(net, own, dz)
+        next(spreading)
         wide_outer(gu, h2, 1)
+        next(spreading)
         up = weight_scatter(net, gu, tmp_u, up_out)
         next(up)
-        next(rows_two)
         for d in range(4):
             projected(part_mlp, d, adu[0, d * 128 : d * 128 + 128], lambda j: wd[j].reshape(512, 1024))
         keep = [
@@ -972,16 +1047,9 @@
             for w in range(2)
             for r in range(4)
         ]
-        next(rows_two)
-        next(rows_two, None)
-        me = load(own, dz.at[y, c], 23)
-        spreading = group_gather(net, own, dz)
-        next(spreading)
         late = [load(h1_in.at[:, pl.ds(w * 1024, 1024)], adu.at[w], 21 + w) for w in range(2)]
         next(spreading)
         next(down)
-        next(spreading)
-        next(up)
         for _ in spreading:
             pass
         me.wait()
@@ -997,8 +1065,9 @@
         next(rows_out)
         for one in keep:
             one.wait()
-        steps = attend_back(z, x, q, wd, o, go, log_sum, vec[8:9, 0:128], parents[0:1], wu, lone, dq_sum, dq)
+        steps = attend_back(z, x, q, wd, o, go, log_sum, vec[8:9, 0:128], vec[9:10, 0:128], wu, lone, dq_sum, dq)
         next(steps)
+        next(up)
         next(rows_out)
         next(steps)
         next(rows_out)
@@ -1205,7 +1274,7 @@
             f32(16, 256),
             f32(8, 128),
         ),
-        in_specs=[INV, INV, INV] + [ANY] * 8 + [INV, ANY] + [INV] * 5,
+        in_specs=[INV, INV] + [ANY] * 8 + [INV, ANY] + [INV] * 5,
         out_specs=(INV,) * 10,
         scratch_shapes=[
             VMEM((4, 2, n, d), BF16),
@@ -1256,7 +1325,77 @@
         + sems(200),
         compiler_params=params(2, 62 << 20),
         name="backward",
-    )(tokens, cotangent, parents, cot_all, h2, wu, wd, wq, wo, packs, h1, q, kv, o, log_sum, x1, vec, ub)
+    )(tokens, cotangent, cot_all, h2, wu, wd, wq, wo, packs, h1, q, kv, o, log_sum, x1, vec, ub)
+
+
+def finish(up, down, out, query, grad_input, output, keyval, vec, bias, value_bias, best, w_query, query_bias, tau):
+    def kernel(up, down, out, query, grad_input, output, keyval, vec, bias, vb, best, wq, qb, tau,
+               output_o, grad_o, query_o, up_o, out_o, down_o, qb_o, ub_o, kv_o, vb_o, v0, v1, v2, v3, v4, v5, wq_o, cb_o):
+        for src, dst in ((output, output_o), (grad_input, grad_o), (keyval, kv_o)):
+            dst[...] = src[...]
+        z, yh, x, yl, c = (lax.axis_index(a) for a in AXES)
+        tp = yl * 2 + c
+        dp = (z * 2 + yh) * 4 + x
+        for src, dst in ((up, up_o), (down, down_o), (out, out_o), (query, query_o)):
+            dst[...] = src[...].astype(F32)
+
+        def pick(rows, count, start):
+            lanes = rows.shape[1]
+            hot = (
+                lax.broadcasted_iota(jnp.int32, (lanes, count), 0)
+                == lax.broadcasted_iota(jnp.int32, (lanes, count), 1) + start
+            ).astype(F32)
+            return hot, rows
+
+        low, high = jnp.where(yh == 0, bias[0], bias[1]), jnp.where(yh == 0, bias[1], bias[0])
+        exact = lax.Precision.HIGHEST
+        hot, rows = pick(jnp.concatenate([low[0:8], high[0:8]], axis=0), 4, dp * 4)
+        ub_o[...] = lax.dot_general(hot, rows, (((0,), (1,)), ((), ())), precision=exact, preferred_element_type=F32)
+        hot, rows = pick(jnp.concatenate([low[8:10], high[8:10], low[10:14]], axis=0), 4, dp * 4)
+        heads = lax.dot_general(hot, rows, (((0,), (1,)), ((), ())), precision=exact, preferred_element_type=F32)
+        qb_o[...] = heads[:, 0:4]
+        hot, rows = pick(vec[...], 16, x * 64 + tp * 16)
+        own = jnp.dot(rows, hot, precision=exact, preferred_element_type=F32)
+        for i, ref in enumerate((v0, v1, v2, v3, v4, v5)):
+            ref[...] = own[i : i + 1]
+        lane = lax.broadcasted_iota(jnp.int32, (1, 128), 1)
+        vb_o[...] = splat(vb[0:1], lane, dp * 4 + tp)
+        limit = tau[0]
+        factors = jnp.zeros((1, 128), F32)
+        for h in range(4):
+            factor = limit / jnp.maximum(best[h // 2, 8 * (h % 2) : 8 * (h % 2) + 1], limit)
+            at = slice(h * 128, (h + 1) * 128)
+            wq_o[:, at] = (wq[:, at].astype(F32) * factor).astype(BF16)
+            factors = jnp.where(lane == h, factor, factors)
+        cb_o[...] = (qb[...].astype(F32) * factors[:, 0:4]).astype(BF16)
+
+    n, d = output.shape
+
+    def f32(*shape):
+        return jax.ShapeDtypeStruct(shape, F32)
+
+    shapes = (
+        jax.ShapeDtypeStruct((n, d), BF16),
+        f32(n, d),
+        f32(n, 512),
+        f32(n, d),
+        f32(n, 512),
+        f32(n, d),
+        f32(4, 4),
+        f32(4, 16),
+        f32(16, 256),
+        f32(1, 1),
+    )
+    shapes += (f32(1, 16),) * 6
+    shapes += (jax.ShapeDtypeStruct((n, 512), BF16), jax.ShapeDtypeStruct((4, 4), BF16))
+    return pl.pallas_call(
+        kernel,
+        out_shape=shapes,
+        in_specs=[INV] * 13 + [INS],
+        out_specs=(INV,) * 18,
+        compiler_params=pltpu.CompilerParams(vmem_limit_bytes=60 << 20),
+        name="finish",
+    )(up, down, out, query, grad_input, output, keyval, vec, bias, value_bias, best, w_query, query_bias, tau)
 
 
 def local(
@@ -1280,59 +1419,20 @@
     out_bias,
     down_bias,
 ):
-    z, yh, x, yl, c = (lax.axis_index(a) for a in AXES)
-    tp = yl * 2 + c
-    dp = (z * 2 + yh) * 4 + x
-
-    def row(values):
-        return jnp.tile(values.astype(BF16).reshape(1, -1), (1, 128 // values.size))
-
-    tile = [row(v) for v in (norm1_gain, norm1_bias, norm2_gain, norm2_bias, out_bias, down_bias, value_bias, seg_ids[:1])]
-    tile = jnp.concatenate(tile + [jnp.zeros((8, 128), BF16)], axis=0)
-    pack = jnp.stack([jnp.concatenate([w_keyval[:, :128], tile]), jnp.concatenate([w_keyval[:, 128:], tile])])
-    qbt = jnp.pad(jnp.tile(query_bias.T, (1, 32)).reshape(2, 2, 128), ((0, 0), (0, 14), (0, 0)))
-    ubt = jnp.pad(jnp.tile(up_bias.T, (1, 32)).reshape(2, 8, 128), ((0, 0), (0, 8), (0, 0)))
-    biases = jnp.concatenate([qbt, ubt], axis=2)
-    ancestors = jnp.pad(jnp.broadcast_to(parents.astype(F32)[None], (8, 18)), ((0, 0), (0, 110)))
-    (cot_all, h2, wu, wd, wq, wo, packs, h1, q, kv, o, log_sum, x1, best, vec, ub) = forward(
-        tokens, cotangent, pack, biases, ancestors, w_query, w_out, w_up, w_down
+    vectors = jnp.pad(value_bias.reshape(1, 1), ((6, 9), (0, 15)))
+    for i, one in enumerate((norm1_gain, norm1_bias, norm2_gain, norm2_bias, out_bias, down_bias)):
+        vectors = vectors + jnp.pad(one.reshape(1, 16), ((i, 15 - i), (0, 0)))
+    (cot_all, h2, wu, wd, wq, wo, wkv, h1, q, kv, o, log_sum, x1, best, vec, ub) = forward(
+        tokens, cotangent, seg_ids, parents, vectors, query_bias, up_bias, w_keyval, w_query, w_out, w_up, w_down
     )
     output, grad_input, up_sum, down_sum, out_sum, query_sum, vec_sum, bias_sum, keyval_sum, vb_sum = backward(
-        tokens, cotangent, ancestors, cot_all, h2, wu, wd, wq, wo, packs, h1, q, kv, o, log_sum, x1, vec, ub
+        tokens, cotangent, cot_all, h2, wu, wd, wq, wo, wkv, h1, q, kv, o, log_sum, x1, vec, ub
     )
-    limit = tau[0]
-    head_max = best.reshape(4, 8, 128)[:, 0, 0]
-    factor = limit / jnp.maximum(head_max, limit)
-    clipped_query = (w_query.astype(F32) * jnp.repeat(factor, 128)[None, :]).astype(BF16)
-    clipped_bias = (query_bias.astype(F32) * factor[None, :]).astype(BF16)
-
-    own = lax.dynamic_slice(bias_sum, (jnp.int32(0), jnp.int32(0), dp * 4), (2, 10, 4))
-    low = jnp.where(yh == 0, own[0], own[1])
-    high = jnp.where(yh == 0, own[1], own[0])
-    qbias_sum = jnp.concatenate([low[8:10], high[8:10]], axis=0).T
-    ubias_sum = jnp.concatenate([low[:8], high[:8]], axis=0).T
-    valueb_sum = lax.dynamic_slice(vb_sum, (jnp.int32(0), dp * 4 + tp), (1, 1)).reshape(1)
-    vec_sum = lax.dynamic_slice(vec_sum, (jnp.int32(0), x * 64 + tp * 16), (6, 16))
-    return (
-        output,
-        grad_input,
-        query_sum.astype(F32),
-        up_sum.astype(F32),
-        out_sum.astype(F32),
-        down_sum.astype(F32),
-        qbias_sum,
-        ubias_sum,
-        keyval_sum,
-        valueb_sum,
-        vec_sum[0],
-        vec_sum[1],
-        vec_sum[2],
-        vec_sum[3],
-        vec_sum[4],
-        vec_sum[5],
-        clipped_query,
-        clipped_bias,
+    outs = finish(
+        up_sum, down_sum, out_sum, query_sum, grad_input, output, keyval_sum, vec_sum, bias_sum, vb_sum, best,
+        w_query, query_bias, tau,
     )
+    return outs[:9] + tuple(v.reshape(-1) for v in outs[9:16]) + outs[16:]
 
 
 def solution(mesh):

time: 305 us -> 266 us (0.87)
  Pallas kernels: 277 us -> 263 us
  local copies, waits for them, and re-layouts: 13.5 us -> 0 us
  other arithmetic: 11.9 us -> 1.35 us
    pallas_call x1, Pallas kernels: 126 us -> 107 us  [forward(): pl.pallas_call(kernel, out_shape=(rows, rows, bf(4, 2, 4, n, 1024), bf(4,...]
    convert_element_type x7 -> x0, other arithmetic: 8.43 us -> none  [the longest x1 1.78 us: local(): up_sum.astype(F32)]
    another operation x19 -> x0, local copies, waits for them, and re-layouts: 5.5 us -> none  [the longest x14 4.53 us: row(): return jnp.tile(values.astype(BF16).reshape(1, -1), (1, 128 // values.size))]
where the time goes in v4:
time: 266 us
  Pallas kernels  263 us (99%)
    pallas_call x1, Pallas kernels, backward(): pl.pallas_call(kernel, out_shape=(bf(n, d), f32(n, d), bf(n, d), bf(n, d)...  153 us
    pallas_call x1, Pallas kernels, forward(): pl.pallas_call(kernel, out_shape=(rows, rows, bf(4, 2, 4, n, 1024), bf(4,...  107 us

profile of v4, /device:TPU:0, one launch (start us, length us, event | category | flops | bytes accessed | tf_op | source)
XLA Modules:
  0.0 266.2 jit_solution(8506992694861492638)
XLA Ops:
  1.3 1.3 pad_add_fusion.vec_in
  2.7 106.5 %forward.1 = (bf16[4,2,64,2048]{3,2,1,0:T(8,128)(2,1)}, bf16[4,2,64,2048]{3,2,1,0:T(8,128)(2,1)}, bf16[4,2,4,64,1024]{4,3,2,1,0:T(8,128)(2,1)}, bf16[4,2,4,64,10...) custom-call(bf16[64,2048]{1,0:T(8,128)(2,1)} %tok.3, ...), custom_call_target="tpu_custom_call" | custom-call | tf_op jit(solution)/shard_map/forward/pallas_call | solution.py:696
  109.2 153.2 %backward.1 = (bf16[64,2048]{1,0:T(8,128)(2,1)}, f32[64,2048]{1,0:T(8,128)}, bf16[64,2048]{1,0:T(8,128)(2,1)}, bf16[64,2048]{1,0:T(8,128)(2,1)}, bf16[64,512]{1,...) custom-call(bf16[64,2048]{1,0:T(8,128)(2,1)} %tok.3, ...), custom_call_target="tpu_custom_call" | custom-call | tf_op jit(solution)/shard_map/backward/pallas_call | solution.py:1263
  263.0 3.0 %finish.1 = (bf16[64,2048]{1,0:T(8,128)(2,1)}, f32[64,2048]{1,0:T(8,128)}, f32[64,512]{1,0:T(8,128)}, f32[64,2048]{1,0:T(8,128)}, f32[64,512]{1,0:T(8,128)}, /*i...) custom-call(bf16[64,2048]{1,0:T(8,128)(2,1)} %get-tuple-element.77.u, ...), custom_call_target="tpu_custom_call" | custom-call | tf_op jit(solution)/shard_map/finish/pallas_call | solution.py:1391

commit v5 on v4

--- a/solution.py
+++ b/solution.py
@@ -88,7 +88,39 @@
         live = rest
 
 
+def in_turn(*steps):
+    live = list(steps)
+    while live:
+        live = [one for one in live if next(one, 1) is None]
+        if live:
+            yield
+
+
+def columns_of(ref, h):
+    w = ref.shape[-1] // 2
+    return ref.at[(slice(None),) * (len(ref.shape) - 1) + (pl.ds(h * w, w),)]
+
+
 def group_gather(net, src, out):
+    return in_turn(*(group_gather_one(net, columns_of(src, h), columns_of(out, h)) for h in range(2)))
+
+
+def group_scatter(net, part, acc, from_half, from_full, whole, total, make=None):
+    def one(h):
+        refs = [columns_of(ref, h) for ref in (part, acc, from_half, from_full)]
+        place = columns_of(whole, h)
+
+        def keep(summed):
+            place[...] = summed
+
+        produce = None if make is None else lambda i, d: make(i, d, h)
+        return group_scatter_one(net, *refs, keep, produce)
+
+    yield from in_turn(one(0), one(1))
+    total(whole[...])
+
+
+def group_gather_one(net, src, out):
     y, c, yu, yd, yo = net.y, net.c, net.yu, net.yd, net.yo
     k = [net.slot() for _ in range(9)]
     half = src.shape[0] // 2
@@ -117,7 +149,7 @@
     net.got(out.at[yo, 1 - c, hi], k[8])
 
 
-def group_scatter(net, part, acc, from_half, from_full, total, make=None):
+def group_scatter_one(net, part, acc, from_half, from_full, total, make=None):
     y, c, yu, yd, yo = net.y, net.c, net.yu, net.yd, net.yo
     k = [net.slot() for _ in range(8)]
     n = part.shape[2]
@@ -167,7 +199,7 @@
 
 
 def scatter_scratch(n, w):
-    return [VMEM((4, n, w), BF16), VMEM((2, n // 2, w), BF16), VMEM((2, n, w), BF16)]
+    return [VMEM((4, n, w), BF16), VMEM((2, n // 2, w), BF16), VMEM((2, n, w), BF16), VMEM((n, w), F32)]
 
 
 BOTH = slice(None)
@@ -411,11 +443,12 @@
 NT = (((1,), (1,)), ((), ()))
 TN = (((0,), (0,)), ((), ()))
 SCALE = 128**-0.5
+LOG2E = 1.4426950408889634
 
 
 def attend(b, z, x, q, kv, segs, parents, scores, o, log_sum):
     lane = (lax.broadcasted_iota(jnp.int32, (256, 512), 1) & 255).astype(F32)
-    row = lax.broadcasted_iota(jnp.int32, (256, 512), 0).astype(F32)
+    ahead = lax.broadcasted_iota(jnp.int32, (256, 512), 0).astype(F32) - lane
     block = z * 8 + b * 4 + x
     trunk, leaf, branch, above = place_of(segs, parents, block)
     rows = pl.ds(b * 256, 256)
@@ -423,11 +456,11 @@
     start = block.astype(F32) - 8.0 * trunk
 
     def score(key):
-        return lax.dot_general(key, both, NT, preferred_element_type=F32) * SCALE
+        return lax.dot_general(key, both, NT, preferred_element_type=F32) * (SCALE * LOG2E)
 
     def trunk_score(i, top):
         gap = (start - i.astype(F32)) * 256.0
-        s = jnp.where(row - lane <= gap, score(trunk_block(kv, 0, i, trunk)), NEG)
+        s = jnp.where(ahead <= gap, score(trunk_block(kv, 0, i, trunk)), NEG)
         scores[i] = s
         return jnp.maximum(top, jnp.max(s, axis=0, keepdims=True))
 
@@ -435,13 +468,13 @@
     s = score(parent_block(kv, 0, above)) + (leaf - 1.0) * 1e30
     scores[8] = s
     top = jnp.maximum(top, jnp.max(s, axis=0, keepdims=True))
-    s = jnp.where(row <= lane, score(kv[0, z, b, x]), NEG) + (branch - 1.0) * 1e30
+    s = jnp.where(ahead <= 0.0, score(kv[0, z, b, x]), NEG) + (branch - 1.0) * 1e30
     scores[9] = s
     top = jnp.maximum(top, jnp.max(s, axis=0, keepdims=True))
 
     def weigh(i, value, carry):
         acc, total = carry
-        w = jnp.exp(scores[i] - top)
+        w = jnp.exp2(scores[i] - top)
         acc = acc + lax.dot_general(value, w.astype(BF16), TN, preferred_element_type=F32)
         return acc, total + jnp.sum(w, axis=0, keepdims=True)
 
@@ -452,8 +485,8 @@
     heads = (acc / total).T.astype(BF16)
     o[rows, :128] = heads[:256]
     o[rows, 128:] = heads[256:]
-    log_sum[b] = jnp.broadcast_to(top + jnp.log(total), (8, 512))
-    return top
+    log_sum[b] = jnp.broadcast_to(top + jnp.log2(total), (8, 512))
+    return top * (1.0 / LOG2E)
 
 
 def one_hot(rows, lanes, hit):
@@ -607,15 +640,19 @@
 
         lax.fori_loop(0, 2, project, 0)
 
-        def view(zz, half, xx, part):
-            rows = pl.ds(0, 256) if half == BOTH else pl.ds(128 * half, 128)
-            return kv.at[c, zz, part, xx, rows]
-
-        def their_view(zz, half, xx, part):
-            rows = pl.ds(0, 256) if half == BOTH else pl.ds(128 * half, 128)
-            return kv.at[1 - c, zz, part, xx, rows]
-
-        keys = plane_gather(net, view, their_view)
+        def keys_of(r):
+            def rows(half):
+                return pl.ds(r * 128, 128) if half == BOTH else pl.ds(r * 128 + 64 * half, 64)
+
+            def view(zz, half, xx, part):
+                return kv.at[c, zz, part, xx, rows(half)]
+
+            def their_view(zz, half, xx, part):
+                return kv.at[1 - c, zz, part, xx, rows(half)]
+
+            return plane_gather(net, view, their_view)
+
+        keys = in_turn(keys_of(0), keys_of(1))
         cots = group_gather(net, cot, cot_out)
         next(keys)
         later.tick()
@@ -646,9 +683,9 @@
             pass
         saves[5].start()
 
-        def project_out(i, d):
+        def project_out(i, d, h):
             rows = o[pl.ds(pl.multiple_of(d * 128, 128), 128)]
-            for j in range(4):
+            for j in (2 * h, 2 * h + 1):
                 weight = wo[j].reshape(512, 256)
                 out = lax.dot_general(rows, weight, NT, preferred_element_type=F32).astype(BF16)
                 part[d, 0, :, j * 512 : (j + 1) * 512] = out[:64]
@@ -735,7 +772,7 @@
             pltpu.SemaphoreType.DMA((15,)),
         ]
         + scatter_scratch(n, d)
-        + sems(190),
+        + sems(280),
         compiler_params=params(1),
         name="forward",
     )(tokens, cotangent, seg_ids, parents, vectors, query_bias, up_bias, w_keyval, w_query, w_out, w_up, w_down)
@@ -812,7 +849,7 @@
 
 def attend_back(z, x, q, kv, o, go, log_sum, segs, parents, grad, lone, dq_sum, dq):
     lane = (lax.broadcasted_iota(jnp.int32, (256, 512), 1) & 255).astype(F32)
-    row = lax.broadcasted_iota(jnp.int32, (256, 512), 0).astype(F32)
+    ahead = lax.broadcasted_iota(jnp.int32, (256, 512), 0).astype(F32) - lane
     places = [place_of(segs, parents, z * 8 + b * 4 + x) for b in range(2)]
 
     def stacked(ref, b):
@@ -827,8 +864,8 @@
 
     def one(b, key, value, masked, first):
         both, up = stacked(q, b), stacked(go, b)
-        s = masked(lax.dot_general(key, both, NT, preferred_element_type=F32) * SCALE)
-        p = jnp.exp(s - logs[b])
+        s = masked(lax.dot_general(key, both, NT, preferred_element_type=F32) * (SCALE * LOG2E))
+        p = jnp.exp2(s - logs[b])
         dp = lax.dot_general(value, up, NT, preferred_element_type=F32)
         ds = (p * (dp - inner[b])).astype(BF16)
         more = lax.dot_general(key, ds, TN, preferred_element_type=F32)
@@ -843,7 +880,7 @@
             b,
             piece(kv, 0, z, b, x),
             piece(kv, 1, z, b, x),
-            lambda s: jnp.where(row <= lane, s, NEG) + (branch - 1.0) * 1e30,
+            lambda s: jnp.where(ahead <= 0.0, s, NEG) + (branch - 1.0) * 1e30,
             True,
         )
         key, value = (
@@ -870,7 +907,7 @@
             key, value = (piece(kv, w, 0, yy, xx) * first + piece(kv, w, 1, yy, xx) * second for w in range(2))
             start = (z * 8 + b * 4 + x).astype(F32) - 8.0 * trunk
             gap = (start - i.astype(F32)) * 256.0
-            dk, dv = one(b, key, value, lambda s: jnp.where(row - lane <= gap, s, NEG), False)
+            dk, dv = one(b, key, value, lambda s: jnp.where(ahead <= gap, s, NEG), False)
             parts = [dk * first, dv * first, dk * second, dv * second]
             totals = parts if totals is None else [t + p for t, p in zip(totals, parts)]
         for t in range(2):
@@ -878,9 +915,9 @@
                 put_piece(grad, w, t, yy, xx, totals[2 * t + w])
         return carry
 
-    lax.fori_loop(0, 4, trunk_one, 0)
-    yield
-    lax.fori_loop(4, 8, trunk_one, 0)
+    for i in range(0, 8, 2):
+        lax.fori_loop(i, i + 2, trunk_one, 0)
+        yield
     for b in range(2):
         rows = (dq_sum[b] * SCALE).T.astype(BF16)
         dq[b * 256 : b * 256 + 256, :128] = rows[:256]
@@ -914,14 +951,15 @@
                lone, dq_sum, dq, dkv_from, dkv, gkv, gkv_z, gkv_x, bias, bias_x, bias_z, vecs, vec_z, vec_x,
                local, *rest):
         *scratch, ss, rs = rest
-        first, second, tmp_u, tmp_d, tmp_o, tmp_q, tmp_k = (
-            scratch[:3],
-            scratch[3:6],
-            scratch[6:14],
-            scratch[14:22],
-            scratch[22:30],
-            scratch[30:38],
-            scratch[38:46],
+        first, second, tmp_u, tmp_d, tmp_o, tmp_q, tmp_k, tmp_v = (
+            scratch[:4],
+            scratch[4:8],
+            scratch[8:16],
+            scratch[16:24],
+            scratch[24:32],
+            scratch[32:40],
+            scratch[40:48],
+            scratch[48:56],
         )
         net = Net(ss, rs)
         z, yh, x, yl, c, y = net.z, net.yh, net.x, net.yl, net.c, net.y
@@ -975,7 +1013,7 @@
 
         lax.fori_loop(0, 4, hidden, 0)
 
-        def projected(dst, d, rows, weight):
+        def projected(dst, d, rows, weight, h=None):
             def column(j, carry):
                 out = lax.dot_general(rows, weight(j), NT, preferred_element_type=F32).astype(BF16)
                 at = pl.ds(pl.multiple_of(j * 512, 512), 512)
@@ -983,13 +1021,13 @@
                 dst[d, 1, :, at] = out[64:]
                 return carry
 
-            lax.fori_loop(0, 4, column, 0)
+            lax.fori_loop(0 if h is None else 2 * h, 4 if h is None else 2 * h + 2, column, 0)
 
         def ring_rows(d):
             return pl.ds(pl.multiple_of(d * 128, 128), 128)
 
-        def make_two(i, d):
-            projected(part, d, adu[1, ring_rows(d)], lambda j: wu[j].reshape(512, 1024))
+        def make_two(i, d, h):
+            projected(part, d, adu[1, ring_rows(d)], lambda j: wu[j].reshape(512, 1024), h)
 
         def total_two(summed):
             norm, inverse = normed(x1[...])
@@ -1026,30 +1064,33 @@
 
         rows_two = group_scatter(net, part, *first, total_two, make_two)
         next(rows_two)
+        next(rows_two)
         wide_outer(gd, cots, 0)
         down = weight_scatter(net, gd, tmp_d, down_out)
         next(down)
         next(rows_two)
-        next(rows_two)
+        wide_outer(gu, h2, 1)
+        up = weight_scatter(net, gu, tmp_u, up_out)
+        next(up)
         next(rows_two)
         next(rows_two, None)
         me = load(own, dz.at[y, c], 23)
         spreading = group_gather(net, own, dz)
         next(spreading)
-        wide_outer(gu, h2, 1)
+        for d in range(2):
+            projected(part_mlp, d, adu[0, d * 128 : d * 128 + 128], lambda j: wd[j].reshape(512, 1024))
         next(spreading)
-        up = weight_scatter(net, gu, tmp_u, up_out)
-        next(up)
-        for d in range(4):
+        next(down)
+        for d in range(2, 4):
             projected(part_mlp, d, adu[0, d * 128 : d * 128 + 128], lambda j: wd[j].reshape(512, 1024))
         keep = [
             load(kv_in.at[w, :, :, :, pl.ds(r * 64, 64)], wd.at[:, :, :, :, pl.ds((w * 4 + r) * 128, 128)], 13 + 4 * w + r)
             for w in range(2)
             for r in range(4)
         ]
+        next(spreading)
+        next(up)
         late = [load(h1_in.at[:, pl.ds(w * 1024, 1024)], adu.at[w], 21 + w) for w in range(2)]
-        next(spreading)
-        next(down)
         for _ in spreading:
             pass
         me.wait()
@@ -1063,40 +1104,64 @@
 
         rows_out = group_scatter(net, part_mlp, *second, total_out)
         next(rows_out)
+        outer(gwo, lambda j: dz[:, :, :, pl.ds(pl.multiple_of(j * 512, 512), 512)].reshape(512, 512), o[...])
+        project = weight_scatter(net, gwo, tmp_o, wo_out)
+        next(project)
         for one in keep:
             one.wait()
         steps = attend_back(z, x, q, wd, o, go, log_sum, vec[8:9, 0:128], vec[9:10, 0:128], wu, lone, dq_sum, dq)
+
+        theirs = pl.ds(pl.multiple_of((1 - c) * 512, 512), 512)
+        ours = pl.ds(pl.multiple_of(c * 512, 512), 512)
+
+        def swap(zs, ys):
+            k = [net.slot() for _ in range(4)]
+            zr, yr = pl.ds(zs, 2), pl.ds(ys[0], len(ys))
+            for i in range(4):
+                net.send(wu.at[zr, yr, i, :, theirs], cots.at[zr, yr, :, pl.ds(i * 512, 512)], k[i], "c")
+            yield
+            for i in range(4):
+                net.got(cots.at[zr, yr, :, pl.ds(i * 512, 512)], k[i])
+                for zz in (zs, zs + 1):
+                    for yy in ys:
+                        wu[zz, yy, i, :, ours] = wu[zz, yy, i, :, ours] + cots[zz, yy, :, i * 512 : i * 512 + 512]
+
+        swaps = [swap(2, (0, 1)), swap(0, (0,)), swap(0, (1,))]
         next(steps)
-        next(up)
+        next(down)
         next(rows_out)
         next(steps)
+        next(swaps[0])
+        next(up)
+        next(steps)
+        next(swaps[1])
+        next(down)
         next(rows_out)
+        next(steps)
+        next(swaps[0], None)
+        next(up)
+        next(steps)
+        next(swaps[2])
+        next(swaps[1], None)
         next(down)
+        next(rows_out)
+        next(project)
+        next(steps, None)
         next(up)
-        next(steps, None)
-        next(rows_out)
         next(rows_out, None)
-
-        kc = [net.slot() for _ in range(4)]
-        theirs = pl.ds(pl.multiple_of((1 - c) * 512, 512), 512)
-        for i in range(4):
-            net.send(wu.at[:, :, i, :, theirs], cots.at[:, :, :, pl.ds(i * 512, 512)], kc[i], "c")
         for one in loads[1:] + late:
             one.wait()
 
-        def make_one(i, d):
+        def make_one(i, d, h):
+            projected(h2, d, dq[ring_rows(d)], lambda j: wq[j].reshape(512, 256), h)
             if i == 3:
-                lower = lax.dot_general(
-                    dkv[y], packs[...].reshape(2048, 128), NT, preferred_element_type=F32
-                )
-                upper = lax.dot_general(
-                    dq[ring_rows(d)], wq[...].reshape(2048, 256), NT, preferred_element_type=F32
-                )
-                out = (lower + upper).astype(BF16)
-                h2[d, 0] = out[:64]
-                h2[d, 1] = out[64:]
-            else:
-                projected(h2, d, dq[ring_rows(d)], lambda j: wq[j].reshape(512, 256))
+                for j in (2 * h, 2 * h + 1):
+                    more = lax.dot_general(
+                        dkv[y], packs[j].reshape(512, 128), NT, preferred_element_type=F32
+                    ).astype(BF16)
+                    at = slice(j * 512, (j + 1) * 512)
+                    h2[d, 0, :, at] = h2[d, 0, :, at] + more[:64]
+                    h2[d, 1, :, at] = h2[d, 1, :, at] + more[64:]
 
         def total_one(summed):
             norm, inverse = normed(tok[...].astype(F32))
@@ -1108,22 +1173,18 @@
 
         rows_one = group_scatter(net, h2, *first, total_one, make_one)
         next(rows_one)
-        ours = pl.ds(pl.multiple_of(c * 512, 512), 512)
-        for i in range(4):
-            net.got(cots.at[:, :, :, pl.ds(i * 512, 512)], kc[i])
-
-            def core_sum(j, carry):
-                zz, yy = j // 2, j % 2
-                wu[zz, yy, i, :, ours] = wu[zz, yy, i, :, ours] + cots[zz, yy, :, i * 512 : i * 512 + 512]
-                return carry
-
-            lax.fori_loop(0, 8, core_sum, 0)
-
-        def view(zz, half, xx, part):
-            at = ours if half == BOTH else pl.ds(pl.multiple_of(c * 512 + 256 * half, 256), 256)
-            return wu.at[zz, part, xx, :, at]
-
-        keys = plane_scatter(net, view, tmp_k)
+        next(swaps[2], None)
+
+        def keys_of(r, tmp):
+            def view(zz, half, xx, part):
+                start = c * 512 + r * 256
+                if half == BOTH:
+                    return wu.at[zz, part, xx, :, pl.ds(pl.multiple_of(start, 256), 256)]
+                return wu.at[zz, part, xx, :, pl.ds(pl.multiple_of(start + half * 128, 128), 128)]
+
+            return plane_scatter(net, view, tmp)
+
+        keys = in_turn(keys_of(0, tmp_k), keys_of(1, tmp_v))
         next(keys)
         next(rows_one)
         outer(gq, lambda j: adu[j // 2, :, pl.ds(pl.multiple_of((j % 2) * 512, 512), 512)], dq[...])
@@ -1136,12 +1197,9 @@
         small = all_sums(net, bias, bias_x, bias_z)
         next(small)
         next(rows_one)
-        outer(gwo, lambda j: dz[:, :, :, pl.ds(pl.multiple_of(j * 512, 512), 512)].reshape(512, 512), o[...])
         next(keys)
-        project = weight_scatter(net, gwo, tmp_o, wo_out)
-        next(project)
-        next(down)
-        next(up)
+        next(down, None)
+        next(up, None)
         next(query)
         next(small)
         next(keys)
@@ -1168,8 +1226,8 @@
         for i, name in enumerate(("yu", "yd", "yo")):
             net.send(dkv.at[y], dkv.at[y], kr[3 + i], name)
         next(rows_one)
-        next(down)
-        next(up)
+        next(down, None)
+        next(up, None)
         next(small, None)
         for i, d in enumerate((net.yd, net.yu, net.yo)):
             net.got(dkv.at[d], kr[3 + i])
@@ -1320,9 +1378,11 @@
         + plane_scratch(n, 512)
         + plane_scratch(n, 128)
         + plane_scratch(n, 128)
-        + [VMEM(s, BF16) for s in ((2, 4, n, 256), (2, 4, n, 256), (2, 4, n, 512), (2, 4, n, 512))]
-        + [VMEM(s, BF16) for s in ((2, n, 256), (2, n, 256), (2, n, 512), (2, n, 512))]
-        + sems(200),
+        + [VMEM(s, BF16) for s in ((2, 4, n, 128), (2, 4, n, 128), (2, 4, n, 256), (2, 4, n, 256))]
+        + [VMEM(s, BF16) for s in ((2, n, 128), (2, n, 128), (2, n, 256), (2, n, 256))]
+        + [VMEM(s, BF16) for s in ((2, 4, n, 128), (2, 4, n, 128), (2, 4, n, 256), (2, 4, n, 256))]
+        + [VMEM(s, BF16) for s in ((2, n, 128), (2, n, 128), (2, n, 256), (2, n, 256))]
+        + sems(280),
         compiler_params=params(2, 62 << 20),
         name="backward",
     )(tokens, cotangent, cot_all, h2, wu, wd, wq, wo, packs, h1, q, kv, o, log_sum, x1, vec, ub)

time: 266 us -> 252 us (0.947)
  Pallas kernels: 263 us -> 248 us
    pallas_call x1, Pallas kernels: 153 us -> 138 us  [backward(): pl.pallas_call(kernel, out_shape=(bf(n, d), f32(n, d), bf(n, d), bf(n, d)...]
where the time goes in v5:
time: 252 us; the launch traced here: 251 us
  Pallas kernels  248 us (98%)
    pallas_call x1, Pallas kernels, backward(): pl.pallas_call(kernel, out_shape=(bf(n, d), f32(n, d), bf(n, d), bf(n, d)...  138 us
    pallas_call x1, Pallas kernels, forward(): pl.pallas_call(kernel, out_shape=(rows, rows, bf(4, 2, 4, n, 1024), bf(4,...  107 us

profile of v5, /device:TPU:0, one launch (start us, length us, event | category | flops | bytes accessed | tf_op | source)
XLA Modules:
  0.0 251.3 jit_solution(10864084303098901081)
XLA Ops:
  1.3 1.3 pad_add_fusion.vec_in
  2.7 107.2 %forward.1 = (bf16[4,2,64,2048]{3,2,1,0:T(8,128)(2,1)}, bf16[4,2,64,2048]{3,2,1,0:T(8,128)(2,1)}, bf16[4,2,4,64,1024]{4,3,2,1,0:T(8,128)(2,1)}, bf16[4,2,4,64,10...) custom-call(bf16[64,2048]{1,0:T(8,128)(2,1)} %tok.3, ...), custom_call_target="tpu_custom_call" | custom-call | tf_op jit(solution)/shard_map/forward/pallas_call | solution.py:733
  109.9 137.6 %backward.1 = (bf16[64,2048]{1,0:T(8,128)(2,1)}, f32[64,2048]{1,0:T(8,128)}, bf16[64,2048]{1,0:T(8,128)(2,1)}, bf16[64,2048]{1,0:T(8,128)(2,1)}, bf16[64,512]{1,...) custom-call(bf16[64,2048]{1,0:T(8,128)(2,1)} %tok.3, ...), custom_call_target="tpu_custom_call" | custom-call | tf_op jit(solution)/shard_map/backward/pallas_call | solution.py:1321
  248.1 3.0 %finish.1 = (bf16[64,2048]{1,0:T(8,128)(2,1)}, f32[64,2048]{1,0:T(8,128)}, f32[64,512]{1,0:T(8,128)}, f32[64,2048]{1,0:T(8,128)}, f32[64,512]{1,0:T(8,128)}, /*i...) custom-call(bf16[64,2048]{1,0:T(8,128)(2,1)} %get-tuple-element.77.u, ...), custom_call_target="tpu_custom_call" | custom-call | tf_op jit(solution)/shard_map/finish/pallas_call | solution.py:1451

commit v6 on v5

--- a/solution.py
+++ b/solution.py
@@ -205,7 +205,7 @@
 BOTH = slice(None)
 
 
-def plane_gather(net, o, theirs=None):
+def plane_gather(net, o, theirs=None, last=True):
     z, x, xu, xd, xo, zu, zd, zo = net.z, net.x, net.xu, net.xd, net.xo, net.zu, net.zd, net.zo
     k = [net.slot() for _ in range(16)]
     every = slice(None)
@@ -252,6 +252,10 @@
     relay(z, BOTH, xo, 0)
     relay(zo, BOTH, x, 1)
     yield
+    if not last:
+        for at, i in (((zd, BOTH, every, 0), 8), ((every, BOTH, xd, 1), 10), ((zu, BOTH, every, 0), 9), ((every, BOTH, xu, 1), 11)):
+            got(at, i)
+        return
     got((zd, BOTH, every, 0), 8)
     send((zd, 0, every, 0), 12, "zu")
     got((every, BOTH, xd, 1), 10)
@@ -391,7 +395,7 @@
                 next(one, None)
 
 
-def weight_gather(net, weight, out, local):
+def weight_gather(net, weight, out, local, last=True):
     z, yh, x = net.z, net.yh, net.x
     n, w = weight.shape[0], weight.shape[1] // 2
     k = net.slot()
@@ -405,7 +409,7 @@
     yield
     mine.wait()
     net.got(out.at[z, 1 - yh, x, pl.ds(0, n)], k)
-    yield from plane_gather(net, column_view(out))
+    yield from plane_gather(net, column_view(out), last=last)
 
 
 def splat(row, lane, at):
@@ -528,7 +532,7 @@
         net.barrier(PLANE + RING + ("yo", "xo", "zo"))
 
         query = weight_gather(net, wq_in, wq, local.at[4])
-        later = Ticks(weight_gather(net, wu_in, wu, local.at[6]), weight_gather(net, wd_in, wd, local.at[7]))
+        later = Ticks(weight_gather(net, wu_in, wu, local.at[6]), weight_gather(net, wd_in, wd, local.at[7], False))
         project_weight = weight_gather(net, wo_in, wo, local.at[5])
         toks = group_gather(net, tok, tok_all)
         ks = [net.slot() for _ in range(11)]
@@ -975,24 +979,38 @@
         load(h2_in, h2, 0)
         load(columns(wu_in, 0), columns(wu, 0), 2)
         load(cot_in, cots, 1)
-        load(columns(wd_in, 0), columns(wd, 0), 6)
         for j in range(1, 4):
             load(columns(wu_in, j), columns(wu, j), 2 + j)
-            load(columns(wd_in, j), columns(wd, j), 6 + j)
+        there_d, here_d, every = column_view(wd_in), column_view(wd), slice(None)
+        parts_d = [(zz, BOTH, every, 0) for zz in (z, net.zu, net.zd)]
+        parts_d += [(every, BOTH, xx, 1) for xx in (x, net.xu, net.xd)]
+        loads_d = [load(there_d(*at), here_d(*at), i) for at, i in zip(parts_d, (6, 7, 8, 9, 24, 25))]
         loads = [load(wo_in, wo, 10), load(wq_in, wq, 11)]
         loads.append(load(packs_in, packs, 12))
         net.barrier(PLANE + RING + ("yo", "xo", "zo"))
+        kd = [net.slot() for _ in range(4)]
+        last_parts = (
+            ((net.zd, 0, every, 0), "zu"),
+            ((net.zu, 1, every, 0), "zd"),
+            ((every, 0, net.xd, 1), "xu"),
+            ((every, 1, net.xu, 1), "xd"),
+        )
+        for k, (at, name) in zip(kd, last_parts):
+            net.send(there_d(*at), here_d(*at), k, name)
         pltpu.make_async_copy(h2_in, h2, local.at[0]).wait()
-        pltpu.make_async_copy(cot_in, cots, local.at[1]).wait()
 
         def hidden(j, carry):
             at = pl.ds(pl.multiple_of(j * 256, 256), 256)
             there = pl.ds(0, 4), pl.ds(0, 2), pl.ds(0, 4), pl.ds(0, 64), at
             pltpu.make_async_copy(wu_in.at[there], wu.at[there], local.at[2 + j]).wait()
-            us[...] = jnp.dot(
+            us[:, at] = jnp.dot(
                 h2[...].reshape(512, 2048), wu[there].reshape(2048, 256), preferred_element_type=F32
             )
-            pltpu.make_async_copy(wd_in.at[there], wd.at[there], local.at[6 + j]).wait()
+            return carry
+
+        def hidden_back(j, carry):
+            at = pl.ds(pl.multiple_of(j * 256, 256), 256)
+            there = pl.ds(0, 4), pl.ds(0, 2), pl.ds(0, 4), pl.ds(0, 64), at
             das[...] = jnp.dot(
                 cots[...].reshape(512, 2048), wd[there].reshape(2048, 256), preferred_element_type=F32
             )
@@ -1000,7 +1018,7 @@
 
             def gate(i, total):
                 rows = pl.ds(pl.multiple_of(i * 64, 64), 64)
-                value, slope = smooth_gate(us[rows] + bias_row)
+                value, slope = smooth_gate(us[rows, at] + bias_row)
                 adu[0, rows, at] = value.astype(BF16)
                 du = (das[rows] * slope).astype(BF16)
                 adu[1, rows, at] = du
@@ -1012,6 +1030,12 @@
             return carry
 
         lax.fori_loop(0, 4, hidden, 0)
+        pltpu.make_async_copy(cot_in, cots, local.at[1]).wait()
+        for one in loads_d:
+            one.wait()
+        for k, at in zip(kd, ((net.zo, 0, every, 0), (net.zo, 1, every, 0), (every, 0, net.xo, 1), (every, 1, net.xo, 1))):
+            net.got(here_d(*at), k)
+        lax.fori_loop(0, 4, hidden_back, 0)
 
         def projected(dst, d, rows, weight, h=None):
             def column(j, carry):
@@ -1214,8 +1238,6 @@
         kr = [net.slot() for _ in range(7)]
         for i, (name, d) in enumerate((("yu", net.yu), ("yd", net.yd), ("yo", net.yo))):
             net.send(ring_piece(wu, d), dkv_from.at[i], kr[i], name)
-        next(query)
-        next(project)
         for i in range(3):
             net.got(dkv_from.at[i], kr[i])
         mine = ring_piece(wu, y)[...].astype(F32)
@@ -1226,46 +1248,8 @@
         for i, name in enumerate(("yu", "yd", "yo")):
             net.send(dkv.at[y], dkv.at[y], kr[3 + i], name)
         next(rows_one)
-        next(down, None)
-        next(up, None)
-        next(small, None)
-        for i, d in enumerate((net.yd, net.yu, net.yo)):
-            net.got(dkv.at[d], kr[3 + i])
-
-        every = dkv[...].reshape(512, 128)
-        value_sum = jnp.broadcast_to(jnp.sum(every.astype(F32), axis=0, keepdims=True), (8, 128))
-        for j in range(4):
-            at = pl.ds(pl.multiple_of((j % 2) * 512 + yh * 256, 256), 256)
-            out = lax.dot_general(adu[j // 2, :, at], every, TN, preferred_element_type=F32).reshape(4, 2, 32, 128)
-            for i in range(4):
-                gkv[j, i, 0:32] = jnp.where(yl == 0, out[i, 0], out[i, 1])
-                gkv[j, i, 32:40] = value_sum
-
-        def key_value():
-            k = [net.slot() for _ in range(7)]
-            for i, (name, d) in enumerate((("zu", net.zu), ("zd", net.zd), ("zo", net.zo))):
-                net.send(gkv.at[d], gkv_z.at[i], k[i], name)
-            yield
-            for i in range(3):
-                net.got(gkv_z.at[i], k[i])
-            for i in range(4):
-                gkv_x[i] = gkv[z, i] + gkv_z[0, i] + gkv_z[1, i] + gkv_z[2, i]
-            for i, (name, d) in enumerate((("xu", net.xu), ("xd", net.xd), ("xo", net.xo))):
-                net.send(gkv_x.at[d], gkv_x.at[4 + i], k[3 + i], name)
-            yield
-            for i in range(3):
-                net.got(gkv_x.at[4 + i], k[3 + i])
-            total = gkv_x[x] + gkv_x[4] + gkv_x[5] + gkv_x[6]
-            gkv_x[7, 0:16] = jnp.where(c == 0, total[0:16], total[16:32])
-            gkv_x[7, 16:32] = jnp.where(c == 0, total[16:32], total[0:16])
-            gkv_x[7, 32:40] = total[32:40]
-            net.send(gkv_x.at[7, pl.ds(16, 24)], gkv_x.at[8, pl.ds(16, 24)], k[6], "c")
-            yield
-            net.got(gkv_x.at[8, pl.ds(16, 24)], k[6])
-            here, there = gkv_x[7, 0:16], gkv_x[8, 16:32]
-            kv_out[:, 0:128] = jnp.where(c == 0, here, there)
-            kv_out[:, 128:256] = jnp.where(c == 0, there, here)
-            vb_out[...] = jnp.where(c == 0, gkv_x[8, 32:40], gkv_x[7, 32:40])
+        next(query)
+        next(rows_one, None)
 
         def vectors():
             k = [net.slot() for _ in range(13)]
@@ -1297,6 +1281,47 @@
                 net.got(vec_x.at[1 + i], k[10 + i])
             vec_out[...] = vec_x[0] + vec_x[1] + vec_x[2] + vec_x[3]
 
+        vector = vectors()
+        next(vector)
+        next(small, None)
+        for i, d in enumerate((net.yd, net.yu, net.yo)):
+            net.got(dkv.at[d], kr[3 + i])
+
+        every = dkv[...].reshape(512, 128)
+        value_sum = jnp.broadcast_to(jnp.sum(every.astype(F32), axis=0, keepdims=True), (8, 128))
+        for j in range(4):
+            at = pl.ds(pl.multiple_of((j % 2) * 512 + yh * 256, 256), 256)
+            out = lax.dot_general(adu[j // 2, :, at], every, TN, preferred_element_type=F32).reshape(4, 2, 32, 128)
+            for i in range(4):
+                gkv[j, i, 0:32] = jnp.where(yl == 0, out[i, 0], out[i, 1])
+                gkv[j, i, 32:40] = value_sum
+
+        def key_value():
+            k = [net.slot() for _ in range(7)]
+            for i, (name, d) in enumerate((("zu", net.zu), ("zd", net.zd), ("zo", net.zo))):
+                net.send(gkv.at[d], gkv_z.at[i], k[i], name)
+            yield
+            for i in range(3):
+                net.got(gkv_z.at[i], k[i])
+            for i in range(4):
+                gkv_x[i] = gkv[z, i] + gkv_z[0, i] + gkv_z[1, i] + gkv_z[2, i]
+            for i, (name, d) in enumerate((("xu", net.xu), ("xd", net.xd), ("xo", net.xo))):
+                net.send(gkv_x.at[d], gkv_x.at[4 + i], k[3 + i], name)
+            yield
+            for i in range(3):
+                net.got(gkv_x.at[4 + i], k[3 + i])
+            total = gkv_x[x] + gkv_x[4] + gkv_x[5] + gkv_x[6]
+            gkv_x[7, 0:16] = jnp.where(c == 0, total[0:16], total[16:32])
+            gkv_x[7, 16:32] = jnp.where(c == 0, total[16:32], total[0:16])
+            gkv_x[7, 32:40] = total[32:40]
+            net.send(gkv_x.at[7, pl.ds(16, 24)], gkv_x.at[8, pl.ds(16, 24)], k[6], "c")
+            yield
+            net.got(gkv_x.at[8, pl.ds(16, 24)], k[6])
+            here, there = gkv_x[7, 0:16], gkv_x[8, 16:32]
+            kv_out[:, 0:128] = jnp.where(c == 0, here, there)
+            kv_out[:, 128:256] = jnp.where(c == 0, there, here)
+            vb_out[...] = jnp.where(c == 0, gkv_x[8, 32:40], gkv_x[7, 32:40])
+
         def partner_bias():
             k = net.slot()
             net.send(bias.at[2], bias_out.at[1], k, "yo")
@@ -1306,8 +1331,7 @@
 
         last = key_value()
         next(last)
-        next(rows_one, None)
-        run_all(vectors(), last, partner_bias(), query, project, down, up)
+        run_all(vector, last, partner_bias(), query, project, down, up)
         net.finish()
 
     n, d = tokens.shape
@@ -1343,7 +1367,7 @@
             VMEM((4, 2, 4, n, 256), BF16),
             VMEM((4, 2, 4, 2, 2, 16, 128), BF16),
             VMEM((2, 512, 1024), BF16),
-            VMEM((512, 256), F32),
+            VMEM((512, 1024), F32),
             VMEM((512, 256), F32),
             VMEM((4, 2, n, d), BF16),
             VMEM((4, 2, n, d), BF16),
@@ -1370,7 +1394,7 @@
             VMEM((4, 2, 8, d), F32),
             VMEM((7, 8, 512), F32),
             VMEM((4, 8, 256), F32),
-            pltpu.SemaphoreType.DMA((24,)),
+            pltpu.SemaphoreType.DMA((26,)),
         ]
         + scatter_scratch(n, d)
         + scatter_scratch(n, d)

time: 252 us -> 247 us (0.980)
  Pallas kernels: 248 us -> 243 us
    pallas_call x1, Pallas kernels: 107 us -> 102 us  [forward(): pl.pallas_call(kernel, out_shape=(rows, rows, bf(4, 2, 4, n, 1024), bf(4,...]
where the time goes in v6:
time: 247 us
  Pallas kernels  243 us (98%)
    pallas_call x1, Pallas kernels, backward(): pl.pallas_call(kernel, out_shape=(bf(n, d), f32(n, d), bf(n, d), bf(n, d)...  138 us
    pallas_call x1, Pallas kernels, forward(): pl.pallas_call(kernel, out_shape=(rows, rows, bf(4, 2, 4, n, 1024), bf(4,...  102 us

profile of v6, /device:TPU:0, one launch (start us, length us, event | category | flops | bytes accessed | tf_op | source)
XLA Modules:
  0.0 246.8 jit_solution(9305109354369066367)
XLA Ops:
  1.3 1.3 pad_add_fusion.vec_in
  2.7 102.5 %forward.1 = (bf16[4,2,64,2048]{3,2,1,0:T(8,128)(2,1)}, bf16[4,2,64,2048]{3,2,1,0:T(8,128)(2,1)}, bf16[4,2,4,64,1024]{4,3,2,1,0:T(8,128)(2,1)}, bf16[4,2,4,64,10...) custom-call(bf16[64,2048]{1,0:T(8,128)(2,1)} %tok.3, ...), custom_call_target="tpu_custom_call" | custom-call | tf_op jit(solution)/shard_map/forward/pallas_call | solution.py:737
  105.1 137.8 %backward.1 = (bf16[64,2048]{1,0:T(8,128)(2,1)}, f32[64,2048]{1,0:T(8,128)}, bf16[64,2048]{1,0:T(8,128)(2,1)}, bf16[64,2048]{1,0:T(8,128)(2,1)}, bf16[64,512]{1,...) custom-call(bf16[64,2048]{1,0:T(8,128)(2,1)} %tok.3, ...), custom_call_target="tpu_custom_call" | custom-call | tf_op jit(solution)/shard_map/backward/pallas_call | solution.py:1345
  243.6 3.0 %finish.1 = (bf16[64,2048]{1,0:T(8,128)(2,1)}, f32[64,2048]{1,0:T(8,128)}, f32[64,512]{1,0:T(8,128)}, f32[64,2048]{1,0:T(8,128)}, f32[64,512]{1,0:T(8,128)}, /*i...) custom-call(bf16[64,2048]{1,0:T(8,128)(2,1)} %get-tuple-element.77.u, ...), custom_call_target="tpu_custom_call" | custom-call | tf_op jit(solution)/shard_map/finish/pallas_call | solution.py:1475

commit v7 on v6

--- a/solution.py
+++ b/solution.py
@@ -665,8 +665,8 @@
         next(project_weight)
         next(keys)
         next(cots)
+        later.tick()
         next(keys)
-        later.tick()
         next(cots)
         for _ in keys:
             pass

time: 247 us -> 264 us (1.069)
  Pallas kernels: 243 us -> 261 us
    pallas_call x1, Pallas kernels: 102 us -> 120 us  [forward(): pl.pallas_call(kernel, out_shape=(rows, rows, bf(4, 2, 4, n, 1024), bf(4,...]
where the time goes in v7:
time: 264 us
  Pallas kernels  261 us (99%)
    pallas_call x1, Pallas kernels, backward(): pl.pallas_call(kernel, out_shape=(bf(n, d), f32(n, d), bf(n, d), bf(n, d)...  138 us
    pallas_call x1, Pallas kernels, forward(): pl.pallas_call(kernel, out_shape=(rows, rows, bf(4, 2, 4, n, 1024), bf(4,...  120 us

profile of v7, /device:TPU:0, one launch (start us, length us, event | category | flops | bytes accessed | tf_op | source)
XLA Modules:
  0.0 264.2 jit_solution(6094196170191694450)
XLA Ops:
  1.3 1.3 pad_add_fusion.vec_in
  2.7 120.0 %forward.1 = (bf16[4,2,64,2048]{3,2,1,0:T(8,128)(2,1)}, bf16[4,2,64,2048]{3,2,1,0:T(8,128)(2,1)}, bf16[4,2,4,64,1024]{4,3,2,1,0:T(8,128)(2,1)}, bf16[4,2,4,64,10...) custom-call(bf16[64,2048]{1,0:T(8,128)(2,1)} %tok.3, ...), custom_call_target="tpu_custom_call" | custom-call | tf_op jit(solution)/shard_map/forward/pallas_call | solution.py:737
  122.7 137.7 %backward.1 = (bf16[64,2048]{1,0:T(8,128)(2,1)}, f32[64,2048]{1,0:T(8,128)}, bf16[64,2048]{1,0:T(8,128)(2,1)}, bf16[64,2048]{1,0:T(8,128)(2,1)}, bf16[64,512]{1,...) custom-call(bf16[64,2048]{1,0:T(8,128)(2,1)} %tok.3, ...), custom_call_target="tpu_custom_call" | custom-call | tf_op jit(solution)/shard_map/backward/pallas_call | solution.py:1345
  261.0 3.0 %finish.1 = (bf16[64,2048]{1,0:T(8,128)(2,1)}, f32[64,2048]{1,0:T(8,128)}, f32[64,512]{1,0:T(8,128)}, f32[64,2048]{1,0:T(8,128)}, f32[64,512]{1,0:T(8,128)}, /*i...) custom-call(bf16[64,2048]{1,0:T(8,128)(2,1)} %get-tuple-element.77.u, ...), custom_call_target="tpu_custom_call" | custom-call | tf_op jit(solution)/shard_map/finish/pallas_call | solution.py:1475
